TPU v7x, 256 devices: a whole 4x4x8 slice. The times are simulated.
256 devices in a mesh: dp: 8 (over y_hi, x), tensor: 32 (over z, y_lo, core).
Axes of the slice: x: 4, y: 4 (y_hi: 2, y_lo: 2; y = y_hi * 2 + y_lo), z: 8, core: 2. Of those that a mesh axis runs over, the one named last changes fastest.
Arguments:
- tokens: bfloat16 [1024, 8192], P(('dp', 'tensor')), may hold values from -6 to 6
- grad_out: bfloat16 [1024, 8192], P(('dp', 'tensor')), may hold values from -6 to 6
- w1_blocks: bfloat16 [2048, 128, 128], P('tensor'), may hold values from -0.125 to 0.125
- w1_rows: int32 [2048], P('tensor'), may hold values from 0 to 63, as said below
- w1_cols: int32 [2048], P('tensor'), may hold values from 0 to 127, as said below
- w1_count: int32 [32], P('tensor'), may hold values from 21 to 64, as said below
- w2_blocks: bfloat16 [2048, 128, 128], P('tensor'), may hold values from -0.09375 to 0.09375
- w2_rows: int32 [2048], P('tensor'), may hold values from 0 to 127, as said below
- w2_cols: int32 [2048], P('tensor'), may hold values from 0 to 63
- w2_count: int32 [32], P('tensor'), may hold values from 21 to 64, as said below
Outputs:
- layer_out: bfloat16 [1024, 8192], P(('dp', 'tensor'))
- grad_tokens: bfloat16 [1024, 8192], P(('dp', 'tensor'))
- grad_w1: float32 [2048, 128, 128], P('tensor', 'dp')
- grad_w2: float32 [2048, 128, 128], P('tensor', 'dp')
Inputs may be any that keep to these rules, and one draw needn't show every extreme that they name: `w1_rows`: the slots of stripe t hold distinct (row, column) block pairs; for the up projection the block columns lie in t * 4 to t * 4 + 3. `w1_cols`: block columns of stripe t lie in t * 4 to t * 4 + 3. `w1_count`: some stripe has all 64 slots live. `w2_rows`: block rows of stripe t lie in t * 4 to t * 4 + 3; the slots of a stripe hold distinct (row, column) block pairs. `w2_count`: some stripe has all 64 slots live.
All inputs are finite; a program needn't handle non-finite values.
Results may differ from a plain program's by a relative error of at most 0.023.
Values may be sent and summed in bfloat16 or wider, within the bound.
No kernel may reach another device: no remote copies, remote signals or barrier semaphores. Data moves between devices by JAX's collectives and lax.ppermute only.
A program may use at most 128 MiB of HBM per device.

v0:
```python
import jax
import jax.numpy as jnp
from jax import lax
from jax.sharding import PartitionSpec as P

FF = 16384


HIGHEST = lax.Precision.HIGHEST


def gelu_tanh(values):
    return jax.nn.gelu(values, approximate=True)


def selector(labels, label_width, out_type):
    return (labels[:, None] == jnp.arange(label_width, dtype=jnp.int32)[None, :]).astype(out_type)


def shards(
    tokens, grad_out, w1_blocks, w1_rows, w1_cols, w1_count, w2_blocks, w2_rows, w2_cols, w2_count
):
    block_size = w1_blocks.shape[1]
    slot_count = w1_blocks.shape[0]
    width_blocks = tokens.shape[1] // block_size
    stripe_width = FF // (block_size * lax.axis_size("tensor"))
    stripe = lax.axis_index("tensor")
    slot_ids = jnp.arange(slot_count, dtype=jnp.int32)
    live_first = (slot_ids < w1_count[0]).astype(jnp.float32)
    live_second = (slot_ids < w2_count[0]).astype(jnp.float32)
    first_kept = w1_blocks * live_first.astype(jnp.bfloat16)[:, None, None]
    second_kept = w2_blocks * live_second.astype(jnp.bfloat16)[:, None, None]
    first_local = w1_cols - stripe * stripe_width
    second_local = w2_rows - stripe * stripe_width
    first_colsel = selector(first_local, stripe_width, jnp.float32)
    first_colsel_narrow = selector(first_local, stripe_width, jnp.bfloat16)
    first_rowsel = selector(w1_rows, width_blocks, jnp.float32)
    second_rowsel = selector(second_local, stripe_width, jnp.float32)
    second_rowsel_narrow = selector(second_local, stripe_width, jnp.bfloat16)
    second_colsel = selector(w2_cols, width_blocks, jnp.float32)
    all_tokens = lax.all_gather(tokens, "tensor", axis=0, tiled=True)
    total_rows = all_tokens.shape[0]
    own_rows = total_rows // lax.axis_size("tensor")
    token_blocks = jnp.take(
        all_tokens.reshape(total_rows, width_blocks, block_size), w1_rows, axis=1
    )
    products = jnp.einsum(
        "tsk,skj->tsj", token_blocks, first_kept, preferred_element_type=jnp.float32
    )
    preact = jnp.einsum("tsj,sc->tcj", products, first_colsel, precision=HIGHEST)
    hidden = gelu_tanh(preact).astype(jnp.bfloat16)
    hidden_blocks = jnp.einsum(
        "tcj,sc->tsj", hidden, second_rowsel_narrow, preferred_element_type=jnp.float32
    ).astype(jnp.bfloat16)
    rows_part = hidden_blocks
    partial_out = jnp.einsum(
        "tsk,skj->tsj", rows_part, second_kept, preferred_element_type=jnp.float32
    )
    spread = jnp.einsum("tsj,sd->tdj", partial_out, second_colsel, precision=HIGHEST)
    layer_out = lax.psum_scatter(
        spread.reshape(lax.axis_size("tensor") * own_rows, width_blocks * block_size).astype(
            jnp.bfloat16
        ),
        "tensor",
        scatter_dimension=0,
        tiled=True,
    )
    all_grads = lax.all_gather(grad_out, "tensor", axis=0, tiled=True)
    grad_blocks = jnp.take(all_grads.reshape(total_rows, width_blocks, block_size), w2_cols, axis=1)
    back_hidden = jnp.einsum(
        "tsj,skj->tsk", grad_blocks, second_kept, preferred_element_type=jnp.float32
    )
    grad_hidden = jnp.einsum("tsk,sr->trk", back_hidden, second_rowsel, precision=HIGHEST)
    unused, pullback = jax.vjp(gelu_tanh, preact)
    grad_pre = pullback(grad_hidden)[0].astype(jnp.bfloat16)
    grad_pre_blocks = jnp.einsum(
        "tcj,sc->tsj", grad_pre, first_colsel_narrow, preferred_element_type=jnp.float32
    ).astype(jnp.bfloat16)
    rows_part = grad_pre_blocks
    partial_back = jnp.einsum(
        "tsj,skj->tsk", rows_part, first_kept, preferred_element_type=jnp.float32
    )
    spread = jnp.einsum("tsk,sr->trk", partial_back, first_rowsel, precision=HIGHEST)
    grad_tokens = lax.psum_scatter(
        spread.reshape(lax.axis_size("tensor") * own_rows, width_blocks * block_size).astype(
            jnp.bfloat16
        ),
        "tensor",
        scatter_dimension=0,
        tiled=True,
    )
    first_grad = (
        jnp.einsum(
            "tsk,tsj->skj", token_blocks, grad_pre_blocks, preferred_element_type=jnp.float32
        )
        * live_first[:, None, None]
    )
    second_grad = (
        jnp.einsum("tsk,tsj->skj", hidden_blocks, grad_blocks, preferred_element_type=jnp.float32)
        * live_second[:, None, None]
    )
    first_full, second_full = (
        lax.psum(first_grad.astype(jnp.bfloat16), "dp").astype(jnp.float32),
        lax.psum(second_grad.astype(jnp.bfloat16), "dp").astype(jnp.float32),
    )
    share_rows = block_size // lax.axis_size("dp")
    offset = lax.axis_index("dp") * share_rows
    first_sum = lax.dynamic_slice_in_dim(first_full, offset, share_rows, 1)
    second_sum = lax.dynamic_slice_in_dim(second_full, offset, share_rows, 1)
    return (layer_out, grad_tokens, first_sum, second_sum)


def solution(mesh):
    in_specs = (
        P(("dp", "tensor"), None),
        P(("dp", "tensor"), None),
        P("tensor", None, None),
        P("tensor"),
        P("tensor"),
        P("tensor"),
        P("tensor", None, None),
        P("tensor"),
        P("tensor"),
        P("tensor"),
    )
    out_specs = (
        P(("dp", "tensor"), None),
        P(("dp", "tensor"), None),
        P("tensor", "dp", None),
        P("tensor", "dp", None),
    )
    return jax.shard_map(shards, mesh=mesh, in_specs=in_specs, out_specs=out_specs, check_vma=False)
```

profile of v0, /device:TPU:1, one launch (start us, length us, event | category | flops | bytes accessed | tf_op | source)
XLA Modules:
  0.0 554.3 jit_solution(13443408507528910959)
XLA Ops:
  7.2 0.0 all-gather.5.cloned.1.call-start
  7.2 0.7 all-gather.5.cloned.1.call-update
  7.9 0.0 all-gather.7.cloned.1.call-start
  7.9 0.7 all-gather.7.cloned.1.call-update
  8.6 0.0 all-reduce.9.cloned.1.call-start
  10.0 0.7 compare_select_fusion.1
  10.7 0.7 compare_select_fusion
  11.4 0.7 compare_and_fusion
  12.0 0.7 broadcast_subtract_fusion
  12.7 66.1 %all-gather.5.cloned.1.call-done = bf16[32,4,8192]{2,1,0:T(4,128)(2,1)} async-done(((bf16[1,4,8192]{2,1,0:T(4,128)(2,1)}), bf16[32,4,8192]{2,1,0:T(4,128)(2,1)}) %all-gather.5.cloned.1.call-update) | async-done | bytes 2097168 | tf_op jit(solution)/shard_map/all_gather | solution.py:41
  78.8 3.8 reshape.43
  82.6 2.7 copy.45
  85.3 2.5 gather_fusion
  87.8 5.4 convolution_bitcast_fusion.3
  93.2 5.4 copy.47
  98.6 46.4 %all-gather.7.cloned.1.call-done = bf16[32,4,8192]{2,1,0:T(4,128)(2,1)} async-done(((bf16[1,4,8192]{2,1,0:T(4,128)(2,1)}), bf16[32,4,8192]{2,1,0:T(4,128)(2,1)}) %all-gather.7.cloned.1.call-update) | async-done | bytes 2097168 | tf_op jit(solution)/shard_map/all_gather | solution.py:68
  145.1 4.8 reshape.44
  149.9 4.3 copy.53
  154.2 3.7 gather_fusion.1
  157.9 5.9 %convolution_bitcast_fusion.1 = f32[128,64,128]{0,2,1:T(8,128)} fusion(bf16[64,128,128]{2,1,0:T(8,128)(2,1)} %param.18, bf16[64]{0:T(256)(128)(2,1)S(1)} %get-tuple-element.12, bf16[64,128,128]{2,1,0:T(8,128)(2,1)} %gather_fusion.1, pred[64]{0:T(512)(128)(4,1)S(1)} %get-tuple-element.13), kind=kOutput, calls=%fused_computation.5 | convolution fusion | flops 270532608 | bytes 8388800 | tf_op jit(solution)/shard_map/tsj,skj->tsk/dot_general | solution.py:70
  163.8 5.4 copy.54
  169.2 3.8 fusion.36
  173.0 1.5 fusion.38
  174.5 0.2 fusion.20
  174.7 2.1 convert_bitcast_fusion.1
  176.7 4.2 copy.61
  180.9 0.8 convert_bitcast_fusion
  181.7 0.8 copy-done.1
  182.5 3.7 multiply_convert_fusion
  186.2 4.1 multiply_convert_fusion.1
  190.4 0.0 all-reduce.7.cloned.1.call-start
  190.4 1.5 copy-done.2
  191.9 4.5 convolution_bitcast_fusion.2
  196.4 5.4 copy.52
  201.8 4.7 convolution_convert_fusion.1
  206.6 3.2 copy.86
  209.8 4.3 convolution_bitcast_fusion
  214.1 5.5 copy.58
  219.5 4.7 convolution_convert_fusion
  224.3 3.1 copy.85
  227.5 0.6 copy-done.8
  228.1 0.6 dynamic-slice
  229.3 75.7 %all-reduce.9.cloned.1.call-done = (bf16[64,128,128]{2,1,0:T(8,128)(2,1)}, bf16[64,128,128]{2,1,0:T(8,128)(2,1)}) async-done(((bf16[64,128,128]{2,1,0:T(8,128)(2,1)}, bf16[64,128,128]{2,1,0:T(8,128)(2,1)}), (bf16[64,128,128]{2,1,0:T(8,128)(2,1)}, bf16[64,128,128]{2,1,0:T(8,128)(2,1)})) %all-reduce.9.cloned.1.call-update) | async-done | bytes 4194320 | tf_op jit(solution)/shard_map/psum | solution.py:103
  305.0 1.8 dynamic-slice_convert_fusion
  306.8 1.8 dynamic-slice_convert_fusion.1
  308.6 236.0 %all-reduce.7.cloned.1.call-done = (bf16[128,8192]{1,0:T(8,128)(2,1)}, bf16[128,8192]{1,0:T(8,128)(2,1)}) async-done(((bf16[128,8192]{1,0:T(8,128)(2,1)}, bf16[128,8192]{1,0:T(8,128)(2,1)}), (bf16[128,8192]{1,0:T(8,128)(2,1)}, bf16[128,8192]{1,0:T(8,128)(2,1)})) %all-reduce.7.cloned.1.call-update) | async-done | bytes 4194320
  544.6 1.6 constant_dynamic-slice_fusion
  546.2 1.6 constant_dynamic-slice_fusion.1
  (21 shorter events, 0.1 us)
Async XLA Ops:
  7.2 71.6 %all-gather.5.cloned.1.call-start = ((), (), s32[]{:S(2)}) async-start(), calls=%async_computation | async-start | bytes 2162688 | tf_op jit(solution)/shard_map/all_gather | solution.py:41
  7.9 137.2 %all-gather.7.cloned.1.call-start = ((), (), s32[]{:S(2)}) async-start(), calls=%async_computation.1 | async-start | bytes 2162688 | tf_op jit(solution)/shard_map/all_gather | solution.py:68
  8.6 296.4 %all-reduce.9.cloned.1.call-start = ((), (), s32[]{:S(2)}) async-start(), calls=%async_computation.3 | async-start | bytes 8388608 | tf_op jit(solution)/shard_map/psum | solution.py:103
  169.2 3.8 copy-start
  180.9 1.6 copy-start.1
  181.7 4.5 copy-start.4
  190.3 1.6 copy-start.2
  190.4 354.2 %all-reduce.7.cloned.1.call-start = ((), (), s32[]{:S(2)}) async-start(), calls=%async_computation.2 | async-start | bytes 8388608
  196.4 5.4 copy-start.6
  206.5 3.2 copy-start.3
  206.6 3.2 copy-start.5
  214.1 5.5 copy-start.7
  227.4 0.7 copy-start.8
Sparse Core Ops, SparseCore 0:
  9.9 68.8 all-gather.4
  80.6 64.3 all-gather.6
  190.5 114.4 all-reduce.8
  307.6 236.9 all-reduce.6
where the time goes:
time: 555 us; the launch traced here: 554 us
  waiting for transfers between devices  426 us (77%)
  local copies, waits for them, and re-layouts  60.7 us (11%)
  matrix products  45.5 us (8%)
  between operations  15.8 us (3%)
  other arithmetic  6.47 us (1%)
    unnamed x5, waiting for transfers between devices  237 us
    psum x1, waiting for transfers between devices, shards(): lax.psum(first_grad.astype(jnp.bfloat16), 'dp').astype(jnp.float32)  75.7 us
    all_gather x1, waiting for transfers between devices, shards(): all_tokens = lax.all_gather(tokens, 'tensor', axis=0, tiled=True)  66.1 us
    all_gather x1, waiting for transfers between devices, shards(): all_grads = lax.all_gather(grad_out, 'tensor', axis=0, tiled=True)  46.4 us
    unnamed x23, local copies, waits for them, and re-layouts  13 us
  transfers between devices with their start and end apart: 4, of which 4 were waited for; matrix products, arithmetic and copies ran while one was open for 11% of the time, Pallas kernels for 0%

commit v1 on v0

v1 whole, which is shorter than its diff:
```python
import functools

import jax
import jax.numpy as jnp
from jax import lax
from jax.experimental import pallas as pl
from jax.experimental.pallas import tpu as pltpu
from jax.sharding import Mesh
from jax.sharding import PartitionSpec as P

AXES = ("yh", "x", "z", "yl", "c")
SIZES = (2, 4, 8, 2, 2)
BLK = 128
SB = 4
CAP = 64
HALF = 32
F32 = jnp.float32
BF16 = jnp.bfloat16
GROUP = 8
R1, C1, R2, C2, LIVE1, LIVE2, CORE, PX, PYH = 0, 64, 128, 192, 256, 257, 258, 259, 260


def gelu_pair(v):
    a = 0.7978845608028654
    b = 0.044715
    v2 = v * v
    t = jnp.tanh(a * v * (1.0 + b * v2))
    half = 0.5 * (1.0 + t)
    slope = half + 0.5 * v * (1.0 - t * t) * (a * (1.0 + 3.0 * b * v2))
    return v * half, slope


def place(block, core):
    side = jnp.where(block // HALF == core, 0, 1)
    return side, pl.ds(pl.multiple_of((block % HALF) * BLK, BLK), BLK)


def load_rows(pieces, tok, grad, sem):
    copies = []
    for side in range(2):
        for rel in range(8):
            for which, dst in enumerate((tok, grad)):
                copies.append(
                    pltpu.make_async_copy(
                        pieces[side][rel][which],
                        dst.at[side, pl.ds(16 * rel, 16)],
                        sem.at[len(copies)],
                    )
                )
    for cp in copies:
        cp.start()
    return copies


def split_pieces(refs):
    sides = []
    for side in range(2):
        r = refs[9 * side : 9 * side + 9]
        row = [(q.at[0], q.at[1]) for q in r[:4]] + [(r[4], r[5])]
        row += [(q.at[0], q.at[1]) for q in r[6:]]
        sides.append(row)
    return sides


def loop(body):
    def group(i, carry):
        for j in range(GROUP):
            body(i * GROUP + j)
        return carry

    lax.fori_loop(0, CAP // GROUP, group, 0)


def dot(a, b, dims):
    return lax.dot_general(a, b, (dims, ((), ())), preferred_element_type=F32)


def forward_kernel(meta, w1, w2, *refs):
    pieces = split_pieces(refs[:18])
    hid, gp, own, oth = refs[18:22]
    tok, grad, pre, back, acc, sem = refs[22:]
    copies = load_rows(pieces, tok, grad, sem)
    pre[...] = jnp.zeros_like(pre)
    back[...] = jnp.zeros_like(back)
    core = meta[CORE]
    n1 = meta[LIVE1]
    n2 = meta[LIVE2]
    for cp in copies:
        cp.wait()

    def up(s):
        side, lanes = place(meta[R1 + s], core)
        col = jnp.where(s < n1, meta[C1 + s], SB)
        pre[col] += dot(tok[side, :, lanes], w1[s], ((1,), (0,)))

    loop(up)

    def down(s):
        side, lanes = place(meta[C2 + s], core)
        row = jnp.where(s < n2, meta[R2 + s], SB)
        back[row] += dot(grad[side, :, lanes], w2[s], ((1,), (1,)))

    loop(down)
    for k in range(SB):
        h, slope = gelu_pair(pre[k])
        hid[k] = h.astype(BF16)
        gp[k] = (back[k] * slope).astype(BF16)

    def finish(which):
        for b in range(HALF):
            own[which, :, b * BLK : (b + 1) * BLK] = acc[core * HALF + b].astype(BF16)
            oth[which, :, b * BLK : (b + 1) * BLK] = acc[(1 - core) * HALF + b].astype(BF16)

    acc[...] = jnp.zeros_like(acc)

    def out(s):
        col = jnp.where(s < n2, meta[C2 + s], 2 * HALF)
        acc[col] += dot(hid[meta[R2 + s]], w2[s], ((1,), (0,)))

    loop(out)
    finish(0)
    acc[...] = jnp.zeros_like(acc)

    def tback(s):
        row = jnp.where(s < n1, meta[R1 + s], 2 * HALF)
        acc[row] += dot(gp[meta[C1 + s]], w1[s], ((1,), (1,)))

    loop(tback)
    finish(1)


def weight_kernel(meta, hid, gp, *refs):
    pieces = split_pieces(refs[:18])
    o2 = refs[18:22]
    o1 = refs[22:24]
    tok, grad, d2, d1, sem, osem = refs[24:]
    copies = load_rows(pieces, tok, grad, sem)
    core = meta[CORE]
    px = meta[PX]
    pyh = meta[PYH]
    n1 = meta[LIVE1]
    n2 = meta[LIVE2]
    for cp in copies:
        cp.wait()

    def second(s):
        side, lanes = place(meta[C2 + s], core)
        v = dot(hid[meta[R2 + s]], grad[side, :, lanes], ((0,), (0,)))
        v = jnp.where(s < n2, v, 0.0).astype(BF16)
        for j in range(8):
            d2[(j % 4 - px) & 3, (j // 4) ^ pyh, s] = v[16 * j : 16 * j + 16]

    loop(second)

    def first(s):
        side, lanes = place(meta[R1 + s], core)
        v = dot(tok[side, :, lanes], gp[meta[C1 + s]], ((0,), (0,)))
        v = jnp.where(s < n1, v, 0.0).astype(BF16)
        for j in range(8):
            d1[(j // 4) ^ pyh, (j % 4 - px) & 3, s] = v[16 * j : 16 * j + 16]

    loop(first)
    outs = [pltpu.make_async_copy(d2.at[k], o2[k], osem.at[k]) for k in range(4)]
    outs += [pltpu.make_async_copy(d1.at[k], o1[k], osem.at[4 + k]) for k in range(2)]
    for cp in outs:
        cp.start()
    for cp in outs:
        cp.wait()


VMEM = pl.BlockSpec(memory_space=pltpu.VMEM)
SMEM = pl.BlockSpec(memory_space=pltpu.SMEM)
ANY = pl.BlockSpec(memory_space=pl.ANY)
LIMIT = 48 * 1024 * 1024


def run_forward(meta, w1, w2, pieces):
    sd = jax.ShapeDtypeStruct
    return pl.pallas_call(
        forward_kernel,
        out_shape=[
            sd((SB, BLK, BLK), BF16),
            sd((SB, BLK, BLK), BF16),
            sd((2, BLK, HALF * BLK), BF16),
            sd((2, BLK, HALF * BLK), BF16),
        ],
        in_specs=[SMEM, VMEM, VMEM] + [ANY] * 18,
        out_specs=[VMEM] * 4,
        scratch_shapes=[
            pltpu.VMEM((2, BLK, HALF * BLK), BF16),
            pltpu.VMEM((2, BLK, HALF * BLK), BF16),
            pltpu.VMEM((SB + 1, BLK, BLK), F32),
            pltpu.VMEM((SB + 1, BLK, BLK), F32),
            pltpu.VMEM((2 * HALF + 1, BLK, BLK), F32),
            pltpu.SemaphoreType.DMA((32,)),
        ],
        compiler_params=pltpu.CompilerParams(vmem_limit_bytes=LIMIT),
        cost_estimate=pl.CostEstimate(flops=1 << 32, bytes_accessed=12 << 20, transcendentals=1 << 16),
    )(meta, w1, w2, *pieces)


def run_weight(meta, hid, gp, pieces):
    sd = jax.ShapeDtypeStruct
    return pl.pallas_call(
        weight_kernel,
        out_shape=[sd((2, CAP, 16, BLK), BF16)] * 4 + [sd((4, CAP, 16, BLK), BF16)] * 2,
        in_specs=[SMEM, VMEM, VMEM] + [ANY] * 18,
        out_specs=[ANY] * 6,
        scratch_shapes=[
            pltpu.VMEM((2, BLK, HALF * BLK), BF16),
            pltpu.VMEM((2, BLK, HALF * BLK), BF16),
            pltpu.VMEM((4, 2, CAP, 16, BLK), BF16),
            pltpu.VMEM((2, 4, CAP, 16, BLK), BF16),
            pltpu.SemaphoreType.DMA((32,)),
            pltpu.SemaphoreType.DMA((6,)),
        ],
        compiler_params=pltpu.CompilerParams(vmem_limit_bytes=LIMIT),
        cost_estimate=pl.CostEstimate(flops=1 << 31, bytes_accessed=8 << 20, transcendentals=0),
    )(meta, hid, gp, *pieces)


def shift(n, k):
    return [(i, (i + k) % n) for i in range(n)]


def flip(k):
    return [(i, i ^ k) for i in range(4)]


def f32(v):
    return v.astype(F32)


def gather_rows(tokens, grads):
    c = lax.axis_index("c")
    low = c == 0
    both = jnp.stack([tokens, grads])
    width = both.shape[2] // 2
    mine = jnp.where(low, both[:, :, :width], both[:, :, width:])
    other = jnp.where(low, both[:, :, width:], both[:, :, :width])
    one = lax.ppermute(other, ("yl", "c"), flip(1))
    two = lax.ppermute(mine, ("yl", "c"), flip(2))
    three = lax.ppermute(other, ("yl", "c"), flip(3))
    chunk = jnp.concatenate(
        [
            jnp.where(low, mine, one),
            jnp.where(low, one, mine),
            jnp.where(low, two, three),
            jnp.where(low, three, two),
        ],
        axis=1,
    )
    up = [chunk]
    down = [chunk]
    for _ in range(3):
        up.append(lax.ppermute(up[-1], "z", shift(8, 1)))
        down.append(lax.ppermute(down[-1], "z", shift(8, 7)))
    far_t = lax.ppermute(up[-1][0], "z", shift(8, 1))
    far_g = lax.ppermute(down[-1][1], "z", shift(8, 7))
    own = [chunk, down[1], down[2], down[3], far_t, far_g, up[3], up[2], up[1]]
    oth = [lax.ppermute(q, "c", shift(2, 1)) for q in own]
    return own + oth


def reduce_tensor(own, oth):
    got = lax.ppermute(oth, "c", shift(2, 1))
    s = (f32(own) + f32(got)).reshape(2, 8, 16, -1)
    up = lax.ppermute(s[0, 4].astype(BF16), "z", shift(8, 1))
    down = lax.ppermute(s[1, 4].astype(BF16), "z", shift(8, 7))
    u = jnp.stack([s[0, 3] + f32(up), s[1, 3]])
    d = jnp.stack([s[0, 5], s[1, 5] + f32(down)])
    for k in (2, 3):
        up = lax.ppermute(u.astype(BF16), "z", shift(8, 1))
        down = lax.ppermute(d.astype(BF16), "z", shift(8, 7))
        u = s[:, 4 - k] + f32(up)
        d = s[:, 4 + k] + f32(down)
    up = lax.ppermute(u.astype(BF16), "z", shift(8, 1))
    down = lax.ppermute(d.astype(BF16), "z", shift(8, 7))
    t = s[:, 0] + f32(up) + f32(down)
    got = lax.ppermute(t[:, 8:].astype(BF16), "yl", shift(2, 1))
    t = (t[:, :8] + f32(got)).astype(BF16)
    low = lax.axis_index("c") == 0
    mine = jnp.where(low, t[:, :4], t[:, 4:])
    got = lax.ppermute(jnp.where(low, t[:, 4:], t[:, :4]), "c", shift(2, 1))
    both = jnp.concatenate([jnp.where(low, mine, got), jnp.where(low, got, mine)], axis=2)
    return both[0], both[1]


def reduce_x_first(parts):
    got = [lax.ppermute(parts[k], "x", shift(4, k)) for k in (1, 2, 3)]
    s = f32(parts[0]) + f32(got[0]) + f32(got[1]) + f32(got[2])
    far = lax.ppermute(s[1].astype(BF16), "yh", shift(2, 1))
    return s[0] + f32(far)


def reduce_y_first(parts):
    far = lax.ppermute(parts[1], "yh", shift(2, 1))
    s = f32(parts[0]) + f32(far)
    got = [lax.ppermute(s[k].astype(BF16), "x", shift(4, k)) for k in (1, 2, 3)]
    return s[0] + f32(got[0]) + f32(got[1]) + f32(got[2])


def shards(tokens, grads, w1, w1_rows, w1_cols, w1_count, w2, w2_rows, w2_cols, w2_count):
    stripe = (lax.axis_index("z") * 2 + lax.axis_index("yl")) * 2 + lax.axis_index("c")
    here = jnp.stack([lax.axis_index("c"), lax.axis_index("x"), lax.axis_index("yh")])
    meta = jnp.concatenate(
        [
            w1_rows,
            w1_cols - stripe * SB,
            w2_rows - stripe * SB,
            w2_cols,
            w1_count,
            w2_count,
            here.astype(jnp.int32),
        ]
    )
    pieces = gather_rows(tokens, grads)
    hid, gp, own, oth = run_forward(meta, w1, w2, pieces)
    parts = run_weight(meta, hid, gp, pieces)
    grad_w2 = reduce_x_first(parts[:4])
    grad_w1 = reduce_y_first(parts[4:])
    layer_out, grad_tokens = reduce_tensor(own, oth)
    return layer_out, grad_tokens, grad_w1, grad_w2


def solution(mesh):
    fine = Mesh(mesh.devices.reshape(SIZES), AXES)
    rows = P(AXES, None)
    stripe = ("z", "yl", "c")
    flat = P(stripe)
    blocks = P(stripe, None, None)
    in_specs = (rows, rows, blocks, flat, flat, flat, blocks, flat, flat, flat)
    grads = P(stripe, ("yh", "x"), None)
    out_specs = (rows, rows, grads, grads)
    return jax.shard_map(
        shards, mesh=fine, in_specs=in_specs, out_specs=out_specs, check_vma=False
    )
```

time: 555 us -> 171 us (0.31)
  waiting for transfers between devices: 426 us -> 72 us
  local copies, waits for them, and re-layouts: 60.7 us -> 2.33 us
  starting transfers between devices: 0.16 us -> 53.3 us
  matrix products: 45.5 us -> 0 us
  Pallas kernels: 0 us -> 32.5 us
  between operations: 15.8 us -> 2.18 us
    unnamed x5 -> x0, waiting for transfers between devices: 237 us -> none
    all_gather x2 -> x0, waiting for transfers between devices: 113 us -> none  [the longest x1 66.1 us: shards(): all_tokens = lax.all_gather(tokens, 'tensor', axis=0, tiled=True)]
    psum x1 -> x0, waiting for transfers between devices: 75.7 us -> none  [shards(): lax.psum(first_grad.astype(jnp.bfloat16), 'dp').astype(jnp.float32)]
    ppermute x0 -> x39, waiting for transfers between devices: none -> 72 us  [the longest x3 22.5 us: reduce_x_first(): got = [lax.ppermute(parts[k], 'x', shift(4, k)) for k in (1, 2, 3)]]
    ppermute x0 -> x39, starting transfers between devices: none -> 53.3 us  [the longest x9 10.8 us: gather_rows(): oth = [lax.ppermute(q, 'c', shift(2, 1)) for q in own]]
    dot_general x12 -> x0, matrix products: 45.5 us -> none  [the longest x1 5.86 us: shards(): jnp.einsum('tsj,skj->tsk', grad_blocks, second_kept, preferred_element_ty...]
    pallas_call x0 -> x2, Pallas kernels: none -> 32.5 us  [the longest x1 20.1 us: run_forward(): pl.pallas_call(forward_kernel, out_shape=[sd((SB, BLK, BLK), BF16), sd((S...]
    transpose x4 -> x0, local copies, waits for them, and re-layouts: 21.7 us -> none  [the longest x1 5.46 us: shards(): jnp.einsum('tsj,skj->tsk', rows_part, first_kept, preferred_element_type=...]
  transfers between devices with their start and end apart: 4 -> 39, of which waited for: 4 -> 17; matrix products, arithmetic and copies ran while one was open for 11% -> 3% of each run, Pallas kernels for 0% -> 7%
where the time goes in v1:
time: 171 us; the launch traced here: 170 us
  waiting for transfers between devices  72 us (42%)
  starting transfers between devices  53.3 us (31%)
  Pallas kernels  32.5 us (19%)
  other arithmetic  8.15 us (5%)
  local copies, waits for them, and re-layouts  2.33 us (1%)
  between operations  2.18 us (1%)
    ppermute x3, waiting for transfers between devices, reduce_x_first(): got = [lax.ppermute(parts[k], 'x', shift(4, k)) for k in (1, 2, 3)]  22.5 us
    pallas_call x1, Pallas kernels, run_forward(): pl.pallas_call(forward_kernel, out_shape=[sd((SB, BLK, BLK), BF16), sd((S...  20.1 us
    ppermute x1, waiting for transfers between devices, reduce_y_first(): far = lax.ppermute(parts[1], 'yh', shift(2, 1))  16.7 us
    pallas_call x1, Pallas kernels, run_weight(): pl.pallas_call(weight_kernel, out_shape=[sd((2, CAP, 16, BLK), BF16)] * 4...  12.4 us
    ppermute x9, starting transfers between devices, gather_rows(): oth = [lax.ppermute(q, 'c', shift(2, 1)) for q in own]  10.8 us
    ppermute x3, starting transfers between devices, gather_rows(): down.append(lax.ppermute(down[-1], 'z', shift(8, 7)))  9.65 us
    ppermute x3, waiting for transfers between devices, reduce_y_first(): got = [lax.ppermute(s[k].astype(BF16), 'x', shift(4, k)) for k in (1, 2, 3)]  9.53 us
    ppermute x3, waiting for transfers between devices, gather_rows(): up.append(lax.ppermute(up[-1], 'z', shift(8, 1)))  9.06 us
  transfers between devices with their start and end apart: 39, of which 17 were waited for; matrix products, arithmetic and copies ran while one was open for 3% of the time, Pallas kernels for 7%

profile of v1, /device:TPU:1, one launch (start us, length us, event | category | flops | bytes accessed | tf_op | source)
XLA Modules:
  0.0 170.5 jit_solution(17941576153961383721)
XLA Ops:
  0.7 0.9 broadcast_select_fusion.8
  1.5 3.3 %collective-permute-start = (bf16[2,4,4096]{2,1,0:T(4,128)(2,1)S(1)}, bf16[2,4,4096]{2,1,0:T(4,128)(2,1)S(1)}, u32[]{:S(2)}, u32[]{:S(2)}) collective-permute-start(bf16[2,4,4096]{2,1,0:T(4,128)(2,1)S(1)} %broadcast_select_fusion.8), channel_id=1, source_target_pairs={{0,1},{1,0},{2,3},{3,2},{4,5},{5,4},{6,7},{7,6},{8,9},{9,8},{10,11... | collective-permute-start | bytes 196616 | tf_op jit(solution)/shard_map/ppermute | solution.py:241
  4.9 0.9 collective-permute-done
  5.8 0.9 broadcast_select_fusion.7
  7.3 1.4 collective-permute-done.2
  8.7 1.2 collective-permute-done.1
  10.4 4.0 %collective-permute-start.3 = (bf16[2,16,4096]{2,1,0:T(8,128)(2,1)S(1)}, bf16[2,16,4096]{2,1,0:T(8,128)(2,1)S(1)}, u32[]{:S(2)}, u32[]{:S(2)}) collective-permute-start(bf16[2,16,4096]{2,1,0:T(8,128)(2,1)S(1)} %pad_maximum_fusion.refs_0_), channel_id=1, source_target_pairs={{0,28},{4,0},{8,4},{12,8},{16,12},{20,16},{24,20},{28,24},{1,29},{... | collective-permute-start | bytes 786440 | tf_op jit(solution)/shard_map/ppermute | solution.py:257
  14.4 4.9 %collective-permute-done.6.refs_8_ = bf16[2,16,4096]{2,1,0:T(8,128)(2,1)S(1)} collective-permute-done((bf16[2,16,4096]{2,1,0:T(8,128)(2,1)S(1)}, bf16[2,16,4096]{2,1,0:T(8,128)(2,1)S(1)}, u32[]{:S(2)}, u32[]{:S(2)}) %collective-permute-start.6) | collective-permute-done | bytes 262176 | tf_op jit(solution)/shard_map/ppermute | solution.py:256
  19.4 2.7 %collective-permute-start.4 = (bf16[2,16,4096]{2,1,0:T(8,128)(2,1)S(1)}, bf16[2,16,4096]{2,1,0:T(8,128)(2,1)S(1)}, u32[]{:S(2)}, u32[]{:S(2)}) collective-permute-start(bf16[2,16,4096]{2,1,0:T(8,128)(2,1)S(1)} %collective-permute-done.3.refs_1_), channel_id=1, source_target_pairs={{0,28},{4,0},{8,4},{12,8},{16,12},{20,16},{24,20},{28,24},{1,29},{... | collective-permute-start | bytes 786440 | tf_op jit(solution)/shard_map/ppermute | solution.py:257
  22.1 4.1 %collective-permute-done.7.refs_7_ = bf16[2,16,4096]{2,1,0:T(8,128)(2,1)S(1)} collective-permute-done((bf16[2,16,4096]{2,1,0:T(8,128)(2,1)S(1)}, bf16[2,16,4096]{2,1,0:T(8,128)(2,1)S(1)}, u32[]{:S(2)}, u32[]{:S(2)}) %collective-permute-start.7) | collective-permute-done | bytes 262176 | tf_op jit(solution)/shard_map/ppermute | solution.py:256
  26.2 3.1 %collective-permute-start.11 = (bf16[2,16,4096]{2,1,0:T(8,128)(2,1)S(1)}, bf16[2,16,4096]{2,1,0:T(8,128)(2,1)S(1)}, u32[]{:S(2)}, u32[]{:S(2)}) collective-permute-start(bf16[2,16,4096]{2,1,0:T(8,128)(2,1)S(1)} %pad_maximum_fusion.refs_0_), channel_id=1, source_target_pairs={{0,1},{1,0},{2,3},{3,2},{4,5},{5,4},{6,7},{7,6},{8,9},{9,8},{10,11... | collective-permute-start | bytes 786440 | tf_op jit(solution)/shard_map/ppermute | solution.py:261
  29.8 3.0 %collective-permute-start.5 = (bf16[2,16,4096]{2,1,0:T(8,128)(2,1)S(1)}, bf16[2,16,4096]{2,1,0:T(8,128)(2,1)S(1)}, u32[]{:S(2)}, u32[]{:S(2)}) collective-permute-start(bf16[2,16,4096]{2,1,0:T(8,128)(2,1)S(1)} %collective-permute-done.4.refs_2_), channel_id=1, source_target_pairs={{0,28},{4,0},{8,4},{12,8},{16,12},{20,16},{24,20},{28,24},{1,29},{... | collective-permute-start | bytes 786440 | tf_op jit(solution)/shard_map/ppermute | solution.py:257
  32.8 4.1 %collective-permute-start.13 = (bf16[2,16,4096]{2,1,0:T(8,128)(2,1)S(1)}, bf16[2,16,4096]{2,1,0:T(8,128)(2,1)S(1)}, u32[]{:S(2)}, u32[]{:S(2)}) collective-permute-start(bf16[2,16,4096]{2,1,0:T(8,128)(2,1)S(1)} %collective-permute-done.4.refs_2_), channel_id=1, source_target_pairs={{0,1},{1,0},{2,3},{3,2},{4,5},{5,4},{6,7},{7,6},{8,9},{9,8},{10,11... | collective-permute-start | bytes 786440 | tf_op jit(solution)/shard_map/ppermute | solution.py:261
  36.9 0.7 slice_bitcast_fusion.17
  37.6 1.0 collective-permute-done.5.refs_3_
  38.5 0.7 slice_bitcast_fusion.16
  39.2 3.4 %collective-permute-start.10 = (bf16[16,4096]{1,0:T(8,128)(2,1)}, bf16[16,4096]{1,0:T(8,128)(2,1)}, u32[]{:S(2)}, u32[]{:S(2)}) collective-permute-start(bf16[16,4096]{1,0:T(8,128)(2,1)} %slice_bitcast_fusion.16), channel_id=1, source_target_pairs={{0,28},{4,0},{8,4},{12,8},{16,12},{20,16},{24,20},{28,24},{1,29},{... | collective-permute-start | bytes 393224 | tf_op jit(solution)/shard_map/ppermute | solution.py:259
  42.6 1.1 collective-permute-start.18
  45.5 1.1 collective-permute-start.15
  47.0 0.8 concatenate.9.meta
  48.3 20.1 %shard_map.129 = (bf16[4,128,128]{2,1,0:T(8,128)(2,1)S(1)}, bf16[4,128,128]{2,1,0:T(8,128)(2,1)S(1)}, bf16[2,128,4096]{2,1,0:T(8,128)(2,1)}, bf16[2,128,4096]{2,1,0:T(8,128)(2,1)}) custom-call(s32[261]{0:T(512)S(1)} %concatenate.9.meta, bf16[64,128,128]{2,1,0:T(8,128)(2,1)} %w1.1, bf16[64,128,128]{2,1,0:T(8,128)(2,1)} %w2.1, ...), custom_call_target="tpu_custom_call" | custom-call | flops 4294967296 | bytes 12582912 | tf_op jit(solution)/shard_map/pallas_call | solution.py:179
  68.8 4.1 %collective-permute-done.20 = bf16[2,128,4096]{2,1,0:T(8,128)(2,1)S(1)} collective-permute-done((bf16[2,128,4096]{2,1,0:T(8,128)(2,1)}, bf16[2,128,4096]{2,1,0:T(8,128)(2,1)S(1)}, u32[]{:S(2)}, u32[]{:S(2)}) %collective-permute-start.20) | collective-permute-done | bytes 2097184 | tf_op jit(solution)/shard_map/ppermute | solution.py:266
  72.9 2.3 %convert_add_fusion = f32[2,128,4096]{2,1,0:T(8,128)S(1)} fusion(bf16[2,128,4096]{2,1,0:T(8,128)(2,1)S(1)} %collective-permute-done.20, bf16[2,128,4096]{2,1,0:T(8,128)(2,1)} %get-tuple-element.14), kind=kLoop, calls=%fused_computation | loop fusion | flops 3145728 | bytes 8388608 | tf_op jit(solution)/shard_map/add | solution.py:267
  75.5 2.5 %collective-permute-start.21 = (bf16[16,4096]{1,0:T(8,128)(2,1)S(1)}, bf16[16,4096]{1,0:T(8,128)(2,1)S(1)}, u32[]{:S(2)}, u32[]{:S(2)}) collective-permute-start(bf16[16,4096]{1,0:T(8,128)(2,1)S(1)} %get-tuple-element.34), channel_id=1, source_target_pairs={{0,4},{4,8},{8,12},{12,16},{16,20},{20,24},{24,28},{28,0},{1,5},{5... | collective-permute-start | bytes 393224 | tf_op jit(solution)/shard_map/ppermute | solution.py:268
  78.1 0.7 collective-permute-start.25
  78.7 12.4 %shard_map.130 = (bf16[2,64,16,128]{3,2,1,0:T(8,128)(2,1)S(1)}, bf16[2,64,16,128]{3,2,1,0:T(8,128)(2,1)S(1)}, bf16[2,64,16,128]{3,2,1,0:T(8,128)(2,1)S(1)}, bf16...) custom-call(s32[261]{0:T(512)S(1)} %concatenate.9.meta, ...), custom_call_target="tpu_custom_call" | custom-call | flops 2147483648 | bytes 8388608 | tf_op jit(solution)/shard_map/pallas_call | solution.py:204
  91.1 2.6 %collective-permute-start.37 = (bf16[2,64,16,128]{3,2,1,0:T(8,128)(2,1)}, bf16[2,64,16,128]{3,2,1,0:T(8,128)(2,1)S(1)}, u32[]{:S(2)}, u32[]{:S(2)}) collective-permute-start(bf16[2,64,16,128]{3,2,1,0:T(8,128)(2,1)} %get-tuple-element.23), channel_id=1, source_target_pairs={{0,96},{32,0},{64,32},{96,64},{1,97},{33,1},{65,33},{97,65},{2,98}... | collective-permute-start | bytes 1572872 | tf_op jit(solution)/shard_map/ppermute | solution.py:290
  94.9 0.9 collective-permute-start.22
  95.9 1.9 %collective-permute-start.26 = (bf16[2,16,4096]{2,1,0:T(8,128)(2,1)S(1)}, bf16[2,16,4096]{2,1,0:T(8,128)(2,1)S(1)}, u32[]{:S(2)}, u32[]{:S(2)}) collective-permute-start(bf16[2,16,4096]{2,1,0:T(8,128)(2,1)S(1)} %pad_maximum_fusion.2), channel_id=1, source_target_pairs={{0,28},{4,0},{8,4},{12,8},{16,12},{20,16},{24,20},{28,24},{1,29},{... | collective-permute-start | bytes 786440 | tf_op jit(solution)/shard_map/ppermute | solution.py:274
  97.8 7.7 %collective-permute-done.37 = bf16[2,64,16,128]{3,2,1,0:T(8,128)(2,1)S(1)} collective-permute-done((bf16[2,64,16,128]{3,2,1,0:T(8,128)(2,1)}, bf16[2,64,16,128]{3,2,1,0:T(8,128)(2,1)S(1)}, u32[]{:S(2)}, u32[]{:S(2)}) %collective-permute-start.37) | collective-permute-done | bytes 524320 | tf_op jit(solution)/shard_map/ppermute | solution.py:290
  105.5 2.3 %collective-permute-done.36 = bf16[2,64,16,128]{3,2,1,0:T(8,128)(2,1)S(1)} collective-permute-done((bf16[2,64,16,128]{3,2,1,0:T(8,128)(2,1)S(1)}, bf16[2,64,16,128]{3,2,1,0:T(8,128)(2,1)S(1)}, u32[]{:S(2)}, u32[]{:S(2)}) %collective-permute-start.36) | collective-permute-done | bytes 524320 | tf_op jit(solution)/shard_map/ppermute | solution.py:290
  107.8 12.5 %collective-permute-done.35 = bf16[2,64,16,128]{3,2,1,0:T(8,128)(2,1)S(1)} collective-permute-done((bf16[2,64,16,128]{3,2,1,0:T(8,128)(2,1)S(1)}, bf16[2,64,16,128]{3,2,1,0:T(8,128)(2,1)S(1)}, u32[]{:S(2)}, u32[]{:S(2)}) %collective-permute-start.35) | collective-permute-done | bytes 524320 | tf_op jit(solution)/shard_map/ppermute | solution.py:290
  120.6 2.7 %collective-permute-start.38 = (bf16[64,16,128]{2,1,0:T(8,128)(2,1)S(1)}, bf16[64,16,128]{2,1,0:T(8,128)(2,1)S(1)}, u32[]{:S(2)}, u32[]{:S(2)}) collective-permute-start(bf16[64,16,128]{2,1,0:T(8,128)(2,1)S(1)} %fusion.14), channel_id=1, source_target_pairs={{0,128},{128,0},{1,129},{129,1},{2,130},{130,2},{3,131},{131,3},{4... | collective-permute-start | bytes 786440 | tf_op jit(solution)/shard_map/ppermute | solution.py:292
  123.4 1.2 collective-permute-start.23
  124.6 1.8 %collective-permute-start.27 = (bf16[2,16,4096]{2,1,0:T(8,128)(2,1)S(1)}, bf16[2,16,4096]{2,1,0:T(8,128)(2,1)S(1)}, u32[]{:S(2)}, u32[]{:S(2)}) collective-permute-start(bf16[2,16,4096]{2,1,0:T(8,128)(2,1)S(1)} %get-tuple-element.29), channel_id=1, source_target_pairs={{0,28},{4,0},{8,4},{12,8},{16,12},{20,16},{24,20},{28,24},{1,29},{... | collective-permute-start | bytes 786440 | tf_op jit(solution)/shard_map/ppermute | solution.py:274
  126.7 2.8 %collective-permute-done.38 = bf16[64,16,128]{2,1,0:T(8,128)(2,1)S(1)} collective-permute-done((bf16[64,16,128]{2,1,0:T(8,128)(2,1)S(1)}, bf16[64,16,128]{2,1,0:T(8,128)(2,1)S(1)}, u32[]{:S(2)}, u32[]{:S(2)}) %collective-permute-start.38) | collective-permute-done | bytes 262176 | tf_op jit(solution)/shard_map/ppermute | solution.py:292
  129.6 0.8 fusion
  130.4 1.6 collective-permute-done.23
  132.1 2.4 %collective-permute-start.28 = (bf16[2,16,4096]{2,1,0:T(8,128)(2,1)S(1)}, bf16[2,16,4096]{2,1,0:T(8,128)(2,1)S(1)}, u32[]{:S(2)}, u32[]{:S(2)}) collective-permute-start(bf16[2,16,4096]{2,1,0:T(8,128)(2,1)S(1)} %get-tuple-element.27), channel_id=1, source_target_pairs={{0,28},{4,0},{8,4},{12,8},{16,12},{20,16},{24,20},{28,24},{1,29},{... | collective-permute-start | bytes 786440 | tf_op jit(solution)/shard_map/ppermute | solution.py:278
  134.5 16.7 %collective-permute-done.31 = bf16[4,64,16,128]{3,2,1,0:T(8,128)(2,1)S(1)} collective-permute-done((bf16[4,64,16,128]{3,2,1,0:T(8,128)(2,1)S(1)}, bf16[4,64,16,128]{3,2,1,0:T(8,128)(2,1)S(1)}, u32[]{:S(2)}, u32[]{:S(2)}) %collective-permute-start.31) | collective-permute-done | bytes 1048608 | tf_op jit(solution)/shard_map/ppermute | solution.py:297
  151.7 1.5 collective-permute-start.29
  154.0 0.9 collective-permute-start.32
  154.9 0.7 collective-permute-done.29
  155.7 3.5 %collective-permute-start.30 = (bf16[2,4,4096]{2,1,0:T(4,128)(2,1)S(1)}, bf16[2,4,4096]{2,1,0:T(4,128)(2,1)S(1)}, u32[]{:S(2)}, u32[]{:S(2)}) collective-permute-start(bf16[2,4,4096]{2,1,0:T(4,128)(2,1)S(1)} %broadcast_select_fusion.2), channel_id=1, source_target_pairs={{0,1},{1,0},{2,3},{3,2},{4,5},{5,4},{6,7},{7,6},{8,9},{9,8},{10,11... | collective-permute-start | bytes 196616 | tf_op jit(solution)/shard_map/ppermute | solution.py:284
  159.2 1.7 collective-permute-done.33
  160.9 7.9 %collective-permute-done.32 = bf16[64,16,128]{2,1,0:T(8,128)(2,1)S(1)} collective-permute-done((bf16[64,16,128]{2,1,0:T(8,128)(2,1)S(1)}, bf16[64,16,128]{2,1,0:T(8,128)(2,1)S(1)}, u32[]{:S(2)}, u32[]{:S(2)}) %collective-permute-start.32) | collective-permute-done | bytes 262176 | tf_op jit(solution)/shard_map/ppermute | solution.py:299
  168.7 0.9 fusion.3
  169.8 0.7 fusion.25
  (69 shorter events, 7.4 us)
Async XLA Ops:
  0.6 46.3 %copy-start.1 = (s32[64]{0:T(128)S(1)}, s32[64]{0:T(128)}, u32[]{:S(2)}) copy-start(s32[64]{0:T(128)} %param.17) | copy-start | bytes 772
  0.6 46.3 %copy-start.2 = (s32[64]{0:T(128)S(1)}, s32[64]{0:T(128)}, u32[]{:S(2)}) copy-start(s32[64]{0:T(128)} %param.14) | copy-start | bytes 772
  1.5 4.2 %collective-permute-start = (bf16[2,4,4096]{2,1,0:T(4,128)(2,1)S(1)}, bf16[2,4,4096]{2,1,0:T(4,128)(2,1)S(1)}, u32[]{:S(2)}, u32[]{:S(2)}) collective-permute-start(bf16[2,4,4096]{2,1,0:T(4,128)(2,1)S(1)} %broadcast_select_fusion.8), channel_id=1, source_target_pairs={{0,1},{1,0},{2,3},{3,2},{4,5},{5,4},{6,7},{7,6},{8,9},{9,8},{10,11... | collective-permute-start | bytes 196616 | tf_op jit(solution)/shard_map/ppermute | solution.py:241
  4.9 3.8 %collective-permute-start.2 = (bf16[2,4,4096]{2,1,0:T(4,128)(2,1)S(1)}, bf16[2,4,4096]{2,1,0:T(4,128)(2,1)S(1)}, u32[]{:S(2)}, u32[]{:S(2)}) collective-permute-start(bf16[2,4,4096]{2,1,0:T(4,128)(2,1)S(1)} %broadcast_select_fusion.8), channel_id=1, source_target_pairs={{0,3},{1,2},{2,1},{3,0},{4,7},{5,6},{6,5},{7,4},{8,11},{9,10},{10,... | collective-permute-start | bytes 196616 | tf_op jit(solution)/shard_map/ppermute | solution.py:243
  6.6 3.2 %collective-permute-start.1 = (bf16[2,4,4096]{2,1,0:T(4,128)(2,1)S(1)}, bf16[2,4,4096]{2,1,0:T(4,128)(2,1)S(1)}, u32[]{:S(2)}, u32[]{:S(2)}) collective-permute-start(bf16[2,4,4096]{2,1,0:T(4,128)(2,1)S(1)} %get-tuple-element.25), channel_id=1, source_target_pairs={{0,2},{1,3},{2,0},{3,1},{4,6},{5,7},{6,4},{7,5},{8,10},{9,11},{10,... | collective-permute-start | bytes 196616 | tf_op jit(solution)/shard_map/ppermute | solution.py:242
  10.0 9.3 %collective-permute-start.6 = (bf16[2,16,4096]{2,1,0:T(8,128)(2,1)S(1)}, bf16[2,16,4096]{2,1,0:T(8,128)(2,1)S(1)}, u32[]{:S(2)}, u32[]{:S(2)}) collective-permute-start(bf16[2,16,4096]{2,1,0:T(8,128)(2,1)S(1)} %pad_maximum_fusion.refs_0_), channel_id=1, source_target_pairs={{0,4},{4,8},{8,12},{12,16},{16,20},{20,24},{24,28},{28,0},{1,5},{5... | collective-permute-start | bytes 786440 | tf_op jit(solution)/shard_map/ppermute | solution.py:256
  10.4 9.0 %collective-permute-start.3 = (bf16[2,16,4096]{2,1,0:T(8,128)(2,1)S(1)}, bf16[2,16,4096]{2,1,0:T(8,128)(2,1)S(1)}, u32[]{:S(2)}, u32[]{:S(2)}) collective-permute-start(bf16[2,16,4096]{2,1,0:T(8,128)(2,1)S(1)} %pad_maximum_fusion.refs_0_), channel_id=1, source_target_pairs={{0,28},{4,0},{8,4},{12,8},{16,12},{20,16},{24,20},{28,24},{1,29},{... | collective-permute-start | bytes 786440 | tf_op jit(solution)/shard_map/ppermute | solution.py:257
  19.4 6.8 %collective-permute-start.7 = (bf16[2,16,4096]{2,1,0:T(8,128)(2,1)S(1)}, bf16[2,16,4096]{2,1,0:T(8,128)(2,1)S(1)}, u32[]{:S(2)}, u32[]{:S(2)}) collective-permute-start(bf16[2,16,4096]{2,1,0:T(8,128)(2,1)S(1)} %collective-permute-done.6.refs_8_), channel_id=1, source_target_pairs={{0,4},{4,8},{8,12},{12,16},{16,20},{20,24},{24,28},{28,0},{1,5},{5... | collective-permute-start | bytes 786440 | tf_op jit(solution)/shard_map/ppermute | solution.py:256
  19.4 10.4 %collective-permute-start.4 = (bf16[2,16,4096]{2,1,0:T(8,128)(2,1)S(1)}, bf16[2,16,4096]{2,1,0:T(8,128)(2,1)S(1)}, u32[]{:S(2)}, u32[]{:S(2)}) collective-permute-start(bf16[2,16,4096]{2,1,0:T(8,128)(2,1)S(1)} %collective-permute-done.3.refs_1_), channel_id=1, source_target_pairs={{0,28},{4,0},{8,4},{12,8},{16,12},{20,16},{24,20},{28,24},{1,29},{... | collective-permute-start | bytes 786440 | tf_op jit(solution)/shard_map/ppermute | solution.py:257
  26.2 6.6 %collective-permute-start.8 = (bf16[2,16,4096]{2,1,0:T(8,128)(2,1)S(1)}, bf16[2,16,4096]{2,1,0:T(8,128)(2,1)S(1)}, u32[]{:S(2)}, u32[]{:S(2)}) collective-permute-start(bf16[2,16,4096]{2,1,0:T(8,128)(2,1)S(1)} %collective-permute-done.7.refs_7_), channel_id=1, source_target_pairs={{0,4},{4,8},{8,12},{12,16},{16,20},{20,24},{24,28},{28,0},{1,5},{5... | collective-permute-start | bytes 786440 | tf_op jit(solution)/shard_map/ppermute | solution.py:256
  26.2 13.0 %collective-permute-start.11 = (bf16[2,16,4096]{2,1,0:T(8,128)(2,1)S(1)}, bf16[2,16,4096]{2,1,0:T(8,128)(2,1)S(1)}, u32[]{:S(2)}, u32[]{:S(2)}) collective-permute-start(bf16[2,16,4096]{2,1,0:T(8,128)(2,1)S(1)} %pad_maximum_fusion.refs_0_), channel_id=1, source_target_pairs={{0,1},{1,0},{2,3},{3,2},{4,5},{5,4},{6,7},{7,6},{8,9},{9,8},{10,11... | collective-permute-start | bytes 786440 | tf_op jit(solution)/shard_map/ppermute | solution.py:261
  29.3 13.3 %collective-permute-start.12 = (bf16[2,16,4096]{2,1,0:T(8,128)(2,1)S(1)}, bf16[2,16,4096]{2,1,0:T(8,128)(2,1)S(1)}, u32[]{:S(2)}, u32[]{:S(2)}) collective-permute-start(bf16[2,16,4096]{2,1,0:T(8,128)(2,1)S(1)} %collective-permute-done.3.refs_1_), channel_id=1, source_target_pairs={{0,1},{1,0},{2,3},{3,2},{4,5},{5,4},{6,7},{7,6},{8,9},{9,8},{10,11... | collective-permute-start | bytes 786440 | tf_op jit(solution)/shard_map/ppermute | solution.py:261
  29.3 14.4 %collective-permute-start.19 = (bf16[2,16,4096]{2,1,0:T(8,128)(2,1)S(1)}, bf16[2,16,4096]{2,1,0:T(8,128)(2,1)S(1)}, u32[]{:S(2)}, u32[]{:S(2)}) collective-permute-start(bf16[2,16,4096]{2,1,0:T(8,128)(2,1)S(1)} %collective-permute-done.6.refs_8_), channel_id=1, source_target_pairs={{0,1},{1,0},{2,3},{3,2},{4,5},{5,4},{6,7},{7,6},{8,9},{9,8},{10,11... | collective-permute-start | bytes 786440 | tf_op jit(solution)/shard_map/ppermute | solution.py:261
  29.8 8.7 %collective-permute-start.5 = (bf16[2,16,4096]{2,1,0:T(8,128)(2,1)S(1)}, bf16[2,16,4096]{2,1,0:T(8,128)(2,1)S(1)}, u32[]{:S(2)}, u32[]{:S(2)}) collective-permute-start(bf16[2,16,4096]{2,1,0:T(8,128)(2,1)S(1)} %collective-permute-done.4.refs_2_), channel_id=1, source_target_pairs={{0,28},{4,0},{8,4},{12,8},{16,12},{20,16},{24,20},{28,24},{1,29},{... | collective-permute-start | bytes 786440 | tf_op jit(solution)/shard_map/ppermute | solution.py:257
  32.8 11.0 %collective-permute-start.13 = (bf16[2,16,4096]{2,1,0:T(8,128)(2,1)S(1)}, bf16[2,16,4096]{2,1,0:T(8,128)(2,1)S(1)}, u32[]{:S(2)}, u32[]{:S(2)}) collective-permute-start(bf16[2,16,4096]{2,1,0:T(8,128)(2,1)S(1)} %collective-permute-done.4.refs_2_), channel_id=1, source_target_pairs={{0,1},{1,0},{2,3},{3,2},{4,5},{5,4},{6,7},{7,6},{8,9},{9,8},{10,11... | collective-permute-start | bytes 786440 | tf_op jit(solution)/shard_map/ppermute | solution.py:261
  38.5 7.0 %collective-permute-start.9 = (bf16[16,4096]{1,0:T(8,128)(2,1)}, bf16[16,4096]{1,0:T(8,128)(2,1)S(1)}, u32[]{:S(2)}, u32[]{:S(2)}) collective-permute-start(bf16[16,4096]{1,0:T(8,128)(2,1)} %slice_bitcast_fusion.17), channel_id=1, source_target_pairs={{0,4},{4,8},{8,12},{12,16},{16,20},{20,24},{24,28},{28,0},{1,5},{5... | collective-permute-start | bytes 393224 | tf_op jit(solution)/shard_map/ppermute | solution.py:258
  39.2 7.4 %collective-permute-start.10 = (bf16[16,4096]{1,0:T(8,128)(2,1)}, bf16[16,4096]{1,0:T(8,128)(2,1)}, u32[]{:S(2)}, u32[]{:S(2)}) collective-permute-start(bf16[16,4096]{1,0:T(8,128)(2,1)} %slice_bitcast_fusion.16), channel_id=1, source_target_pairs={{0,28},{4,0},{8,4},{12,8},{16,12},{20,16},{24,20},{28,24},{1,29},{... | collective-permute-start | bytes 393224 | tf_op jit(solution)/shard_map/ppermute | solution.py:259
  42.6 5.1 %collective-permute-start.18 = (bf16[2,16,4096]{2,1,0:T(8,128)(2,1)S(1)}, bf16[2,16,4096]{2,1,0:T(8,128)(2,1)S(1)}, u32[]{:S(2)}, u32[]{:S(2)}) collective-permute-start(bf16[2,16,4096]{2,1,0:T(8,128)(2,1)S(1)} %collective-permute-done.7.refs_7_), channel_id=1, source_target_pairs={{0,1},{1,0},{2,3},{3,2},{4,5},{5,4},{6,7},{7,6},{8,9},{9,8},{10,11... | collective-permute-start | bytes 786440 | tf_op jit(solution)/shard_map/ppermute | solution.py:261
  43.7 4.6 %collective-permute-start.14 = (bf16[2,16,4096]{2,1,0:T(8,128)(2,1)S(1)}, bf16[2,16,4096]{2,1,0:T(8,128)(2,1)S(1)}, u32[]{:S(2)}, u32[]{:S(2)}) collective-permute-start(bf16[2,16,4096]{2,1,0:T(8,128)(2,1)S(1)} %collective-permute-done.5.refs_3_), channel_id=1, source_target_pairs={{0,1},{1,0},{2,3},{3,2},{4,5},{5,4},{6,7},{7,6},{8,9},{9,8},{10,11... | collective-permute-start | bytes 786440 | tf_op jit(solution)/shard_map/ppermute | solution.py:261
  43.8 4.5 %collective-permute-start.17 = (bf16[2,16,4096]{2,1,0:T(8,128)(2,1)S(1)}, bf16[2,16,4096]{2,1,0:T(8,128)(2,1)}, u32[]{:S(2)}, u32[]{:S(2)}) collective-permute-start(bf16[2,16,4096]{2,1,0:T(8,128)(2,1)S(1)} %collective-permute-done.8.refs_6_), channel_id=1, source_target_pairs={{0,1},{1,0},{2,3},{3,2},{4,5},{5,4},{6,7},{7,6},{8,9},{9,8},{10,11... | collective-permute-start | bytes 786440 | tf_op jit(solution)/shard_map/ppermute | solution.py:261
  45.5 2.2 %collective-permute-start.15 = (bf16[16,4096]{1,0:T(8,128)(2,1)S(1)}, bf16[16,4096]{1,0:T(8,128)(2,1)}, u32[]{:S(2)}, u32[]{:S(2)}) collective-permute-start(bf16[16,4096]{1,0:T(8,128)(2,1)S(1)} %collective-permute-done.9.refs_4_), channel_id=1, source_target_pairs={{0,1},{1,0},{2,3},{3,2},{4,5},{5,4},{6,7},{7,6},{8,9},{9,8},{10,11... | collective-permute-start | bytes 393224 | tf_op jit(solution)/shard_map/ppermute | solution.py:261
  46.6 1.7 collective-permute-start.16
  68.4 4.5 %collective-permute-start.20 = (bf16[2,128,4096]{2,1,0:T(8,128)(2,1)}, bf16[2,128,4096]{2,1,0:T(8,128)(2,1)S(1)}, u32[]{:S(2)}, u32[]{:S(2)}) collective-permute-start(bf16[2,128,4096]{2,1,0:T(8,128)(2,1)} %get-tuple-element.15), channel_id=1, source_target_pairs={{0,1},{1,0},{2,3},{3,2},{4,5},{5,4},{6,7},{7,6},{8,9},{9,8},{10,11... | collective-permute-start | bytes 6291464 | tf_op jit(solution)/shard_map/ppermute | solution.py:266
  75.5 19.3 %collective-permute-start.21 = (bf16[16,4096]{1,0:T(8,128)(2,1)S(1)}, bf16[16,4096]{1,0:T(8,128)(2,1)S(1)}, u32[]{:S(2)}, u32[]{:S(2)}) collective-permute-start(bf16[16,4096]{1,0:T(8,128)(2,1)S(1)} %get-tuple-element.34), channel_id=1, source_target_pairs={{0,4},{4,8},{8,12},{12,16},{16,20},{20,24},{24,28},{28,0},{1,5},{5... | collective-permute-start | bytes 393224 | tf_op jit(solution)/shard_map/ppermute | solution.py:268
  78.1 16.8 %collective-permute-start.25 = (bf16[16,4096]{1,0:T(8,128)(2,1)S(1)}, bf16[16,4096]{1,0:T(8,128)(2,1)S(1)}, u32[]{:S(2)}, u32[]{:S(2)}) collective-permute-start(bf16[16,4096]{1,0:T(8,128)(2,1)S(1)} %get-tuple-element.35), channel_id=1, source_target_pairs={{0,28},{4,0},{8,4},{12,8},{16,12},{20,16},{24,20},{28,24},{1,29},{... | collective-permute-start | bytes 393224 | tf_op jit(solution)/shard_map/ppermute | solution.py:269
  91.1 14.4 %collective-permute-start.37 = (bf16[2,64,16,128]{3,2,1,0:T(8,128)(2,1)}, bf16[2,64,16,128]{3,2,1,0:T(8,128)(2,1)S(1)}, u32[]{:S(2)}, u32[]{:S(2)}) collective-permute-start(bf16[2,64,16,128]{3,2,1,0:T(8,128)(2,1)} %get-tuple-element.23), channel_id=1, source_target_pairs={{0,96},{32,0},{64,32},{96,64},{1,97},{33,1},{65,33},{97,65},{2,98}... | collective-permute-start | bytes 1572872 | tf_op jit(solution)/shard_map/ppermute | solution.py:290
  93.7 14.0 %collective-permute-start.36 = (bf16[2,64,16,128]{3,2,1,0:T(8,128)(2,1)S(1)}, bf16[2,64,16,128]{3,2,1,0:T(8,128)(2,1)S(1)}, u32[]{:S(2)}, u32[]{:S(2)}) collective-permute-start(bf16[2,64,16,128]{3,2,1,0:T(8,128)(2,1)S(1)} %get-tuple-element.22), channel_id=1, source_target_pairs={{0,64},{32,96},{64,0},{96,32},{1,65},{33,97},{65,1},{97,33},{2,66}... | collective-permute-start | bytes 1572872 | tf_op jit(solution)/shard_map/ppermute | solution.py:290
  94.2 26.1 %collective-permute-start.35 = (bf16[2,64,16,128]{3,2,1,0:T(8,128)(2,1)S(1)}, bf16[2,64,16,128]{3,2,1,0:T(8,128)(2,1)S(1)}, u32[]{:S(2)}, u32[]{:S(2)}) collective-permute-start(bf16[2,64,16,128]{3,2,1,0:T(8,128)(2,1)S(1)} %get-tuple-element.21), channel_id=1, source_target_pairs={{0,32},{32,64},{64,96},{96,0},{1,33},{33,65},{65,97},{97,1},{2,34}... | collective-permute-start | bytes 1572872 | tf_op jit(solution)/shard_map/ppermute | solution.py:290
  94.9 28.4 %collective-permute-start.22 = (bf16[2,16,4096]{2,1,0:T(8,128)(2,1)S(1)}, bf16[2,16,4096]{2,1,0:T(8,128)(2,1)S(1)}, u32[]{:S(2)}, u32[]{:S(2)}) collective-permute-start(bf16[2,16,4096]{2,1,0:T(8,128)(2,1)S(1)} %pad_maximum_fusion.1), channel_id=1, source_target_pairs={{0,4},{4,8},{8,12},{12,16},{16,20},{20,24},{24,28},{28,0},{1,5},{5... | collective-permute-start | bytes 786440 | tf_op jit(solution)/shard_map/ppermute | solution.py:273
  95.9 27.4 %collective-permute-start.26 = (bf16[2,16,4096]{2,1,0:T(8,128)(2,1)S(1)}, bf16[2,16,4096]{2,1,0:T(8,128)(2,1)S(1)}, u32[]{:S(2)}, u32[]{:S(2)}) collective-permute-start(bf16[2,16,4096]{2,1,0:T(8,128)(2,1)S(1)} %pad_maximum_fusion.2), channel_id=1, source_target_pairs={{0,28},{4,0},{8,4},{12,8},{16,12},{20,16},{24,20},{28,24},{1,29},{... | collective-permute-start | bytes 786440 | tf_op jit(solution)/shard_map/ppermute | solution.py:274
  120.5 5.9 %copy-start.3 = (bf16[4,64,16,128]{3,2,1,0:T(8,128)(2,1)S(1)}, bf16[4,64,16,128]{3,2,1,0:T(8,128)(2,1)}, u32[]{:S(2)}) copy-start(bf16[4,64,16,128]{3,2,1,0:T(8,128)(2,1)} %get-tuple-element.19) | copy-start | bytes 3145732
  120.6 9.0 %collective-permute-start.38 = (bf16[64,16,128]{2,1,0:T(8,128)(2,1)S(1)}, bf16[64,16,128]{2,1,0:T(8,128)(2,1)S(1)}, u32[]{:S(2)}, u32[]{:S(2)}) collective-permute-start(bf16[64,16,128]{2,1,0:T(8,128)(2,1)S(1)} %fusion.14), channel_id=1, source_target_pairs={{0,128},{128,0},{1,129},{129,1},{2,130},{130,2},{3,131},{131,3},{4... | collective-permute-start | bytes 786440 | tf_op jit(solution)/shard_map/ppermute | solution.py:292
  123.4 27.8 %copy-start = (bf16[4,64,16,128]{3,2,1,0:T(8,128)(2,1)S(1)}, bf16[4,64,16,128]{3,2,1,0:T(8,128)(2,1)}, u32[]{:S(2)}) copy-start(bf16[4,64,16,128]{3,2,1,0:T(8,128)(2,1)} %get-tuple-element.18) | copy-start | bytes 3145732
  123.4 8.6 %collective-permute-start.23 = (bf16[2,16,4096]{2,1,0:T(8,128)(2,1)S(1)}, bf16[2,16,4096]{2,1,0:T(8,128)(2,1)S(1)}, u32[]{:S(2)}, u32[]{:S(2)}) collective-permute-start(bf16[2,16,4096]{2,1,0:T(8,128)(2,1)S(1)} %get-tuple-element.28), channel_id=1, source_target_pairs={{0,4},{4,8},{8,12},{12,16},{16,20},{20,24},{24,28},{28,0},{1,5},{5... | collective-permute-start | bytes 786440 | tf_op jit(solution)/shard_map/ppermute | solution.py:273
  124.6 7.4 %collective-permute-start.27 = (bf16[2,16,4096]{2,1,0:T(8,128)(2,1)S(1)}, bf16[2,16,4096]{2,1,0:T(8,128)(2,1)S(1)}, u32[]{:S(2)}, u32[]{:S(2)}) collective-permute-start(bf16[2,16,4096]{2,1,0:T(8,128)(2,1)S(1)} %get-tuple-element.29), channel_id=1, source_target_pairs={{0,28},{4,0},{8,4},{12,8},{16,12},{20,16},{24,20},{28,24},{1,29},{... | collective-permute-start | bytes 786440 | tf_op jit(solution)/shard_map/ppermute | solution.py:274
  126.4 24.8 %collective-permute-start.31 = (bf16[4,64,16,128]{3,2,1,0:T(8,128)(2,1)S(1)}, bf16[4,64,16,128]{3,2,1,0:T(8,128)(2,1)S(1)}, u32[]{:S(2)}, u32[]{:S(2)}) collective-permute-start(bf16[4,64,16,128]{3,2,1,0:T(8,128)(2,1)S(1)} %copy-done.3), channel_id=1, source_target_pairs={{0,128},{128,0},{1,129},{129,1},{2,130},{130,2},{3,131},{131,3},{4... | collective-permute-start | bytes 3145736 | tf_op jit(solution)/shard_map/ppermute | solution.py:297
  132.1 19.5 %collective-permute-start.28 = (bf16[2,16,4096]{2,1,0:T(8,128)(2,1)S(1)}, bf16[2,16,4096]{2,1,0:T(8,128)(2,1)S(1)}, u32[]{:S(2)}, u32[]{:S(2)}) collective-permute-start(bf16[2,16,4096]{2,1,0:T(8,128)(2,1)S(1)} %get-tuple-element.27), channel_id=1, source_target_pairs={{0,28},{4,0},{8,4},{12,8},{16,12},{20,16},{24,20},{28,24},{1,29},{... | collective-permute-start | bytes 786440 | tf_op jit(solution)/shard_map/ppermute | solution.py:278
  134.5 17.0 %collective-permute-start.24 = (bf16[2,16,4096]{2,1,0:T(8,128)(2,1)S(1)}, bf16[2,16,4096]{2,1,0:T(8,128)(2,1)S(1)}, u32[]{:S(2)}, u32[]{:S(2)}) collective-permute-start(bf16[2,16,4096]{2,1,0:T(8,128)(2,1)S(1)} %get-tuple-element.26), channel_id=1, source_target_pairs={{0,4},{4,8},{8,12},{12,16},{16,20},{20,24},{24,28},{28,0},{1,5},{5... | collective-permute-start | bytes 786440 | tf_op jit(solution)/shard_map/ppermute | solution.py:277
  151.7 3.9 %collective-permute-start.29 = (bf16[2,8,4096]{2,1,0:T(8,128)(2,1)S(1)}, bf16[2,8,4096]{2,1,0:T(8,128)(2,1)S(1)}, u32[]{:S(2)}, u32[]{:S(2)}) collective-permute-start(bf16[2,8,4096]{2,1,0:T(8,128)(2,1)S(1)} %slice.247), channel_id=1, source_target_pairs={{0,2},{2,0},{1,3},{3,1},{4,6},{6,4},{5,7},{7,5},{8,10},{10,8},{9,1... | collective-permute-start | bytes 393224 | tf_op jit(solution)/shard_map/ppermute | solution.py:280
  153.3 5.9 %collective-permute-start.34 = (bf16[64,16,128]{2,1,0:T(8,128)(2,1)S(1)}, bf16[64,16,128]{2,1,0:T(8,128)(2,1)S(1)}, u32[]{:S(2)}, u32[]{:S(2)}) collective-permute-start(bf16[64,16,128]{2,1,0:T(8,128)(2,1)S(1)} %get-tuple-element.39), channel_id=1, source_target_pairs={{0,96},{32,0},{64,32},{96,64},{1,97},{33,1},{65,33},{97,65},{2,98}... | collective-permute-start | bytes 786440 | tf_op jit(solution)/shard_map/ppermute | solution.py:299
  153.4 7.4 %collective-permute-start.33 = (bf16[64,16,128]{2,1,0:T(8,128)(2,1)S(1)}, bf16[64,16,128]{2,1,0:T(8,128)(2,1)S(1)}, u32[]{:S(2)}, u32[]{:S(2)}) collective-permute-start(bf16[64,16,128]{2,1,0:T(8,128)(2,1)S(1)} %get-tuple-element.40), channel_id=1, source_target_pairs={{0,64},{32,96},{64,0},{96,32},{1,65},{33,97},{65,1},{97,33},{2,66}... | collective-permute-start | bytes 786440 | tf_op jit(solution)/shard_map/ppermute | solution.py:299
  154.0 14.7 %collective-permute-start.32 = (bf16[64,16,128]{2,1,0:T(8,128)(2,1)S(1)}, bf16[64,16,128]{2,1,0:T(8,128)(2,1)S(1)}, u32[]{:S(2)}, u32[]{:S(2)}) collective-permute-start(bf16[64,16,128]{2,1,0:T(8,128)(2,1)S(1)} %get-tuple-element.38), channel_id=1, source_target_pairs={{0,32},{32,64},{64,96},{96,0},{1,33},{33,65},{65,97},{97,1},{2,34}... | collective-permute-start | bytes 786440 | tf_op jit(solution)/shard_map/ppermute | solution.py:299
  155.7 14.0 %collective-permute-start.30 = (bf16[2,4,4096]{2,1,0:T(4,128)(2,1)S(1)}, bf16[2,4,4096]{2,1,0:T(4,128)(2,1)S(1)}, u32[]{:S(2)}, u32[]{:S(2)}) collective-permute-start(bf16[2,4,4096]{2,1,0:T(4,128)(2,1)S(1)} %broadcast_select_fusion.2), channel_id=1, source_target_pairs={{0,1},{1,0},{2,3},{3,2},{4,5},{5,4},{6,7},{7,6},{8,9},{9,8},{10,11... | collective-permute-start | bytes 196616 | tf_op jit(solution)/shard_map/ppermute | solution.py:284

commit v2 on v1

v2 whole, which is shorter than its diff:
```python
import jax
import jax.numpy as jnp
from jax import lax
from jax.experimental import pallas as pl
from jax.experimental.pallas import tpu as pltpu
from jax.sharding import Mesh
from jax.sharding import PartitionSpec as P

AXES = ("yh", "x", "z", "yl", "c")
SIZES = (2, 4, 8, 2, 2)
BLK = 128
SB = 4
CAP = 64
DB = 64
WIDTH = DB * BLK
F32 = jnp.float32
BF16 = jnp.bfloat16
GROUP = 32
R1, C1, R2, C2, LIVE1, LIVE2, CORE, PX, PYH = 0, 64, 128, 192, 256, 257, 258, 259, 260
MB = 1024 * 1024


def gelu_pair(v):
    a = 0.7978845608028654
    b = 0.044715
    v2 = v * v
    t = jnp.tanh(a * v * (1.0 + b * v2))
    half = 0.5 * (1.0 + t)
    slope = half + 0.5 * v * (1.0 - t * t) * (a * (1.0 + 3.0 * b * v2))
    return v * half, slope


def lanes(block):
    return pl.ds(pl.multiple_of(block * BLK, BLK), BLK)


def loop(body):
    def group(i, carry):
        for j in range(GROUP):
            body(i * GROUP + j)
        return carry

    lax.fori_loop(0, CAP // GROUP, group, 0)


def dot(a, b, dims):
    return lax.dot_general(a, b, (dims, ((), ())), preferred_element_type=F32)


def join(refs, which, dst):
    for i in range(8):
        low, high = refs[2 * i], refs[2 * i + 1]
        rows = jnp.concatenate([low[which].astype(F32), high[which].astype(F32)], axis=0)
        dst[16 * i : 16 * i + 16] = rows.astype(BF16)


def forward_kernel(meta, w1, w2, *refs):
    pieces = refs[:16]
    hid, gp, tok, grad, own, early, late = refs[16:23]
    pre, back, acc = refs[23:]
    join(pieces, 0, tok)
    join(pieces, 1, grad)
    pre[...] = jnp.zeros_like(pre)
    back[...] = jnp.zeros_like(back)
    n1 = meta[LIVE1]
    n2 = meta[LIVE2]

    def up(s):
        col = jnp.where(s < n1, meta[C1 + s], SB)
        pre[col] += dot(tok[:, lanes(meta[R1 + s])], w1[s], ((1,), (0,)))

    loop(up)

    def down(s):
        row = jnp.where(s < n2, meta[R2 + s], SB)
        back[row] += dot(grad[:, lanes(meta[C2 + s])], w2[s], ((1,), (1,)))

    loop(down)
    for k in range(SB):
        h, slope = gelu_pair(pre[k])
        hid[k] = h.astype(BF16)
        gp[k] = (back[k] * slope).astype(BF16)

    def finish(which):
        for b in range(DB):
            here = slice(b * BLK, (b + 1) * BLK)
            v = acc[b].astype(BF16)
            own[which, :, here] = v[:64]
            early[which, :, here] = v[64:80]
            late[which, :, here] = v[80:]

    acc[...] = jnp.zeros_like(acc)

    def out(s):
        col = jnp.where(s < n2, meta[C2 + s], DB)
        acc[col] += dot(hid[meta[R2 + s]], w2[s], ((1,), (0,)))

    loop(out)
    finish(0)
    acc[...] = jnp.zeros_like(acc)

    def tback(s):
        row = jnp.where(s < n1, meta[R1 + s], DB)
        acc[row] += dot(gp[meta[C1 + s]], w1[s], ((1,), (1,)))

    loop(tback)
    finish(1)


def rel_x(meta, j):
    d = j % 4 - meta[PX]
    return jnp.where(meta[CORE] == 0, d, -d) & 3


def weight1_kernel(meta, gp, tok, near, far):
    n1 = meta[LIVE1]
    pyh = meta[PYH]

    def first(s):
        v = dot(tok[:, lanes(meta[R1 + s])], gp[meta[C1 + s]], ((0,), (0,)))
        v = jnp.where(s < n1, v, 0.0).astype(BF16)
        for j in range(4):
            k = rel_x(meta, j)
            low, high = v[16 * j : 16 * j + 16], v[16 * j + 64 : 16 * j + 80]
            near[k, s] = jnp.where(pyh == 0, low, high)
            far[k, s] = jnp.where(pyh == 0, high, low)

    loop(first)


def weight2_kernel(meta, hid, grad, *outs):
    n2 = meta[LIVE2]
    pyh = meta[PYH]
    stage = outs[4]

    def second(s):
        v = dot(hid[meta[R2 + s]], grad[:, lanes(meta[C2 + s])], ((0,), (0,)))
        v = jnp.where(s < n2, v, 0.0).astype(BF16)
        for j in range(8):
            stage[rel_x(meta, j), (j // 4) ^ pyh, s] = v[16 * j : 16 * j + 16]

    loop(second)
    sem = outs[5]
    copies = [pltpu.make_async_copy(stage.at[k], outs[k], sem.at[k]) for k in range(4)]
    for cp in copies:
        cp.start()
    for cp in copies:
        cp.wait()


VMEM = pl.BlockSpec(memory_space=pltpu.VMEM)
SMEM = pl.BlockSpec(memory_space=pltpu.SMEM)
ANY = pl.BlockSpec(memory_space=pl.ANY)


def run_forward(meta, w1, w2, pieces):
    sd = jax.ShapeDtypeStruct
    return pl.pallas_call(
        forward_kernel,
        out_shape=[
            sd((SB, BLK, BLK), BF16),
            sd((SB, BLK, BLK), BF16),
            sd((BLK, WIDTH), BF16),
            sd((BLK, WIDTH), BF16),
            sd((2, 64, WIDTH), BF16),
            sd((2, 16, WIDTH), BF16),
            sd((2, 48, WIDTH), BF16),
        ],
        in_specs=[SMEM, VMEM, VMEM] + [VMEM] * 16,
        out_specs=[VMEM] * 7,
        scratch_shapes=[
            pltpu.VMEM((SB + 1, BLK, BLK), F32),
            pltpu.VMEM((SB + 1, BLK, BLK), F32),
            pltpu.VMEM((DB + 1, BLK, BLK), F32),
        ],
        compiler_params=pltpu.CompilerParams(vmem_limit_bytes=32 * MB),
        cost_estimate=pl.CostEstimate(flops=1 << 32, bytes_accessed=12 * MB, transcendentals=1 << 16),
        name="forward",
    )(meta, w1, w2, *pieces)


def run_weight1(meta, gp, tok):
    sd = jax.ShapeDtypeStruct
    return pl.pallas_call(
        weight1_kernel,
        out_shape=[sd((4, CAP, 16, BLK), BF16)] * 2,
        in_specs=[SMEM, VMEM, VMEM],
        out_specs=[VMEM] * 2,
        compiler_params=pltpu.CompilerParams(vmem_limit_bytes=16 * MB),
        cost_estimate=pl.CostEstimate(flops=1 << 30, bytes_accessed=4 * MB, transcendentals=0),
        name="weight1",
    )(meta, gp, tok)


def run_weight2(meta, hid, grad):
    sd = jax.ShapeDtypeStruct
    return pl.pallas_call(
        weight2_kernel,
        out_shape=[sd((2, CAP, 16, BLK), BF16)] * 4,
        in_specs=[SMEM, VMEM, VMEM],
        out_specs=[ANY] * 4,
        scratch_shapes=[pltpu.VMEM((4, 2, CAP, 16, BLK), BF16), pltpu.SemaphoreType.DMA((4,))],
        compiler_params=pltpu.CompilerParams(vmem_limit_bytes=16 * MB),
        cost_estimate=pl.CostEstimate(flops=1 << 30, bytes_accessed=4 * MB, transcendentals=0),
        name="weight2",
    )(meta, hid, grad)


def swap(v, axis):
    return lax.ppermute(v, axis, [(0, 1), (1, 0)])


def ring(v, axis, n, sign):
    pairs = []
    for i in range(n):
        for c in range(2):
            step = sign if c == 0 else -sign
            pairs.append((i * 2 + c, ((i + step) % n) * 2 + c))
    if axis == "z":
        full = []
        for i in range(n):
            for y in range(2):
                for c in range(2):
                    step = sign if c == 0 else -sign
                    full.append(((i * 2 + y) * 2 + c, (((i + step) % n) * 2 + y) * 2 + c))
        return lax.ppermute(v, ("z", "yl", "c"), full)
    return lax.ppermute(v, (axis, "c"), pairs)


def f32(v):
    return v.astype(F32)


def narrow(v):
    return v.astype(BF16)


def gather_rows(tokens, grads):
    more_t = swap(tokens, "yl")
    more_g = swap(grads, "yl")
    chunk = jnp.stack([jnp.concatenate([tokens, more_t], 0), jnp.concatenate([grads, more_g], 0)])
    a = [chunk]
    b = [chunk]
    for _ in range(3):
        a.append(ring(a[-1], "z", 8, 1))
        b.append(ring(b[-1], "z", 8, -1))
    a.append(ring(a[-1], "z", 8, 1))
    own = [a[4], a[3], b[3], a[2], b[2], a[1], b[1], a[0]]
    arrival = [7, 5, 6, 3, 4, 1, 2, 0]
    oth = {i: swap(own[i], "c") for i in arrival}
    return own + [oth[i] for i in range(8)]


def reduce_tensor(own, early, late):
    got_early = swap(early, "c")
    got_late = swap(late, "c")

    def part(i):
        mine = f32(own[:, 8 * i : 8 * i + 8])
        if i < 2:
            return mine + f32(got_early[:, 8 * i : 8 * i + 8])
        return mine + f32(got_late[:, 8 * i - 16 : 8 * i - 8])

    a = ring(narrow(part(0)), "z", 8, 1)
    b = ring(narrow(part(1)), "z", 8, -1)
    a = ring(narrow(part(2) + f32(a)), "z", 8, 1)
    b = ring(narrow(part(3) + f32(b)), "z", 8, -1)
    a = ring(narrow(part(4) + f32(a)), "z", 8, 1)
    b = ring(narrow(part(5) + f32(b)), "z", 8, -1)
    a = ring(narrow(part(6) + f32(a)), "z", 8, 1)
    t = part(7) + f32(a) + f32(b)
    got = swap(narrow(t[:, 4:]), "yl")
    t = narrow(t[:, :4] + f32(got))
    return t[0], t[1]


def ring_x(parts):
    a = ring(narrow(parts[2]), "x", 4, 1)
    b = ring(narrow(parts[3]), "x", 4, -1)
    a = ring(narrow(f32(parts[1]) + f32(a)), "x", 4, 1)
    return f32(parts[0]) + f32(a) + f32(b)


def reduce_x_first(parts):
    s = ring_x(parts)
    far = swap(narrow(s[1]), "yh")
    return s[0] + f32(far)


def reduce_y_first(near, far):
    got = swap(far, "yh")
    return ring_x([f32(near[k]) + f32(got[k]) for k in range(4)])


def shards(tokens, grads, w1, w1_rows, w1_cols, w1_count, w2, w2_rows, w2_cols, w2_count):
    stripe = (lax.axis_index("z") * 2 + lax.axis_index("yl")) * 2 + lax.axis_index("c")
    here = jnp.stack([lax.axis_index("c"), lax.axis_index("x"), lax.axis_index("yh")])
    meta = jnp.concatenate(
        [
            w1_rows,
            w1_cols - stripe * SB,
            w2_rows - stripe * SB,
            w2_cols,
            w1_count,
            w2_count,
            here.astype(jnp.int32),
        ]
    )
    pieces = gather_rows(tokens, grads)
    hid, gp, tok, grad, own, early, late = run_forward(meta, w1, w2, pieces)
    near, far = run_weight1(meta, gp, tok)
    parts = run_weight2(meta, hid, grad)
    grad_w1 = reduce_y_first(near, far)
    grad_w2 = reduce_x_first(parts)
    layer_out, grad_tokens = reduce_tensor(own, early, late)
    return layer_out, grad_tokens, grad_w1, grad_w2


def solution(mesh):
    fine = Mesh(mesh.devices.reshape(SIZES), AXES)
    rows = P(AXES, None)
    stripe = ("z", "yl", "c")
    flat = P(stripe)
    blocks = P(stripe, None, None)
    in_specs = (rows, rows, blocks, flat, flat, flat, blocks, flat, flat, flat)
    grads = P(stripe, ("yh", "x"), None)
    out_specs = (rows, rows, grads, grads)
    return jax.shard_map(
        shards, mesh=fine, in_specs=in_specs, out_specs=out_specs, check_vma=False
    )
```

time: 171 us -> 129 us (0.75)
  waiting for transfers between devices: 72 us -> 40.5 us
  Pallas kernels: 32.5 us -> 11.7 us
  starting transfers between devices: 53.3 us -> 63.4 us
  other arithmetic: 8.15 us -> 5.69 us
  local copies, waits for them, and re-layouts: 2.33 us -> 4.72 us
    ppermute x39 -> x35, waiting for transfers between devices: 72 us -> 40.5 us  [the longest x15 19.4 us: swap(): return lax.ppermute(v, axis, [(0, 1), (1, 0)])]
    pallas_call x1, Pallas kernels: 20.1 us -> 8.36 us  [run_forward(): pl.pallas_call(forward_kernel, out_shape=[sd((SB, BLK, BLK), BF16), sd((S...]
    ppermute x39 -> x35, starting transfers between devices: 53.3 us -> 63.4 us  [the longest x15 27.6 us: swap(): return lax.ppermute(v, axis, [(0, 1), (1, 0)])]
    pallas_call x1 -> x2, Pallas kernels: 12.4 us -> 3.35 us  [the longest x1 1.74 us: run_weight2(): pl.pallas_call(weight2_kernel, out_shape=[sd((2, CAP, 16, BLK), BF16)] *...]
    unnamed x8 -> x4, local copies, waits for them, and re-layouts: 0.02 us -> 3.18 us
    add x4 -> x3, other arithmetic: 3.58 us -> 1.26 us  [the longest x2 1.13 us: ring_x(): return f32(parts[0]) + f32(a) + f32(b)]
    select_n x6 -> x0, other arithmetic: 1.92 us -> none  [the longest x1 0.89 us: gather_rows(): jnp.where(low, mine, one)]
  transfers between devices with their start and end apart: 39 -> 35, of which waited for: 17 -> 13; matrix products, arithmetic and copies ran while one was open for 3% -> 4% of each run, Pallas kernels for 7% -> 3%
where the time goes in v2:
time: 129 us; the launch traced here: 128 us
  starting transfers between devices  63.4 us (49%)
  waiting for transfers between devices  40.5 us (31%)
  Pallas kernels  11.7 us (9%)
  other arithmetic  5.69 us (4%)
  local copies, waits for them, and re-layouts  4.72 us (4%)
  between operations  2.16 us (2%)
    ppermute x15, starting transfers between devices, swap(): return lax.ppermute(v, axis, [(0, 1), (1, 0)])  27.6 us
    ppermute x14, starting transfers between devices, ring(): return lax.ppermute(v, ('z', 'yl', 'c'), full)  22.6 us
    ppermute x15, waiting for transfers between devices, swap(): return lax.ppermute(v, axis, [(0, 1), (1, 0)])  19.4 us
    ppermute x14, waiting for transfers between devices, ring(): return lax.ppermute(v, ('z', 'yl', 'c'), full)  19 us
    ppermute x6, starting transfers between devices, ring(): return lax.ppermute(v, (axis, 'c'), pairs)  13.2 us
    pallas_call x1, Pallas kernels, run_forward(): pl.pallas_call(forward_kernel, out_shape=[sd((SB, BLK, BLK), BF16), sd((S...  8.36 us
    unnamed x4, local copies, waits for them, and re-layouts  3.18 us
  transfers between devices with their start and end apart: 35, of which 13 were waited for; matrix products, arithmetic and copies ran while one was open for 4% of the time, Pallas kernels for 3%

profile of v2, /device:TPU:1, one launch (start us, length us, event | category | flops | bytes accessed | tf_op | source)
XLA Modules:
  0.0 128.1 jit_solution(13886188354227289163)
XLA Ops:
  0.6 2.2 %collective-permute-start = (bf16[4,8192]{1,0:T(4,128)(2,1)}, bf16[4,8192]{1,0:T(4,128)(2,1)S(1)}, u32[]{:S(2)}, u32[]{:S(2)}) collective-permute-start(bf16[4,8192]{1,0:T(4,128)(2,1)} %param.10), channel_id=1, source_target_pairs={{0,2},{2,0},{1,3},{3,1},{4,6},{6,4},{5,7},{7,5},{8,10},{10,8},{9,1... | collective-permute-start | bytes 196616 | tf_op jit(solution)/shard_map/ppermute | solution.py:210
  2.9 1.8 %collective-permute-done = bf16[4,8192]{1,0:T(4,128)(2,1)S(1)} collective-permute-done((bf16[4,8192]{1,0:T(4,128)(2,1)}, bf16[4,8192]{1,0:T(4,128)(2,1)S(1)}, u32[]{:S(2)}, u32[]{:S(2)}) %collective-permute-start) | collective-permute-done | bytes 65568 | tf_op jit(solution)/shard_map/ppermute | solution.py:210
  4.7 0.9 maximum_bitcast_fusion
  5.6 0.6 collective-permute-done.1
  6.2 0.9 maximum_bitcast_fusion.1
  7.1 6.3 %collective-permute-start.2 = (bf16[2,8,8192]{2,1,0:T(8,128)(2,1)S(1)}, bf16[2,8,8192]{2,1,0:T(8,128)(2,1)S(1)}, u32[]{:S(2)}, u32[]{:S(2)}) collective-permute-start(bf16[2,8,8192]{2,1,0:T(8,128)(2,1)S(1)} %pad_maximum_fusion.refs_7_), channel_id=1, source_target_pairs={{0,4},{1,29},{2,6},{3,31},{4,8},{5,1},{6,10},{7,3},{8,12},{9,5},{1... | collective-permute-start | bytes 786440 | tf_op jit(solution)/shard_map/ppermute | solution.py:226
  13.4 4.1 %collective-permute-done.2.refs_5_ = bf16[2,8,8192]{2,1,0:T(8,128)(2,1)S(1)} collective-permute-done((bf16[2,8,8192]{2,1,0:T(8,128)(2,1)S(1)}, bf16[2,8,8192]{2,1,0:T(8,128)(2,1)S(1)}, u32[]{:S(2)}, u32[]{:S(2)}) %collective-permute-start.2) | collective-permute-done | bytes 262176 | tf_op jit(solution)/shard_map/ppermute | solution.py:226
  17.5 3.4 %collective-permute-start.3 = (bf16[2,8,8192]{2,1,0:T(8,128)(2,1)S(1)}, bf16[2,8,8192]{2,1,0:T(8,128)(2,1)S(1)}, u32[]{:S(2)}, u32[]{:S(2)}) collective-permute-start(bf16[2,8,8192]{2,1,0:T(8,128)(2,1)S(1)} %collective-permute-done.2.refs_5_), channel_id=1, source_target_pairs={{0,4},{1,29},{2,6},{3,31},{4,8},{5,1},{6,10},{7,3},{8,12},{9,5},{1... | collective-permute-start | bytes 786440 | tf_op jit(solution)/shard_map/ppermute | solution.py:226
  20.9 0.7 collective-permute-done.6.refs_6_
  21.6 2.6 %collective-permute-done.3.refs_3_ = bf16[2,8,8192]{2,1,0:T(8,128)(2,1)S(1)} collective-permute-done((bf16[2,8,8192]{2,1,0:T(8,128)(2,1)S(1)}, bf16[2,8,8192]{2,1,0:T(8,128)(2,1)S(1)}, u32[]{:S(2)}, u32[]{:S(2)}) %collective-permute-start.3) | collective-permute-done | bytes 262176 | tf_op jit(solution)/shard_map/ppermute | solution.py:226
  24.2 3.1 %collective-permute-start.4 = (bf16[2,8,8192]{2,1,0:T(8,128)(2,1)S(1)}, bf16[2,8,8192]{2,1,0:T(8,128)(2,1)S(1)}, u32[]{:S(2)}, u32[]{:S(2)}) collective-permute-start(bf16[2,8,8192]{2,1,0:T(8,128)(2,1)S(1)} %collective-permute-done.3.refs_3_), channel_id=1, source_target_pairs={{0,4},{1,29},{2,6},{3,31},{4,8},{5,1},{6,10},{7,3},{8,12},{9,5},{1... | collective-permute-start | bytes 786440 | tf_op jit(solution)/shard_map/ppermute | solution.py:226
  27.4 4.2 %collective-permute-start.16 = (bf16[2,8,8192]{2,1,0:T(8,128)(2,1)S(1)}, bf16[2,8,8192]{2,1,0:T(8,128)(2,1)S(1)}, u32[]{:S(2)}, u32[]{:S(2)}) collective-permute-start(bf16[2,8,8192]{2,1,0:T(8,128)(2,1)S(1)} %pad_maximum_fusion.refs_7_), channel_id=1, source_target_pairs={{0,1},{1,0},{2,3},{3,2},{4,5},{5,4},{6,7},{7,6},{8,9},{9,8},{10,11... | collective-permute-start | bytes 786440 | tf_op jit(solution)/shard_map/ppermute | solution.py:210
  31.6 0.5 collective-permute-start.14
  32.1 3.0 %collective-permute-start.5 = (bf16[2,8,8192]{2,1,0:T(8,128)(2,1)S(1)}, bf16[2,8,8192]{2,1,0:T(8,128)(2,1)S(1)}, u32[]{:S(2)}, u32[]{:S(2)}) collective-permute-start(bf16[2,8,8192]{2,1,0:T(8,128)(2,1)S(1)} %collective-permute-done.4.refs_1_), channel_id=1, source_target_pairs={{0,4},{1,29},{2,6},{3,31},{4,8},{5,1},{6,10},{7,3},{8,12},{9,5},{1... | collective-permute-start | bytes 786440 | tf_op jit(solution)/shard_map/ppermute | solution.py:226
  35.1 6.5 %collective-permute-start.13 = (bf16[2,8,8192]{2,1,0:T(8,128)(2,1)S(1)}, bf16[2,8,8192]{2,1,0:T(8,128)(2,1)S(1)}, u32[]{:S(2)}, u32[]{:S(2)}) collective-permute-start(bf16[2,8,8192]{2,1,0:T(8,128)(2,1)S(1)} %collective-permute-done.7.refs_4_), channel_id=1, source_target_pairs={{0,1},{1,0},{2,3},{3,2},{4,5},{5,4},{6,7},{7,6},{8,9},{9,8},{10,11... | collective-permute-start | bytes 786440 | tf_op jit(solution)/shard_map/ppermute | solution.py:210
  41.7 0.4 collective-permute-start.10
  42.2 6.9 %collective-permute-start.9 = (bf16[2,8,8192]{2,1,0:T(8,128)(2,1)S(1)}, bf16[2,8,8192]{2,1,0:T(8,128)(2,1)}, u32[]{:S(2)}, u32[]{:S(2)}) collective-permute-start(bf16[2,8,8192]{2,1,0:T(8,128)(2,1)S(1)} %collective-permute-done.5.refs_0_), channel_id=1, source_target_pairs={{0,1},{1,0},{2,3},{3,2},{4,5},{5,4},{6,7},{7,6},{8,9},{9,8},{10,11... | collective-permute-start | bytes 786440 | tf_op jit(solution)/shard_map/ppermute | solution.py:210
  50.5 0.7 broadcast_subtract_fusion
  51.2 0.7 concatenate.9.meta
  52.0 1.6 %copy-done = bf16[64,128,128]{2,1,0:T(8,128)(2,1)S(1)} copy-done((bf16[64,128,128]{2,1,0:T(8,128)(2,1)S(1)}, bf16[64,128,128]{2,1,0:T(8,128)(2,1)}, u32[]{:S(2)}) %copy-start) | copy-done | bytes 2097176
  53.6 1.6 %copy-done.1 = bf16[64,128,128]{2,1,0:T(8,128)(2,1)S(1)} copy-done((bf16[64,128,128]{2,1,0:T(8,128)(2,1)S(1)}, bf16[64,128,128]{2,1,0:T(8,128)(2,1)}, u32[]{:S(2)}) %copy-start.1) | copy-done | bytes 2097176
  55.1 8.4 %forward.1 = (bf16[4,128,128]{2,1,0:T(8,128)(2,1)S(1)}, bf16[4,128,128]{2,1,0:T(8,128)(2,1)S(1)}, bf16[128,8192]{1,0:T(8,128)(2,1)S(1)}, bf16[128,8192]{1,0:T(8,...) custom-call(s32[261]{0:T(512)S(1)} %concatenate.9.meta, ...), custom_call_target="tpu_custom_call" | custom-call | flops 4294967296 | bytes 12582912 | tf_op jit(solution)/shard_map/forward/pallas_call | solution.py:158
  63.6 0.5 collective-permute-start.17
  64.1 1.4 %collective-permute-done.18 = bf16[2,16,8192]{2,1,0:T(8,128)(2,1)S(1)} collective-permute-done((bf16[2,16,8192]{2,1,0:T(8,128)(2,1)S(1)}, bf16[2,16,8192]{2,1,0:T(8,128)(2,1)S(1)}, u32[]{:S(2)}, u32[]{:S(2)}) %collective-permute-start.18) | collective-permute-done | bytes 524320 | tf_op jit(solution)/shard_map/ppermute | solution.py:210
  65.7 5.5 %collective-permute-done.19 = bf16[2,8,8192]{2,1,0:T(8,128)(2,1)S(1)} collective-permute-done((bf16[2,8,8192]{2,1,0:T(8,128)(2,1)S(1)}, bf16[2,8,8192]{2,1,0:T(8,128)(2,1)S(1)}, u32[]{:S(2)}, u32[]{:S(2)}) %collective-permute-start.19) | collective-permute-done | bytes 262176 | tf_op jit(solution)/shard_map/ppermute | solution.py:226
  71.3 1.0 collective-permute-start.20
  72.3 1.7 %weight2.1 = (bf16[2,64,16,128]{3,2,1,0:T(8,128)(2,1)S(1)}, bf16[2,64,16,128]{3,2,1,0:T(8,128)(2,1)S(1)}, bf16[2,64,16,128]{3,2,1,0:T(8,128)(2,1)S(1)}, bf16[2,64,16,128]{3,2,1,0:T(8,128)(2,1)S(1)}) custom-call(s32[261]{0:T(512)S(1)} %concatenate.9.meta, bf16[4,128,128]{2,1,0:T(8,128)(2,1)S(1)} %get-tuple-element.24.hid, ...), custom_call_target="tpu_custom_call" | custom-call | flops 1073741824 | bytes 4194304 | tf_op jit(solution)/shard_map/weight2/pallas_call | solution.py:197
  74.1 2.6 %collective-permute-start.31 = (bf16[2,64,16,128]{3,2,1,0:T(8,128)(2,1)S(1)}, bf16[2,64,16,128]{3,2,1,0:T(8,128)(2,1)S(1)}, u32[]{:S(2)}, u32[]{:S(2)}) collective-permute-start(bf16[2,64,16,128]{3,2,1,0:T(8,128)(2,1)S(1)} %get-tuple-element.28), channel_id=1, source_target_pairs={{0,32},{1,97},{32,64},{33,1},{64,96},{65,33},{96,0},{97,65},{2,34}... | collective-permute-start | bytes 1572872 | tf_op jit(solution)/shard_map/ppermute | solution.py:227
  76.6 1.6 %weight1.1 = (bf16[4,64,16,128]{3,2,1,0:T(8,128)(2,1)S(1)}, bf16[4,64,16,128]{3,2,1,0:T(8,128)(2,1)S(1)}) custom-call(s32[261]{0:T(512)S(1)} %concatenate.9.meta, bf16[4,128,128]{2,1,0:T(8,128)(2,1)S(1)} %get-tuple-element.20.gp, bf16[128,8192]{1,0:T(8,128)(2,1)S(1)} %get-tuple-element.21.tok), custom_call_target="tpu_custom_call" | custom-call | flops 1073741824 | bytes 4194304 | tf_op jit(solution)/shard_map/weight1/pallas_call | solution.py:184
  78.3 2.9 %collective-permute-start.27 = (bf16[4,64,16,128]{3,2,1,0:T(8,128)(2,1)S(1)}, bf16[4,64,16,128]{3,2,1,0:T(8,128)(2,1)S(1)}, u32[]{:S(2)}, u32[]{:S(2)}) collective-permute-start(bf16[4,64,16,128]{3,2,1,0:T(8,128)(2,1)S(1)} %get-tuple-element.23), channel_id=1, source_target_pairs={{0,128},{128,0},{1,129},{129,1},{2,130},{130,2},{3,131},{131,3},{4... | collective-permute-start | bytes 3145736 | tf_op jit(solution)/shard_map/ppermute | solution.py:210
  81.2 0.5 collective-permute-start.23
  81.8 2.2 %collective-permute-start.21 = (bf16[2,8,8192]{2,1,0:T(8,128)(2,1)S(1)}, bf16[2,8,8192]{2,1,0:T(8,128)(2,1)S(1)}, u32[]{:S(2)}, u32[]{:S(2)}) collective-permute-start(bf16[2,8,8192]{2,1,0:T(8,128)(2,1)S(1)} %add_convert_fusion.7), channel_id=1, source_target_pairs={{0,4},{1,29},{2,6},{3,31},{4,8},{5,1},{6,10},{7,3},{8,12},{9,5},{1... | collective-permute-start | bytes 786440 | tf_op jit(solution)/shard_map/ppermute | solution.py:226
  84.1 2.0 %collective-permute-done.31 = bf16[2,64,16,128]{3,2,1,0:T(8,128)(2,1)S(1)} collective-permute-done((bf16[2,64,16,128]{3,2,1,0:T(8,128)(2,1)S(1)}, bf16[2,64,16,128]{3,2,1,0:T(8,128)(2,1)S(1)}, u32[]{:S(2)}, u32[]{:S(2)}) %collective-permute-start.31) | collective-permute-done | bytes 524320 | tf_op jit(solution)/shard_map/ppermute | solution.py:227
  86.2 3.7 %collective-permute-start.32 = (bf16[2,64,16,128]{3,2,1,0:T(8,128)(2,1)S(1)}, bf16[2,64,16,128]{3,2,1,0:T(8,128)(2,1)S(1)}, u32[]{:S(2)}, u32[]{:S(2)}) collective-permute-start(bf16[2,64,16,128]{3,2,1,0:T(8,128)(2,1)S(1)} %add_convert_fusion), channel_id=1, source_target_pairs={{0,32},{1,97},{32,64},{33,1},{64,96},{65,33},{96,0},{97,65},{2,34}... | collective-permute-start | bytes 1572872 | tf_op jit(solution)/shard_map/ppermute | solution.py:227
  89.9 12.5 %collective-permute-done.27 = bf16[4,64,16,128]{3,2,1,0:T(8,128)(2,1)S(1)} collective-permute-done((bf16[4,64,16,128]{3,2,1,0:T(8,128)(2,1)S(1)}, bf16[4,64,16,128]{3,2,1,0:T(8,128)(2,1)S(1)}, u32[]{:S(2)}, u32[]{:S(2)}) %collective-permute-start.27) | collective-permute-done | bytes 1048608 | tf_op jit(solution)/shard_map/ppermute | solution.py:210
  102.6 4.2 %collective-permute-start.28 = (bf16[64,16,128]{2,1,0:T(8,128)(2,1)S(1)}, bf16[64,16,128]{2,1,0:T(8,128)(2,1)S(1)}, u32[]{:S(2)}, u32[]{:S(2)}) collective-permute-start(bf16[64,16,128]{2,1,0:T(8,128)(2,1)S(1)} %get-tuple-element.34), channel_id=1, source_target_pairs={{0,32},{1,97},{32,64},{33,1},{64,96},{65,33},{96,0},{97,65},{2,34}... | collective-permute-start | bytes 786440 | tf_op jit(solution)/shard_map/ppermute | solution.py:227
  106.8 0.2 add_convert_fusion.6
  107.0 0.5 collective-permute-start.24
  107.8 2.9 %collective-permute-start.34 = (bf16[64,16,128]{2,1,0:T(8,128)(2,1)S(1)}, bf16[64,16,128]{2,1,0:T(8,128)(2,1)S(1)}, u32[]{:S(2)}, u32[]{:S(2)}) collective-permute-start(bf16[64,16,128]{2,1,0:T(8,128)(2,1)S(1)} %fusion.5), channel_id=1, source_target_pairs={{0,128},{128,0},{1,129},{129,1},{2,130},{130,2},{3,131},{131,3},{4... | collective-permute-start | bytes 786440 | tf_op jit(solution)/shard_map/ppermute | solution.py:210
  110.8 2.2 %collective-permute-start.22 = (bf16[2,8,8192]{2,1,0:T(8,128)(2,1)S(1)}, bf16[2,8,8192]{2,1,0:T(8,128)(2,1)S(1)}, u32[]{:S(2)}, u32[]{:S(2)}) collective-permute-start(bf16[2,8,8192]{2,1,0:T(8,128)(2,1)S(1)} %get-tuple-element.30), channel_id=1, source_target_pairs={{0,4},{1,29},{2,6},{3,31},{4,8},{5,1},{6,10},{7,3},{8,12},{9,5},{1... | collective-permute-start | bytes 786440 | tf_op jit(solution)/shard_map/ppermute | solution.py:226
  113.0 0.9 collective-permute-done.24
  114.2 2.7 %collective-permute-start.29 = (bf16[64,16,128]{2,1,0:T(8,128)(2,1)S(1)}, bf16[64,16,128]{2,1,0:T(8,128)(2,1)S(1)}, u32[]{:S(2)}, u32[]{:S(2)}) collective-permute-start(bf16[64,16,128]{2,1,0:T(8,128)(2,1)S(1)} %fusion.1), channel_id=1, source_target_pairs={{0,32},{1,97},{32,64},{33,1},{64,96},{65,33},{96,0},{97,65},{2,34}... | collective-permute-start | bytes 786440 | tf_op jit(solution)/shard_map/ppermute | solution.py:227
  116.9 0.8 fusion
  117.7 0.2 collective-permute-done.22
  118.0 5.0 %collective-permute-done.25 = bf16[2,8,8192]{2,1,0:T(8,128)(2,1)S(1)} collective-permute-done((bf16[2,8,8192]{2,1,0:T(8,128)(2,1)S(1)}, bf16[2,8,8192]{2,1,0:T(8,128)(2,1)S(1)}, u32[]{:S(2)}, u32[]{:S(2)}) %collective-permute-start.25) | collective-permute-done | bytes 262176 | tf_op jit(solution)/shard_map/ppermute | solution.py:226
  123.3 0.9 fusion.2
  124.2 3.2 %collective-permute-done.26 = bf16[2,4,8192]{2,1,0:T(4,128)(2,1)S(1)} collective-permute-done((bf16[2,4,8192]{2,1,0:T(4,128)(2,1)S(1)}, bf16[2,4,8192]{2,1,0:T(4,128)(2,1)S(1)}, u32[]{:S(2)}, u32[]{:S(2)}) %collective-permute-start.26) | collective-permute-done | bytes 131104 | tf_op jit(solution)/shard_map/ppermute | solution.py:210
  127.4 0.7 slice_bitcast_fusion.1
  (50 shorter events, 2.0 us)
Async XLA Ops:
  0.6 4.1 %collective-permute-start = (bf16[4,8192]{1,0:T(4,128)(2,1)}, bf16[4,8192]{1,0:T(4,128)(2,1)S(1)}, u32[]{:S(2)}, u32[]{:S(2)}) collective-permute-start(bf16[4,8192]{1,0:T(4,128)(2,1)} %param.10), channel_id=1, source_target_pairs={{0,2},{2,0},{1,3},{3,1},{4,6},{6,4},{5,7},{7,5},{8,10},{10,8},{9,1... | collective-permute-start | bytes 196616 | tf_op jit(solution)/shard_map/ppermute | solution.py:210
  2.8 3.3 %collective-permute-start.1 = (bf16[4,8192]{1,0:T(4,128)(2,1)}, bf16[4,8192]{1,0:T(4,128)(2,1)S(1)}, u32[]{:S(2)}, u32[]{:S(2)}) collective-permute-start(bf16[4,8192]{1,0:T(4,128)(2,1)} %param.11), channel_id=1, source_target_pairs={{0,2},{2,0},{1,3},{3,1},{4,6},{6,4},{5,7},{7,5},{8,10},{10,8},{9,1... | collective-permute-start | bytes 196616 | tf_op jit(solution)/shard_map/ppermute | solution.py:210
  7.1 10.4 %collective-permute-start.2 = (bf16[2,8,8192]{2,1,0:T(8,128)(2,1)S(1)}, bf16[2,8,8192]{2,1,0:T(8,128)(2,1)S(1)}, u32[]{:S(2)}, u32[]{:S(2)}) collective-permute-start(bf16[2,8,8192]{2,1,0:T(8,128)(2,1)S(1)} %pad_maximum_fusion.refs_7_), channel_id=1, source_target_pairs={{0,4},{1,29},{2,6},{3,31},{4,8},{5,1},{6,10},{7,3},{8,12},{9,5},{1... | collective-permute-start | bytes 786440 | tf_op jit(solution)/shard_map/ppermute | solution.py:226
  13.4 8.2 %collective-permute-start.6 = (bf16[2,8,8192]{2,1,0:T(8,128)(2,1)S(1)}, bf16[2,8,8192]{2,1,0:T(8,128)(2,1)S(1)}, u32[]{:S(2)}, u32[]{:S(2)}) collective-permute-start(bf16[2,8,8192]{2,1,0:T(8,128)(2,1)S(1)} %pad_maximum_fusion.refs_7_), channel_id=1, source_target_pairs={{0,28},{1,5},{2,30},{3,7},{4,0},{5,9},{6,2},{7,11},{8,4},{9,13},{1... | collective-permute-start | bytes 786440 | tf_op jit(solution)/shard_map/ppermute | solution.py:226
  17.5 6.7 %collective-permute-start.3 = (bf16[2,8,8192]{2,1,0:T(8,128)(2,1)S(1)}, bf16[2,8,8192]{2,1,0:T(8,128)(2,1)S(1)}, u32[]{:S(2)}, u32[]{:S(2)}) collective-permute-start(bf16[2,8,8192]{2,1,0:T(8,128)(2,1)S(1)} %collective-permute-done.2.refs_5_), channel_id=1, source_target_pairs={{0,4},{1,29},{2,6},{3,31},{4,8},{5,1},{6,10},{7,3},{8,12},{9,5},{1... | collective-permute-start | bytes 786440 | tf_op jit(solution)/shard_map/ppermute | solution.py:226
  21.6 10.4 %collective-permute-start.7 = (bf16[2,8,8192]{2,1,0:T(8,128)(2,1)S(1)}, bf16[2,8,8192]{2,1,0:T(8,128)(2,1)S(1)}, u32[]{:S(2)}, u32[]{:S(2)}) collective-permute-start(bf16[2,8,8192]{2,1,0:T(8,128)(2,1)S(1)} %collective-permute-done.6.refs_6_), channel_id=1, source_target_pairs={{0,28},{1,5},{2,30},{3,7},{4,0},{5,9},{6,2},{7,11},{8,4},{9,13},{1... | collective-permute-start | bytes 786440 | tf_op jit(solution)/shard_map/ppermute | solution.py:226
  24.2 7.8 %collective-permute-start.4 = (bf16[2,8,8192]{2,1,0:T(8,128)(2,1)S(1)}, bf16[2,8,8192]{2,1,0:T(8,128)(2,1)S(1)}, u32[]{:S(2)}, u32[]{:S(2)}) collective-permute-start(bf16[2,8,8192]{2,1,0:T(8,128)(2,1)S(1)} %collective-permute-done.3.refs_3_), channel_id=1, source_target_pairs={{0,4},{1,29},{2,6},{3,31},{4,8},{5,1},{6,10},{7,3},{8,12},{9,5},{1... | collective-permute-start | bytes 786440 | tf_op jit(solution)/shard_map/ppermute | solution.py:226
  27.4 7.8 %collective-permute-start.16 = (bf16[2,8,8192]{2,1,0:T(8,128)(2,1)S(1)}, bf16[2,8,8192]{2,1,0:T(8,128)(2,1)S(1)}, u32[]{:S(2)}, u32[]{:S(2)}) collective-permute-start(bf16[2,8,8192]{2,1,0:T(8,128)(2,1)S(1)} %pad_maximum_fusion.refs_7_), channel_id=1, source_target_pairs={{0,1},{1,0},{2,3},{3,2},{4,5},{5,4},{6,7},{7,6},{8,9},{9,8},{10,11... | collective-permute-start | bytes 786440 | tf_op jit(solution)/shard_map/ppermute | solution.py:210
  31.6 10.1 %collective-permute-start.15 = (bf16[2,8,8192]{2,1,0:T(8,128)(2,1)S(1)}, bf16[2,8,8192]{2,1,0:T(8,128)(2,1)S(1)}, u32[]{:S(2)}, u32[]{:S(2)}) collective-permute-start(bf16[2,8,8192]{2,1,0:T(8,128)(2,1)S(1)} %collective-permute-done.6.refs_6_), channel_id=1, source_target_pairs={{0,1},{1,0},{2,3},{3,2},{4,5},{5,4},{6,7},{7,6},{8,9},{9,8},{10,11... | collective-permute-start | bytes 786440 | tf_op jit(solution)/shard_map/ppermute | solution.py:210
  31.6 10.2 %collective-permute-start.14 = (bf16[2,8,8192]{2,1,0:T(8,128)(2,1)S(1)}, bf16[2,8,8192]{2,1,0:T(8,128)(2,1)S(1)}, u32[]{:S(2)}, u32[]{:S(2)}) collective-permute-start(bf16[2,8,8192]{2,1,0:T(8,128)(2,1)S(1)} %collective-permute-done.2.refs_5_), channel_id=1, source_target_pairs={{0,1},{1,0},{2,3},{3,2},{4,5},{5,4},{6,7},{7,6},{8,9},{9,8},{10,11... | collective-permute-start | bytes 786440 | tf_op jit(solution)/shard_map/ppermute | solution.py:210
  32.1 10.1 %collective-permute-start.8 = (bf16[2,8,8192]{2,1,0:T(8,128)(2,1)S(1)}, bf16[2,8,8192]{2,1,0:T(8,128)(2,1)S(1)}, u32[]{:S(2)}, u32[]{:S(2)}) collective-permute-start(bf16[2,8,8192]{2,1,0:T(8,128)(2,1)S(1)} %collective-permute-done.7.refs_4_), channel_id=1, source_target_pairs={{0,28},{1,5},{2,30},{3,7},{4,0},{5,9},{6,2},{7,11},{8,4},{9,13},{1... | collective-permute-start | bytes 786440 | tf_op jit(solution)/shard_map/ppermute | solution.py:226
  32.1 10.2 %collective-permute-start.5 = (bf16[2,8,8192]{2,1,0:T(8,128)(2,1)S(1)}, bf16[2,8,8192]{2,1,0:T(8,128)(2,1)S(1)}, u32[]{:S(2)}, u32[]{:S(2)}) collective-permute-start(bf16[2,8,8192]{2,1,0:T(8,128)(2,1)S(1)} %collective-permute-done.4.refs_1_), channel_id=1, source_target_pairs={{0,4},{1,29},{2,6},{3,31},{4,8},{5,1},{6,10},{7,3},{8,12},{9,5},{1... | collective-permute-start | bytes 786440 | tf_op jit(solution)/shard_map/ppermute | solution.py:226
  35.1 16.8 %collective-permute-start.13 = (bf16[2,8,8192]{2,1,0:T(8,128)(2,1)S(1)}, bf16[2,8,8192]{2,1,0:T(8,128)(2,1)S(1)}, u32[]{:S(2)}, u32[]{:S(2)}) collective-permute-start(bf16[2,8,8192]{2,1,0:T(8,128)(2,1)S(1)} %collective-permute-done.7.refs_4_), channel_id=1, source_target_pairs={{0,1},{1,0},{2,3},{3,2},{4,5},{5,4},{6,7},{7,6},{8,9},{9,8},{10,11... | collective-permute-start | bytes 786440 | tf_op jit(solution)/shard_map/ppermute | solution.py:210
  41.6 10.3 %collective-permute-start.12 = (bf16[2,8,8192]{2,1,0:T(8,128)(2,1)S(1)}, bf16[2,8,8192]{2,1,0:T(8,128)(2,1)S(1)}, u32[]{:S(2)}, u32[]{:S(2)}) collective-permute-start(bf16[2,8,8192]{2,1,0:T(8,128)(2,1)S(1)} %collective-permute-done.3.refs_3_), channel_id=1, source_target_pairs={{0,1},{1,0},{2,3},{3,2},{4,5},{5,4},{6,7},{7,6},{8,9},{9,8},{10,11... | collective-permute-start | bytes 786440 | tf_op jit(solution)/shard_map/ppermute | solution.py:210
  41.7 10.2 %collective-permute-start.10 = (bf16[2,8,8192]{2,1,0:T(8,128)(2,1)S(1)}, bf16[2,8,8192]{2,1,0:T(8,128)(2,1)}, u32[]{:S(2)}, u32[]{:S(2)}) collective-permute-start(bf16[2,8,8192]{2,1,0:T(8,128)(2,1)S(1)} %collective-permute-done.4.refs_1_), channel_id=1, source_target_pairs={{0,1},{1,0},{2,3},{3,2},{4,5},{5,4},{6,7},{7,6},{8,9},{9,8},{10,11... | collective-permute-start | bytes 786440 | tf_op jit(solution)/shard_map/ppermute | solution.py:210
  42.1 9.8 %collective-permute-start.11 = (bf16[2,8,8192]{2,1,0:T(8,128)(2,1)S(1)}, bf16[2,8,8192]{2,1,0:T(8,128)(2,1)}, u32[]{:S(2)}, u32[]{:S(2)}) collective-permute-start(bf16[2,8,8192]{2,1,0:T(8,128)(2,1)S(1)} %collective-permute-done.8.refs_2_), channel_id=1, source_target_pairs={{0,1},{1,0},{2,3},{3,2},{4,5},{5,4},{6,7},{7,6},{8,9},{9,8},{10,11... | collective-permute-start | bytes 786440 | tf_op jit(solution)/shard_map/ppermute | solution.py:210
  42.2 9.7 %collective-permute-start.9 = (bf16[2,8,8192]{2,1,0:T(8,128)(2,1)S(1)}, bf16[2,8,8192]{2,1,0:T(8,128)(2,1)}, u32[]{:S(2)}, u32[]{:S(2)}) collective-permute-start(bf16[2,8,8192]{2,1,0:T(8,128)(2,1)S(1)} %collective-permute-done.5.refs_0_), channel_id=1, source_target_pairs={{0,1},{1,0},{2,3},{3,2},{4,5},{5,4},{6,7},{7,6},{8,9},{9,8},{10,11... | collective-permute-start | bytes 786440 | tf_op jit(solution)/shard_map/ppermute | solution.py:210
  52.0 1.6 %copy-start = (bf16[64,128,128]{2,1,0:T(8,128)(2,1)S(1)}, bf16[64,128,128]{2,1,0:T(8,128)(2,1)}, u32[]{:S(2)}) copy-start(bf16[64,128,128]{2,1,0:T(8,128)(2,1)} %w1.1) | copy-start | bytes 6291460
  53.6 1.6 %copy-start.1 = (bf16[64,128,128]{2,1,0:T(8,128)(2,1)S(1)}, bf16[64,128,128]{2,1,0:T(8,128)(2,1)}, u32[]{:S(2)}) copy-start(bf16[64,128,128]{2,1,0:T(8,128)(2,1)} %w2.1) | copy-start | bytes 6291460
  63.5 2.0 %collective-permute-start.18 = (bf16[2,16,8192]{2,1,0:T(8,128)(2,1)S(1)}, bf16[2,16,8192]{2,1,0:T(8,128)(2,1)S(1)}, u32[]{:S(2)}, u32[]{:S(2)}) collective-permute-start(bf16[2,16,8192]{2,1,0:T(8,128)(2,1)S(1)} %get-tuple-element.19), channel_id=1, source_target_pairs={{0,1},{1,0},{2,3},{3,2},{4,5},{5,4},{6,7},{7,6},{8,9},{9,8},{10,11... | collective-permute-start | bytes 1572872 | tf_op jit(solution)/shard_map/ppermute | solution.py:210
  63.6 7.6 %collective-permute-start.17 = (bf16[2,48,8192]{2,1,0:T(8,128)(2,1)S(1)}, bf16[2,48,8192]{2,1,0:T(8,128)(2,1)S(1)}, u32[]{:S(2)}, u32[]{:S(2)}) collective-permute-start(bf16[2,48,8192]{2,1,0:T(8,128)(2,1)S(1)} %get-tuple-element.18), channel_id=1, source_target_pairs={{0,1},{1,0},{2,3},{3,2},{4,5},{5,4},{6,7},{7,6},{8,9},{9,8},{10,11... | collective-permute-start | bytes 4718600 | tf_op jit(solution)/shard_map/ppermute | solution.py:210
  65.6 5.6 %collective-permute-start.19 = (bf16[2,8,8192]{2,1,0:T(8,128)(2,1)S(1)}, bf16[2,8,8192]{2,1,0:T(8,128)(2,1)S(1)}, u32[]{:S(2)}, u32[]{:S(2)}) collective-permute-start(bf16[2,8,8192]{2,1,0:T(8,128)(2,1)S(1)} %get-tuple-element.32), channel_id=1, source_target_pairs={{0,4},{1,29},{2,6},{3,31},{4,8},{5,1},{6,10},{7,3},{8,12},{9,5},{1... | collective-permute-start | bytes 786440 | tf_op jit(solution)/shard_map/ppermute | solution.py:226
  71.3 10.4 %collective-permute-start.20 = (bf16[2,8,8192]{2,1,0:T(8,128)(2,1)S(1)}, bf16[2,8,8192]{2,1,0:T(8,128)(2,1)S(1)}, u32[]{:S(2)}, u32[]{:S(2)}) collective-permute-start(bf16[2,8,8192]{2,1,0:T(8,128)(2,1)S(1)} %add_convert_fusion.8), channel_id=1, source_target_pairs={{0,4},{1,29},{2,6},{3,31},{4,8},{5,1},{6,10},{7,3},{8,12},{9,5},{1... | collective-permute-start | bytes 786440 | tf_op jit(solution)/shard_map/ppermute | solution.py:226
  74.1 12.0 %collective-permute-start.31 = (bf16[2,64,16,128]{3,2,1,0:T(8,128)(2,1)S(1)}, bf16[2,64,16,128]{3,2,1,0:T(8,128)(2,1)S(1)}, u32[]{:S(2)}, u32[]{:S(2)}) collective-permute-start(bf16[2,64,16,128]{3,2,1,0:T(8,128)(2,1)S(1)} %get-tuple-element.28), channel_id=1, source_target_pairs={{0,32},{1,97},{32,64},{33,1},{64,96},{65,33},{96,0},{97,65},{2,34}... | collective-permute-start | bytes 1572872 | tf_op jit(solution)/shard_map/ppermute | solution.py:227
  76.6 30.9 %collective-permute-start.33 = (bf16[2,64,16,128]{3,2,1,0:T(8,128)(2,1)S(1)}, bf16[2,64,16,128]{3,2,1,0:T(8,128)(2,1)S(1)}, u32[]{:S(2)}, u32[]{:S(2)}) collective-permute-start(bf16[2,64,16,128]{3,2,1,0:T(8,128)(2,1)S(1)} %get-tuple-element.29), channel_id=1, source_target_pairs={{0,96},{1,33},{32,0},{33,65},{64,32},{65,97},{96,64},{97,1},{2,98}... | collective-permute-start | bytes 1572872 | tf_op jit(solution)/shard_map/ppermute | solution.py:227
  78.3 24.2 %collective-permute-start.27 = (bf16[4,64,16,128]{3,2,1,0:T(8,128)(2,1)S(1)}, bf16[4,64,16,128]{3,2,1,0:T(8,128)(2,1)S(1)}, u32[]{:S(2)}, u32[]{:S(2)}) collective-permute-start(bf16[4,64,16,128]{3,2,1,0:T(8,128)(2,1)S(1)} %get-tuple-element.23), channel_id=1, source_target_pairs={{0,128},{128,0},{1,129},{129,1},{2,130},{130,2},{3,131},{131,3},{4... | collective-permute-start | bytes 3145736 | tf_op jit(solution)/shard_map/ppermute | solution.py:210
  81.2 25.6 %collective-permute-start.23 = (bf16[2,8,8192]{2,1,0:T(8,128)(2,1)S(1)}, bf16[2,8,8192]{2,1,0:T(8,128)(2,1)S(1)}, u32[]{:S(2)}, u32[]{:S(2)}) collective-permute-start(bf16[2,8,8192]{2,1,0:T(8,128)(2,1)S(1)} %get-tuple-element.33), channel_id=1, source_target_pairs={{0,28},{1,5},{2,30},{3,7},{4,0},{5,9},{6,2},{7,11},{8,4},{9,13},{1... | collective-permute-start | bytes 786440 | tf_op jit(solution)/shard_map/ppermute | solution.py:226
  81.8 25.0 %collective-permute-start.21 = (bf16[2,8,8192]{2,1,0:T(8,128)(2,1)S(1)}, bf16[2,8,8192]{2,1,0:T(8,128)(2,1)S(1)}, u32[]{:S(2)}, u32[]{:S(2)}) collective-permute-start(bf16[2,8,8192]{2,1,0:T(8,128)(2,1)S(1)} %add_convert_fusion.7), channel_id=1, source_target_pairs={{0,4},{1,29},{2,6},{3,31},{4,8},{5,1},{6,10},{7,3},{8,12},{9,5},{1... | collective-permute-start | bytes 786440 | tf_op jit(solution)/shard_map/ppermute | solution.py:226
  86.2 21.3 %collective-permute-start.32 = (bf16[2,64,16,128]{3,2,1,0:T(8,128)(2,1)S(1)}, bf16[2,64,16,128]{3,2,1,0:T(8,128)(2,1)S(1)}, u32[]{:S(2)}, u32[]{:S(2)}) collective-permute-start(bf16[2,64,16,128]{3,2,1,0:T(8,128)(2,1)S(1)} %add_convert_fusion), channel_id=1, source_target_pairs={{0,32},{1,97},{32,64},{33,1},{64,96},{65,33},{96,0},{97,65},{2,34}... | collective-permute-start | bytes 1572872 | tf_op jit(solution)/shard_map/ppermute | solution.py:227
  102.6 11.4 %collective-permute-start.28 = (bf16[64,16,128]{2,1,0:T(8,128)(2,1)S(1)}, bf16[64,16,128]{2,1,0:T(8,128)(2,1)S(1)}, u32[]{:S(2)}, u32[]{:S(2)}) collective-permute-start(bf16[64,16,128]{2,1,0:T(8,128)(2,1)S(1)} %get-tuple-element.34), channel_id=1, source_target_pairs={{0,32},{1,97},{32,64},{33,1},{64,96},{65,33},{96,0},{97,65},{2,34}... | collective-permute-start | bytes 786440 | tf_op jit(solution)/shard_map/ppermute | solution.py:227
  106.8 16.4 %collective-permute-start.30 = (bf16[64,16,128]{2,1,0:T(8,128)(2,1)S(1)}, bf16[64,16,128]{2,1,0:T(8,128)(2,1)S(1)}, u32[]{:S(2)}, u32[]{:S(2)}) collective-permute-start(bf16[64,16,128]{2,1,0:T(8,128)(2,1)S(1)} %get-tuple-element.35), channel_id=1, source_target_pairs={{0,96},{1,33},{32,0},{33,65},{64,32},{65,97},{96,64},{97,1},{2,98}... | collective-permute-start | bytes 786440 | tf_op jit(solution)/shard_map/ppermute | solution.py:227
  107.0 6.8 %collective-permute-start.24 = (bf16[2,8,8192]{2,1,0:T(8,128)(2,1)S(1)}, bf16[2,8,8192]{2,1,0:T(8,128)(2,1)S(1)}, u32[]{:S(2)}, u32[]{:S(2)}) collective-permute-start(bf16[2,8,8192]{2,1,0:T(8,128)(2,1)S(1)} %get-tuple-element.31), channel_id=1, source_target_pairs={{0,28},{1,5},{2,30},{3,7},{4,0},{5,9},{6,2},{7,11},{8,4},{9,13},{1... | collective-permute-start | bytes 786440 | tf_op jit(solution)/shard_map/ppermute | solution.py:226
  107.8 9.1 %collective-permute-start.34 = (bf16[64,16,128]{2,1,0:T(8,128)(2,1)S(1)}, bf16[64,16,128]{2,1,0:T(8,128)(2,1)S(1)}, u32[]{:S(2)}, u32[]{:S(2)}) collective-permute-start(bf16[64,16,128]{2,1,0:T(8,128)(2,1)S(1)} %fusion.5), channel_id=1, source_target_pairs={{0,128},{128,0},{1,129},{129,1},{2,130},{130,2},{3,131},{131,3},{4... | collective-permute-start | bytes 786440 | tf_op jit(solution)/shard_map/ppermute | solution.py:210
  110.8 7.2 %collective-permute-start.22 = (bf16[2,8,8192]{2,1,0:T(8,128)(2,1)S(1)}, bf16[2,8,8192]{2,1,0:T(8,128)(2,1)S(1)}, u32[]{:S(2)}, u32[]{:S(2)}) collective-permute-start(bf16[2,8,8192]{2,1,0:T(8,128)(2,1)S(1)} %get-tuple-element.30), channel_id=1, source_target_pairs={{0,4},{1,29},{2,6},{3,31},{4,8},{5,1},{6,10},{7,3},{8,12},{9,5},{1... | collective-permute-start | bytes 786440 | tf_op jit(solution)/shard_map/ppermute | solution.py:226
  113.9 9.0 %collective-permute-start.25 = (bf16[2,8,8192]{2,1,0:T(8,128)(2,1)S(1)}, bf16[2,8,8192]{2,1,0:T(8,128)(2,1)S(1)}, u32[]{:S(2)}, u32[]{:S(2)}) collective-permute-start(bf16[2,8,8192]{2,1,0:T(8,128)(2,1)S(1)} %add_convert_fusion.3), channel_id=1, source_target_pairs={{0,28},{1,5},{2,30},{3,7},{4,0},{5,9},{6,2},{7,11},{8,4},{9,13},{1... | collective-permute-start | bytes 786440 | tf_op jit(solution)/shard_map/ppermute | solution.py:226
  114.2 9.1 %collective-permute-start.29 = (bf16[64,16,128]{2,1,0:T(8,128)(2,1)S(1)}, bf16[64,16,128]{2,1,0:T(8,128)(2,1)S(1)}, u32[]{:S(2)}, u32[]{:S(2)}) collective-permute-start(bf16[64,16,128]{2,1,0:T(8,128)(2,1)S(1)} %fusion.1), channel_id=1, source_target_pairs={{0,32},{1,97},{32,64},{33,1},{64,96},{65,33},{96,0},{97,65},{2,34}... | collective-permute-start | bytes 786440 | tf_op jit(solution)/shard_map/ppermute | solution.py:227
  123.1 4.2 %collective-permute-start.26 = (bf16[2,4,8192]{2,1,0:T(4,128)(2,1)S(1)}, bf16[2,4,8192]{2,1,0:T(4,128)(2,1)S(1)}, u32[]{:S(2)}, u32[]{:S(2)}) collective-permute-start(bf16[2,4,8192]{2,1,0:T(4,128)(2,1)S(1)} %slice.176), channel_id=1, source_target_pairs={{0,2},{2,0},{1,3},{3,1},{4,6},{6,4},{5,7},{7,5},{8,10},{10,8},{9,1... | collective-permute-start | bytes 393224 | tf_op jit(solution)/shard_map/ppermute | solution.py:210

commit v3 on v2

--- a/solution.py
+++ b/solution.py
@@ -54,26 +54,21 @@
         dst[16 * i : 16 * i + 16] = rows.astype(BF16)
 
 
-def forward_kernel(meta, w1, w2, *refs):
+def hidden_kernel(meta, w1, w2, *refs):
     pieces = refs[:16]
-    hid, gp, tok, grad, own, early, late = refs[16:23]
-    pre, back, acc = refs[23:]
+    hid, gp, tok, grad, pre, back = refs[16:]
     join(pieces, 0, tok)
     join(pieces, 1, grad)
     pre[...] = jnp.zeros_like(pre)
     back[...] = jnp.zeros_like(back)
-    n1 = meta[LIVE1]
-    n2 = meta[LIVE2]
 
     def up(s):
-        col = jnp.where(s < n1, meta[C1 + s], SB)
-        pre[col] += dot(tok[:, lanes(meta[R1 + s])], w1[s], ((1,), (0,)))
+        pre[meta[C1 + s]] += dot(tok[:, lanes(meta[R1 + s])], w1[s], ((1,), (0,)))
 
     loop(up)
 
     def down(s):
-        row = jnp.where(s < n2, meta[R2 + s], SB)
-        back[row] += dot(grad[:, lanes(meta[C2 + s])], w2[s], ((1,), (1,)))
+        back[meta[R2 + s]] += dot(grad[:, lanes(meta[C2 + s])], w2[s], ((1,), (1,)))
 
     loop(down)
     for k in range(SB):
@@ -81,27 +76,26 @@
         hid[k] = h.astype(BF16)
         gp[k] = (back[k] * slope).astype(BF16)
 
+
+def partial_kernel(meta, w1, w2, hid, gp, own, other, acc):
     def finish(which):
         for b in range(DB):
             here = slice(b * BLK, (b + 1) * BLK)
-            v = acc[b].astype(BF16)
-            own[which, :, here] = v[:64]
-            early[which, :, here] = v[64:80]
-            late[which, :, here] = v[80:]
+            v = acc[b]
+            own[which, :, here] = v[:64].astype(BF16)
+            other[which, :, here] = v[64:].astype(BF16)
 
     acc[...] = jnp.zeros_like(acc)
 
     def out(s):
-        col = jnp.where(s < n2, meta[C2 + s], DB)
-        acc[col] += dot(hid[meta[R2 + s]], w2[s], ((1,), (0,)))
+        acc[meta[C2 + s]] += dot(hid[meta[R2 + s]], w2[s], ((1,), (0,)))
 
     loop(out)
     finish(0)
     acc[...] = jnp.zeros_like(acc)
 
     def tback(s):
-        row = jnp.where(s < n1, meta[R1 + s], DB)
-        acc[row] += dot(gp[meta[C1 + s]], w1[s], ((1,), (1,)))
+        acc[meta[R1 + s]] += dot(gp[meta[C1 + s]], w1[s], ((1,), (1,)))
 
     loop(tback)
     finish(1)
@@ -153,30 +147,34 @@
 ANY = pl.BlockSpec(memory_space=pl.ANY)
 
 
-def run_forward(meta, w1, w2, pieces):
-    sd = jax.ShapeDtypeStruct
+def sds(*shape):
+    return jax.ShapeDtypeStruct(shape, BF16)
+
+
+def run_hidden(meta, w1, w2, pieces):
     return pl.pallas_call(
-        forward_kernel,
-        out_shape=[
-            sd((SB, BLK, BLK), BF16),
-            sd((SB, BLK, BLK), BF16),
-            sd((BLK, WIDTH), BF16),
-            sd((BLK, WIDTH), BF16),
-            sd((2, 64, WIDTH), BF16),
-            sd((2, 16, WIDTH), BF16),
-            sd((2, 48, WIDTH), BF16),
-        ],
+        hidden_kernel,
+        out_shape=[sds(SB, BLK, BLK)] * 2 + [sds(BLK, WIDTH)] * 2,
         in_specs=[SMEM, VMEM, VMEM] + [VMEM] * 16,
-        out_specs=[VMEM] * 7,
-        scratch_shapes=[
-            pltpu.VMEM((SB + 1, BLK, BLK), F32),
-            pltpu.VMEM((SB + 1, BLK, BLK), F32),
-            pltpu.VMEM((DB + 1, BLK, BLK), F32),
-        ],
-        compiler_params=pltpu.CompilerParams(vmem_limit_bytes=32 * MB),
-        cost_estimate=pl.CostEstimate(flops=1 << 32, bytes_accessed=12 * MB, transcendentals=1 << 16),
-        name="forward",
+        out_specs=[VMEM] * 4,
+        scratch_shapes=[pltpu.VMEM((SB, BLK, BLK), F32)] * 2,
+        compiler_params=pltpu.CompilerParams(vmem_limit_bytes=24 * MB),
+        cost_estimate=pl.CostEstimate(flops=1 << 31, bytes_accessed=12 * MB, transcendentals=1 << 16),
+        name="hidden",
     )(meta, w1, w2, *pieces)
+
+
+def run_partial(meta, w1, w2, hid, gp):
+    return pl.pallas_call(
+        partial_kernel,
+        out_shape=[sds(2, 64, WIDTH)] * 2,
+        in_specs=[SMEM] + [VMEM] * 4,
+        out_specs=[VMEM] * 2,
+        scratch_shapes=[pltpu.VMEM((DB, BLK, BLK), F32)],
+        compiler_params=pltpu.CompilerParams(vmem_limit_bytes=24 * MB),
+        cost_estimate=pl.CostEstimate(flops=1 << 31, bytes_accessed=12 * MB, transcendentals=0),
+        name="partial",
+    )(meta, w1, w2, hid, gp)
 
 
 def run_weight1(meta, gp, tok):
@@ -235,84 +233,118 @@
     return v.astype(BF16)
 
 
-def gather_rows(tokens, grads):
+def tie(*values):
+    return lax.optimization_barrier(values)
+
+
+def gather_rows(tokens, grads, early):
     more_t = swap(tokens, "yl")
     more_g = swap(grads, "yl")
     chunk = jnp.stack([jnp.concatenate([tokens, more_t], 0), jnp.concatenate([grads, more_g], 0)])
+    early = prepare(*tie(chunk, *early)[1:])
+    later, *early = tie(chunk, *early)
     a = [chunk]
-    b = [chunk]
+    b = [later]
     for _ in range(3):
         a.append(ring(a[-1], "z", 8, 1))
         b.append(ring(b[-1], "z", 8, -1))
     a.append(ring(a[-1], "z", 8, 1))
     own = [a[4], a[3], b[3], a[2], b[2], a[1], b[1], a[0]]
-    arrival = [7, 5, 6, 3, 4, 1, 2, 0]
-    oth = {i: swap(own[i], "c") for i in arrival}
-    return own + [oth[i] for i in range(8)]
-
-
-def reduce_tensor(own, early, late):
-    got_early = swap(early, "c")
-    got_late = swap(late, "c")
-
+    return own + [swap(v, "c") for v in own], early
+
+
+def reduce_all(own, other, near, far, parts):
     def part(i):
-        mine = f32(own[:, 8 * i : 8 * i + 8])
-        if i < 2:
-            return mine + f32(got_early[:, 8 * i : 8 * i + 8])
-        return mine + f32(got_late[:, 8 * i - 16 : 8 * i - 8])
-
-    a = ring(narrow(part(0)), "z", 8, 1)
-    b = ring(narrow(part(1)), "z", 8, -1)
-    a = ring(narrow(part(2) + f32(a)), "z", 8, 1)
-    b = ring(narrow(part(3) + f32(b)), "z", 8, -1)
-    a = ring(narrow(part(4) + f32(a)), "z", 8, 1)
-    b = ring(narrow(part(5) + f32(b)), "z", 8, -1)
-    a = ring(narrow(part(6) + f32(a)), "z", 8, 1)
-    t = part(7) + f32(a) + f32(b)
-    got = swap(narrow(t[:, 4:]), "yl")
+        here = slice(8 * i, 8 * i + 8)
+        return f32(own[:, here]) + f32(other[:, here])
+
+    across1 = swap(far, "yh")
+    za = ring(narrow(part(0)), "z", 8, 1)
+    zb = ring(narrow(part(1)), "z", 8, -1)
+    xa = ring(parts[2], "x", 4, 1)
+    xb = ring(parts[3], "x", 4, -1)
+
+    za, zb = tie(za, zb)
+    za, zb = tie(narrow(part(2) + f32(za)), narrow(part(3) + f32(zb)))
+    last = za
+    za = ring(za, "z", 8, 1)
+    zb = ring(zb, "z", 8, -1)
+
+    xa, xb, last = tie(xa, xb, last)
+    last = narrow(f32(parts[1]) + f32(xa))
+    xa = ring(last, "x", 4, 1)
+
+    za, zb, last = tie(za, zb, last)
+    za, zb = tie(narrow(part(4) + f32(za)), narrow(part(5) + f32(zb)))
+    last = za
+    za = ring(za, "z", 8, 1)
+    zb = ring(zb, "z", 8, -1)
+
+    across1, last = tie(across1, last)
+    w1 = [f32(near[k]) + f32(across1[k]) for k in range(4)]
+    xc, xd = tie(narrow(w1[2]), narrow(w1[3]))
+    last = xc
+    xc = ring(xc, "x", 4, 1)
+    xd = ring(xd, "x", 4, -1)
+
+    xa, last = tie(xa, last)
+    half = f32(parts[0]) + f32(xa) + f32(xb)
+    last = narrow(half[1])
+    across2 = swap(last, "yh")
+
+    za, zb, last = tie(za, zb, last)
+    last = narrow(part(6) + f32(za))
+    za = ring(last, "z", 8, 1)
+
+    xc, xd, last = tie(xc, xd, last)
+    last = narrow(w1[1] + f32(xc))
+    xc = ring(last, "x", 4, 1)
+
+    za, last = tie(za, last)
+    t = part(7) + f32(za) + f32(zb)
+    last = narrow(t[:, 4:])
+    got = swap(last, "yl")
+
+    across2, last = tie(across2, last)
+    grad_w2 = half[0] + f32(across2)
+    xc, grad_w2 = tie(xc, grad_w2)
+    grad_w1 = w1[0] + f32(xc) + f32(xd)
     t = narrow(t[:, :4] + f32(got))
-    return t[0], t[1]
-
-
-def ring_x(parts):
-    a = ring(narrow(parts[2]), "x", 4, 1)
-    b = ring(narrow(parts[3]), "x", 4, -1)
-    a = ring(narrow(f32(parts[1]) + f32(a)), "x", 4, 1)
-    return f32(parts[0]) + f32(a) + f32(b)
-
-
-def reduce_x_first(parts):
-    s = ring_x(parts)
-    far = swap(narrow(s[1]), "yh")
-    return s[0] + f32(far)
-
-
-def reduce_y_first(near, far):
-    got = swap(far, "yh")
-    return ring_x([f32(near[k]) + f32(got[k]) for k in range(4)])
-
-
-def shards(tokens, grads, w1, w1_rows, w1_cols, w1_count, w2, w2_rows, w2_cols, w2_count):
+    return t[0], t[1], grad_w1, grad_w2
+
+
+def prepare(w1, w2, w1_rows, w1_cols, w1_count, w2_rows, w2_cols, w2_count):
     stripe = (lax.axis_index("z") * 2 + lax.axis_index("yl")) * 2 + lax.axis_index("c")
     here = jnp.stack([lax.axis_index("c"), lax.axis_index("x"), lax.axis_index("yh")])
     meta = jnp.concatenate(
         [
             w1_rows,
-            w1_cols - stripe * SB,
-            w2_rows - stripe * SB,
+            jnp.clip(w1_cols - stripe * SB, 0, SB - 1),
+            jnp.clip(w2_rows - stripe * SB, 0, SB - 1),
             w2_cols,
             w1_count,
             w2_count,
             here.astype(jnp.int32),
         ]
     )
-    pieces = gather_rows(tokens, grads)
-    hid, gp, tok, grad, own, early, late = run_forward(meta, w1, w2, pieces)
+    slot = jnp.arange(CAP, dtype=jnp.int32)[:, None, None]
+    live1 = jnp.where(slot < w1_count[0], w1, jnp.zeros_like(w1))
+    live2 = jnp.where(slot < w2_count[0], w2, jnp.zeros_like(w2))
+    return live1, live2, meta
+
+
+def shards(tokens, grads, w1, w1_rows, w1_cols, w1_count, w2, w2_rows, w2_cols, w2_count):
+    early = (w1, w2, w1_rows, w1_cols, w1_count, w2_rows, w2_cols, w2_count)
+    pieces, (live1, live2, meta) = gather_rows(tokens, grads, early)
+    hid, gp, tok, grad = run_hidden(meta, live1, live2, pieces)
+    own, other = run_partial(meta, live1, live2, hid, gp)
+    gp, other = tie(gp, other)
+    other = swap(other, "c")
     near, far = run_weight1(meta, gp, tok)
+    hid, near = tie(hid, near)
     parts = run_weight2(meta, hid, grad)
-    grad_w1 = reduce_y_first(near, far)
-    grad_w2 = reduce_x_first(parts)
-    layer_out, grad_tokens = reduce_tensor(own, early, late)
+    other, *parts = tie(other, *parts)
+    layer_out, grad_tokens, grad_w1, grad_w2 = reduce_all(own, other, near, far, parts)
     return layer_out, grad_tokens, grad_w1, grad_w2
 
 

time: 129 us -> 110 us (0.85)
  starting transfers between devices: 63.4 us -> 51.5 us
  waiting for transfers between devices: 40.5 us -> 33.7 us
  local copies, waits for them, and re-layouts: 4.72 us -> 1.54 us
  other arithmetic: 5.69 us -> 8.27 us
    ppermute x15 -> x14, waiting for transfers between devices: 19.4 us -> 10.6 us  [swap(): return lax.ppermute(v, axis, [(0, 1), (1, 0)])]
    ppermute x15 -> x14, starting transfers between devices: 27.6 us -> 18.9 us  [swap(): return lax.ppermute(v, axis, [(0, 1), (1, 0)])]
    ppermute x6, waiting for transfers between devices: 2.04 us -> 8.7 us  [ring(): return lax.ppermute(v, (axis, 'c'), pairs)]
    ppermute x14, waiting for transfers between devices: 19 us -> 14.4 us  [ring(): return lax.ppermute(v, ('z', 'yl', 'c'), full)]
    ppermute x6, starting transfers between devices: 13.2 us -> 9.41 us  [ring(): return lax.ppermute(v, (axis, 'c'), pairs)]
    unnamed x4 -> x0, local copies, waits for them, and re-layouts: 3.18 us -> none
    select_n x0 -> x1, other arithmetic: none -> 2.58 us  [prepare(): live2 = jnp.where(slot < w2_count[0], w2, jnp.zeros_like(w2))]
    pallas_call x1 -> x2, Pallas kernels: 8.36 us -> 8.51 us  [the longest x1 4.66 us: run_partial(): pl.pallas_call(partial_kernel, out_shape=[sds(2, 64, WIDTH)] * 2, in_spec...]
  transfers between devices with their start and end apart: 35 -> 34, of which waited for: 13 -> 15; matrix products, arithmetic and copies ran while one was open for 4% -> 7% of each run, Pallas kernels for 3% -> 3%
where the time goes in v3:
time: 110 us; the launch traced here: 109 us
  starting transfers between devices  51.5 us (47%)
  waiting for transfers between devices  33.7 us (31%)
  Pallas kernels  11.9 us (11%)
  other arithmetic  8.27 us (8%)
  between operations  2.14 us (2%)
  local copies, waits for them, and re-layouts  1.54 us (1%)
    ppermute x14, starting transfers between devices, ring(): return lax.ppermute(v, ('z', 'yl', 'c'), full)  23.2 us
    ppermute x14, starting transfers between devices, swap(): return lax.ppermute(v, axis, [(0, 1), (1, 0)])  18.9 us
    ppermute x14, waiting for transfers between devices, ring(): return lax.ppermute(v, ('z', 'yl', 'c'), full)  14.4 us
    ppermute x14, waiting for transfers between devices, swap(): return lax.ppermute(v, axis, [(0, 1), (1, 0)])  10.6 us
    ppermute x6, starting transfers between devices, ring(): return lax.ppermute(v, (axis, 'c'), pairs)  9.41 us
    ppermute x6, waiting for transfers between devices, ring(): return lax.ppermute(v, (axis, 'c'), pairs)  8.7 us
    pallas_call x1, Pallas kernels, run_partial(): pl.pallas_call(partial_kernel, out_shape=[sds(2, 64, WIDTH)] * 2, in_spec...  4.66 us
    pallas_call x1, Pallas kernels, run_hidden(): pl.pallas_call(hidden_kernel, out_shape=[sds(SB, BLK, BLK)] * 2 + [sds(BL...  3.84 us
  transfers between devices with their start and end apart: 34, of which 15 were waited for; matrix products, arithmetic and copies ran while one was open for 7% of the time, Pallas kernels for 3%

profile of v3, /device:TPU:1, one launch (start us, length us, event | category | flops | bytes accessed | tf_op | source)
XLA Modules:
  0.0 109.1 jit_solution(10471861244097311464)
XLA Ops:
  0.6 2.2 %collective-permute-start = (bf16[4,8192]{1,0:T(4,128)(2,1)}, bf16[4,8192]{1,0:T(4,128)(2,1)S(1)}, u32[]{:S(2)}, u32[]{:S(2)}) collective-permute-start(bf16[4,8192]{1,0:T(4,128)(2,1)} %param.10), channel_id=1, source_target_pairs={{0,2},{2,0},{1,3},{3,1},{4,6},{6,4},{5,7},{7,5},{8,10},{10,8},{9,1... | collective-permute-start | bytes 196616 | tf_op jit(solution)/shard_map/ppermute | solution.py:208
  4.3 0.4 collective-permute-done
  4.7 0.9 maximum_bitcast_fusion
  5.6 0.5 collective-permute-done.1
  6.2 0.9 maximum_bitcast_fusion.1
  7.1 6.3 %collective-permute-start.2 = (bf16[2,8,8192]{2,1,0:T(8,128)(2,1)S(1)}, bf16[2,8,8192]{2,1,0:T(8,128)(2,1)S(1)}, u32[]{:S(2)}, u32[]{:S(2)}) collective-permute-start(bf16[2,8,8192]{2,1,0:T(8,128)(2,1)S(1)} %pad_maximum_fusion.refs_7_), channel_id=1, source_target_pairs={{0,4},{1,29},{2,6},{3,31},{4,8},{5,1},{6,10},{7,3},{8,12},{9,5},{1... | collective-permute-start | bytes 786440 | tf_op jit(solution)/shard_map/ppermute | solution.py:224
  13.4 0.7 subtract_clamp_fusion
  14.1 0.7 concatenate.11.meta
  14.9 2.6 %broadcast_select_fusion = (bf16[64,128,128]{2,1,0:T(8,128)(2,1)S(1)}, bf16[64,128,128]{2,1,0:T(8,128)(2,1)S(1)}) fusion(bf16[64,128,128]{2,1,0:T(8,128)(2,1)} %param.16, pred[64]{0:T(512)(128)(4,1)S(1)} %iota_compare_fusion, bf16[64,128,128]{2,1,0:T(8,128)(2,1)} %param.12, pred[64]{0:T(512)(128)(4,1)S(1)} %iota_compare_fusion.1), kind=kLoop, calls=%fused_computation | loop fusion | flops 2097152 | bytes 8388736 | tf_op jit(solution)/shard_map/jit(_where)/select_n | solution.py:332
  17.6 2.7 %collective-permute-start.3 = (bf16[2,8,8192]{2,1,0:T(8,128)(2,1)S(1)}, bf16[2,8,8192]{2,1,0:T(8,128)(2,1)S(1)}, u32[]{:S(2)}, u32[]{:S(2)}) collective-permute-start(bf16[2,8,8192]{2,1,0:T(8,128)(2,1)S(1)} %collective-permute-done.2.refs_5_), channel_id=1, source_target_pairs={{0,4},{1,29},{2,6},{3,31},{4,8},{5,1},{6,10},{7,3},{8,12},{9,5},{1... | collective-permute-start | bytes 786440 | tf_op jit(solution)/shard_map/ppermute | solution.py:224
  20.2 4.3 %collective-permute-done.6.refs_6_ = bf16[2,8,8192]{2,1,0:T(8,128)(2,1)S(1)} collective-permute-done((bf16[2,8,8192]{2,1,0:T(8,128)(2,1)S(1)}, bf16[2,8,8192]{2,1,0:T(8,128)(2,1)S(1)}, u32[]{:S(2)}, u32[]{:S(2)}) %collective-permute-start.6) | collective-permute-done | bytes 262176 | tf_op jit(solution)/shard_map/ppermute | solution.py:224
  24.6 1.0 collective-permute-done.3.refs_3_
  25.6 3.1 %collective-permute-start.4 = (bf16[2,8,8192]{2,1,0:T(8,128)(2,1)S(1)}, bf16[2,8,8192]{2,1,0:T(8,128)(2,1)S(1)}, u32[]{:S(2)}, u32[]{:S(2)}) collective-permute-start(bf16[2,8,8192]{2,1,0:T(8,128)(2,1)S(1)} %collective-permute-done.3.refs_3_), channel_id=1, source_target_pairs={{0,4},{1,29},{2,6},{3,31},{4,8},{5,1},{6,10},{7,3},{8,12},{9,5},{1... | collective-permute-start | bytes 786440 | tf_op jit(solution)/shard_map/ppermute | solution.py:224
  29.4 1.6 %collective-permute-done.7.refs_4_ = bf16[2,8,8192]{2,1,0:T(8,128)(2,1)S(1)} collective-permute-done((bf16[2,8,8192]{2,1,0:T(8,128)(2,1)S(1)}, bf16[2,8,8192]{2,1,0:T(8,128)(2,1)S(1)}, u32[]{:S(2)}, u32[]{:S(2)}) %collective-permute-start.7) | collective-permute-done | bytes 262176 | tf_op jit(solution)/shard_map/ppermute | solution.py:224
  31.0 3.5 %collective-permute-done.4.refs_1_ = bf16[2,8,8192]{2,1,0:T(8,128)(2,1)S(1)} collective-permute-done((bf16[2,8,8192]{2,1,0:T(8,128)(2,1)S(1)}, bf16[2,8,8192]{2,1,0:T(8,128)(2,1)S(1)}, u32[]{:S(2)}, u32[]{:S(2)}) %collective-permute-start.4) | collective-permute-done | bytes 262176 | tf_op jit(solution)/shard_map/ppermute | solution.py:224
  34.5 3.4 %collective-permute-start.5 = (bf16[2,8,8192]{2,1,0:T(8,128)(2,1)S(1)}, bf16[2,8,8192]{2,1,0:T(8,128)(2,1)S(1)}, u32[]{:S(2)}, u32[]{:S(2)}) collective-permute-start(bf16[2,8,8192]{2,1,0:T(8,128)(2,1)S(1)} %collective-permute-done.4.refs_1_), channel_id=1, source_target_pairs={{0,4},{1,29},{2,6},{3,31},{4,8},{5,1},{6,10},{7,3},{8,12},{9,5},{1... | collective-permute-start | bytes 786440 | tf_op jit(solution)/shard_map/ppermute | solution.py:224
  37.9 1.1 %collective-permute-start.12 = (bf16[2,8,8192]{2,1,0:T(8,128)(2,1)S(1)}, bf16[2,8,8192]{2,1,0:T(8,128)(2,1)S(1)}, u32[]{:S(2)}, u32[]{:S(2)}) collective-permute-start(bf16[2,8,8192]{2,1,0:T(8,128)(2,1)S(1)} %collective-permute-done.3.refs_3_), channel_id=1, source_target_pairs={{0,1},{1,0},{2,3},{3,2},{4,5},{5,4},{6,7},{7,6},{8,9},{9,8},{10,11... | collective-permute-start | bytes 786440 | tf_op jit(solution)/shard_map/ppermute | solution.py:208
  39.1 0.4 collective-permute-start.10
  39.5 4.9 %collective-permute-start.11 = (bf16[2,8,8192]{2,1,0:T(8,128)(2,1)S(1)}, bf16[2,8,8192]{2,1,0:T(8,128)(2,1)S(1)}, u32[]{:S(2)}, u32[]{:S(2)}) collective-permute-start(bf16[2,8,8192]{2,1,0:T(8,128)(2,1)S(1)} %collective-permute-done.8.refs_2_), channel_id=1, source_target_pairs={{0,1},{1,0},{2,3},{3,2},{4,5},{5,4},{6,7},{7,6},{8,9},{9,8},{10,11... | collective-permute-start | bytes 786440 | tf_op jit(solution)/shard_map/ppermute | solution.py:208
  44.4 2.1 %collective-permute-start.9 = (bf16[2,8,8192]{2,1,0:T(8,128)(2,1)S(1)}, bf16[2,8,8192]{2,1,0:T(8,128)(2,1)S(1)}, u32[]{:S(2)}, u32[]{:S(2)}) collective-permute-start(bf16[2,8,8192]{2,1,0:T(8,128)(2,1)S(1)} %collective-permute-done.5.refs_0_), channel_id=1, source_target_pairs={{0,1},{1,0},{2,3},{3,2},{4,5},{5,4},{6,7},{7,6},{8,9},{9,8},{10,11... | collective-permute-start | bytes 786440 | tf_op jit(solution)/shard_map/ppermute | solution.py:208
  46.5 1.1 %collective-permute-done.9.refs_8_ = bf16[2,8,8192]{2,1,0:T(8,128)(2,1)S(1)} collective-permute-done((bf16[2,8,8192]{2,1,0:T(8,128)(2,1)S(1)}, bf16[2,8,8192]{2,1,0:T(8,128)(2,1)S(1)}, u32[]{:S(2)}, u32[]{:S(2)}) %collective-permute-start.9) | collective-permute-done | bytes 262176 | tf_op jit(solution)/shard_map/ppermute | solution.py:208
  47.6 3.8 %hidden.1 = (bf16[4,128,128]{2,1,0:T(8,128)(2,1)S(1)}, bf16[4,128,128]{2,1,0:T(8,128)(2,1)S(1)}, bf16[128,8192]{1,0:T(8,128)(2,1)S(1)}, bf16[128,8192]{1,0:T(8,128)(2,1)S(1)}) custom-call(s32[261]{0:T(512)S(1)} %concatenate.11.meta, bf16[64,128,128]{2,1,0:T(8,128)(2,1)S(1)} %get-tuple-element.68.w1, bf16[64,128,128]{2,1,0:T(8,128)(2,1)S(1)} %get-tuple-element.69.w2, ...), custom_call_target="tpu_custom_call" | custom-call | flops 2147483648 | bytes 12582912 | tf_op jit(solution)/shard_map/hidden/pallas_call | solution.py:155
  51.5 4.7 %partial.1 = (bf16[2,64,8192]{2,1,0:T(8,128)(2,1)S(1)}, bf16[2,64,8192]{2,1,0:T(8,128)(2,1)S(1)}) custom-call(s32[261]{0:T(512)S(1)} %concatenate.11.meta, bf16[64,128,128]{2,1,0:T(8,128)(2,1)S(1)} %get-tuple-element.68.w1, bf16[64,128,128]{2,1,0:T(8,128)(2,1)S(1)} %get-tuple-element.69.w2, bf16[4,128,128]{2,1,0:T(8,128)(2,1)S(1)} %get-tuple-element.79.hid, ...), custom_call_target="tpu_custom_call" | custom-call | flops 2147483648 | bytes 12582912 | tf_op jit(solution)/shard_map/partial/pallas_call | solution.py:168
  56.2 0.4 collective-permute-start.17
  56.6 1.6 %weight1.1 = (bf16[4,64,16,128]{3,2,1,0:T(8,128)(2,1)S(1)}, bf16[4,64,16,128]{3,2,1,0:T(8,128)(2,1)S(1)}) custom-call(s32[261]{0:T(512)S(1)} %concatenate.11.meta, bf16[4,128,128]{2,1,0:T(8,128)(2,1)S(1)} %get-tuple-element.76.gp, bf16[128,8192]{1,0:T(8,128)(2,1)S(1)} %get-tuple-element.77.tok), custom_call_target="tpu_custom_call" | custom-call | flops 1073741824 | bytes 4194304 | tf_op jit(solution)/shard_map/weight1/pallas_call | solution.py:182
  58.2 1.7 %weight2.1 = (bf16[2,64,16,128]{3,2,1,0:T(8,128)(2,1)S(1)}, bf16[2,64,16,128]{3,2,1,0:T(8,128)(2,1)S(1)}, bf16[2,64,16,128]{3,2,1,0:T(8,128)(2,1)S(1)}, bf16[2,64,16,128]{3,2,1,0:T(8,128)(2,1)S(1)}) custom-call(s32[261]{0:T(512)S(1)} %concatenate.11.meta, bf16[4,128,128]{2,1,0:T(8,128)(2,1)S(1)} %get-tuple-element.79.hid, ...), custom_call_target="tpu_custom_call" | custom-call | flops 1073741824 | bytes 4194304 | tf_op jit(solution)/shard_map/weight2/pallas_call | solution.py:195
  60.0 0.4 collective-permute-done.17
  60.6 2.7 %collective-permute-start.18 = (bf16[2,8,8192]{2,1,0:T(8,128)(2,1)S(1)}, bf16[2,8,8192]{2,1,0:T(8,128)(2,1)S(1)}, u32[]{:S(2)}, u32[]{:S(2)}) collective-permute-start(bf16[2,8,8192]{2,1,0:T(8,128)(2,1)S(1)} %get-tuple-element.119), channel_id=1, source_target_pairs={{0,4},{1,29},{2,6},{3,31},{4,8},{5,1},{6,10},{7,3},{8,12},{9,5},{1... | collective-permute-start | bytes 786440 | tf_op jit(solution)/shard_map/ppermute | solution.py:224
  63.3 2.8 %collective-permute-start.27 = (bf16[4,64,16,128]{3,2,1,0:T(8,128)(2,1)S(1)}, bf16[4,64,16,128]{3,2,1,0:T(8,128)(2,1)S(1)}, u32[]{:S(2)}, u32[]{:S(2)}) collective-permute-start(bf16[4,64,16,128]{3,2,1,0:T(8,128)(2,1)S(1)} %get-tuple-element.100), channel_id=1, source_target_pairs={{0,128},{128,0},{1,129},{129,1},{2,130},{130,2},{3,131},{131,3},{4... | collective-permute-start | bytes 3145736 | tf_op jit(solution)/shard_map/ppermute | solution.py:208
  66.1 2.5 %collective-permute-start.22 = (bf16[2,64,16,128]{3,2,1,0:T(8,128)(2,1)S(1)}, bf16[2,64,16,128]{3,2,1,0:T(8,128)(2,1)S(1)}, u32[]{:S(2)}, u32[]{:S(2)}) collective-permute-start(bf16[2,64,16,128]{3,2,1,0:T(8,128)(2,1)S(1)} %get-tuple-element.91), channel_id=1, source_target_pairs={{0,32},{1,97},{32,64},{33,1},{64,96},{65,33},{96,0},{97,65},{2,34}... | collective-permute-start | bytes 1572872 | tf_op jit(solution)/shard_map/ppermute | solution.py:225
  68.6 0.7 collective-permute-done.18
  69.6 3.4 %collective-permute-start.20 = (bf16[2,8,8192]{2,1,0:T(8,128)(2,1)S(1)}, bf16[2,8,8192]{2,1,0:T(8,128)(2,1)S(1)}, u32[]{:S(2)}, u32[]{:S(2)}) collective-permute-start(bf16[2,8,8192]{2,1,0:T(8,128)(2,1)S(1)} %get-tuple-element.88), channel_id=1, source_target_pairs={{0,4},{1,29},{2,6},{3,31},{4,8},{5,1},{6,10},{7,3},{8,12},{9,5},{1... | collective-permute-start | bytes 786440 | tf_op jit(solution)/shard_map/ppermute | solution.py:224
  73.0 6.4 %collective-permute-done.22 = bf16[2,64,16,128]{3,2,1,0:T(8,128)(2,1)S(1)} collective-permute-done((bf16[2,64,16,128]{3,2,1,0:T(8,128)(2,1)S(1)}, bf16[2,64,16,128]{3,2,1,0:T(8,128)(2,1)S(1)}, u32[]{:S(2)}, u32[]{:S(2)}) %collective-permute-start.22) | collective-permute-done | bytes 524320 | tf_op jit(solution)/shard_map/ppermute | solution.py:225
  79.4 2.3 %collective-permute-done.23 = bf16[2,64,16,128]{3,2,1,0:T(8,128)(2,1)S(1)} collective-permute-done((bf16[2,64,16,128]{3,2,1,0:T(8,128)(2,1)S(1)}, bf16[2,64,16,128]{3,2,1,0:T(8,128)(2,1)S(1)}, u32[]{:S(2)}, u32[]{:S(2)}) %collective-permute-start.23) | collective-permute-done | bytes 524320 | tf_op jit(solution)/shard_map/ppermute | solution.py:225
  81.9 1.3 %collective-permute-start.26 = (bf16[2,64,16,128]{3,2,1,0:T(8,128)(2,1)S(1)}, bf16[2,64,16,128]{3,2,1,0:T(8,128)(2,1)S(1)}, u32[]{:S(2)}, u32[]{:S(2)}) collective-permute-start(bf16[2,64,16,128]{3,2,1,0:T(8,128)(2,1)S(1)} %add_convert_fusion), channel_id=1, source_target_pairs={{0,32},{1,97},{32,64},{33,1},{64,96},{65,33},{96,0},{97,65},{2,34}... | collective-permute-start | bytes 1572872 | tf_op jit(solution)/shard_map/ppermute | solution.py:225
  83.4 1.3 %collective-permute-start.24 = (bf16[2,8,8192]{2,1,0:T(8,128)(2,1)S(1)}, bf16[2,8,8192]{2,1,0:T(8,128)(2,1)S(1)}, u32[]{:S(2)}, u32[]{:S(2)}) collective-permute-start(bf16[2,8,8192]{2,1,0:T(8,128)(2,1)S(1)} %get-tuple-element.96), channel_id=1, source_target_pairs={{0,4},{1,29},{2,6},{3,31},{4,8},{5,1},{6,10},{7,3},{8,12},{9,5},{1... | collective-permute-start | bytes 786440 | tf_op jit(solution)/shard_map/ppermute | solution.py:224
  84.7 5.1 %collective-permute-done.27 = bf16[4,64,16,128]{3,2,1,0:T(8,128)(2,1)S(1)} collective-permute-done((bf16[4,64,16,128]{3,2,1,0:T(8,128)(2,1)S(1)}, bf16[4,64,16,128]{3,2,1,0:T(8,128)(2,1)S(1)}, u32[]{:S(2)}, u32[]{:S(2)}) %collective-permute-start.27) | collective-permute-done | bytes 1048608 | tf_op jit(solution)/shard_map/ppermute | solution.py:208
  89.9 1.3 %collective-permute-start.30 = (bf16[64,16,128]{2,1,0:T(8,128)(2,1)S(1)}, bf16[64,16,128]{2,1,0:T(8,128)(2,1)S(1)}, u32[]{:S(2)}, u32[]{:S(2)}) collective-permute-start(bf16[64,16,128]{2,1,0:T(8,128)(2,1)S(1)} %get-tuple-element.106), channel_id=1, source_target_pairs={{0,96},{1,33},{32,0},{33,65},{64,32},{65,97},{96,64},{97,1},{2,98}... | collective-permute-start | bytes 786440 | tf_op jit(solution)/shard_map/ppermute | solution.py:225
  91.2 1.5 %collective-permute-start.29 = (bf16[64,16,128]{2,1,0:T(8,128)(2,1)S(1)}, bf16[64,16,128]{2,1,0:T(8,128)(2,1)S(1)}, u32[]{:S(2)}, u32[]{:S(2)}) collective-permute-start(bf16[64,16,128]{2,1,0:T(8,128)(2,1)S(1)} %get-tuple-element.102), channel_id=1, source_target_pairs={{0,32},{1,97},{32,64},{33,1},{64,96},{65,33},{96,0},{97,65},{2,34}... | collective-permute-start | bytes 786440 | tf_op jit(solution)/shard_map/ppermute | solution.py:225
  93.0 3.3 %collective-permute-done.25 = bf16[2,8,8192]{2,1,0:T(8,128)(2,1)S(1)} collective-permute-done((bf16[2,8,8192]{2,1,0:T(8,128)(2,1)S(1)}, bf16[2,8,8192]{2,1,0:T(8,128)(2,1)S(1)}, u32[]{:S(2)}, u32[]{:S(2)}) %collective-permute-start.25) | collective-permute-done | bytes 262176 | tf_op jit(solution)/shard_map/ppermute | solution.py:224
  96.4 2.9 %collective-permute-start.33 = (bf16[64,16,128]{2,1,0:T(8,128)(2,1)S(1)}, bf16[64,16,128]{2,1,0:T(8,128)(2,1)S(1)}, u32[]{:S(2)}, u32[]{:S(2)}) collective-permute-start(bf16[64,16,128]{2,1,0:T(8,128)(2,1)S(1)} %fusion.5), channel_id=1, source_target_pairs={{0,128},{128,0},{1,129},{129,1},{2,130},{130,2},{3,131},{131,3},{4... | collective-permute-start | bytes 786440 | tf_op jit(solution)/shard_map/ppermute | solution.py:208
  99.5 2.8 %collective-permute-start.32 = (bf16[64,16,128]{2,1,0:T(8,128)(2,1)S(1)}, bf16[64,16,128]{2,1,0:T(8,128)(2,1)S(1)}, u32[]{:S(2)}, u32[]{:S(2)}) collective-permute-start(bf16[64,16,128]{2,1,0:T(8,128)(2,1)S(1)} %fusion.2), channel_id=1, source_target_pairs={{0,32},{1,97},{32,64},{33,1},{64,96},{65,33},{96,0},{97,65},{2,34}... | collective-permute-start | bytes 786440 | tf_op jit(solution)/shard_map/ppermute | solution.py:225
  102.5 1.1 collective-permute-start.31
  103.6 1.8 %collective-permute-done.33 = bf16[64,16,128]{2,1,0:T(8,128)(2,1)S(1)} collective-permute-done((bf16[64,16,128]{2,1,0:T(8,128)(2,1)S(1)}, bf16[64,16,128]{2,1,0:T(8,128)(2,1)S(1)}, u32[]{:S(2)}, u32[]{:S(2)}) %collective-permute-start.33) | collective-permute-done | bytes 262176 | tf_op jit(solution)/shard_map/ppermute | solution.py:208
  105.4 0.8 fusion
  106.2 0.9 fusion.1
  107.2 1.1 %collective-permute-done.31 = bf16[2,4,8192]{2,1,0:T(4,128)(2,1)S(1)} collective-permute-done((bf16[2,4,8192]{2,1,0:T(4,128)(2,1)S(1)}, bf16[2,4,8192]{2,1,0:T(4,128)(2,1)S(1)}, u32[]{:S(2)}, u32[]{:S(2)}) %collective-permute-start.31) | collective-permute-done | bytes 131104 | tf_op jit(solution)/shard_map/ppermute | solution.py:208
  108.4 0.7 slice_bitcast_fusion.1
  (47 shorter events, 2.9 us)
Async XLA Ops:
  0.6 4.1 %collective-permute-start = (bf16[4,8192]{1,0:T(4,128)(2,1)}, bf16[4,8192]{1,0:T(4,128)(2,1)S(1)}, u32[]{:S(2)}, u32[]{:S(2)}) collective-permute-start(bf16[4,8192]{1,0:T(4,128)(2,1)} %param.10), channel_id=1, source_target_pairs={{0,2},{2,0},{1,3},{3,1},{4,6},{6,4},{5,7},{7,5},{8,10},{10,8},{9,1... | collective-permute-start | bytes 196616 | tf_op jit(solution)/shard_map/ppermute | solution.py:208
  2.8 3.3 %collective-permute-start.1 = (bf16[4,8192]{1,0:T(4,128)(2,1)}, bf16[4,8192]{1,0:T(4,128)(2,1)S(1)}, u32[]{:S(2)}, u32[]{:S(2)}) collective-permute-start(bf16[4,8192]{1,0:T(4,128)(2,1)} %param.11), channel_id=1, source_target_pairs={{0,2},{2,0},{1,3},{3,1},{4,6},{6,4},{5,7},{7,5},{8,10},{10,8},{9,1... | collective-permute-start | bytes 196616 | tf_op jit(solution)/shard_map/ppermute | solution.py:208
  7.1 10.4 %collective-permute-start.2 = (bf16[2,8,8192]{2,1,0:T(8,128)(2,1)S(1)}, bf16[2,8,8192]{2,1,0:T(8,128)(2,1)S(1)}, u32[]{:S(2)}, u32[]{:S(2)}) collective-permute-start(bf16[2,8,8192]{2,1,0:T(8,128)(2,1)S(1)} %pad_maximum_fusion.refs_7_), channel_id=1, source_target_pairs={{0,4},{1,29},{2,6},{3,31},{4,8},{5,1},{6,10},{7,3},{8,12},{9,5},{1... | collective-permute-start | bytes 786440 | tf_op jit(solution)/shard_map/ppermute | solution.py:224
  17.5 7.1 %collective-permute-start.6 = (bf16[2,8,8192]{2,1,0:T(8,128)(2,1)S(1)}, bf16[2,8,8192]{2,1,0:T(8,128)(2,1)S(1)}, u32[]{:S(2)}, u32[]{:S(2)}) collective-permute-start(bf16[2,8,8192]{2,1,0:T(8,128)(2,1)S(1)} %pad_maximum_fusion.refs_7_), channel_id=1, source_target_pairs={{0,28},{1,5},{2,30},{3,7},{4,0},{5,9},{6,2},{7,11},{8,4},{9,13},{1... | collective-permute-start | bytes 786440 | tf_op jit(solution)/shard_map/ppermute | solution.py:224
  17.6 8.0 %collective-permute-start.3 = (bf16[2,8,8192]{2,1,0:T(8,128)(2,1)S(1)}, bf16[2,8,8192]{2,1,0:T(8,128)(2,1)S(1)}, u32[]{:S(2)}, u32[]{:S(2)}) collective-permute-start(bf16[2,8,8192]{2,1,0:T(8,128)(2,1)S(1)} %collective-permute-done.2.refs_5_), channel_id=1, source_target_pairs={{0,4},{1,29},{2,6},{3,31},{4,8},{5,1},{6,10},{7,3},{8,12},{9,5},{1... | collective-permute-start | bytes 786440 | tf_op jit(solution)/shard_map/ppermute | solution.py:224
  24.6 6.4 %collective-permute-start.7 = (bf16[2,8,8192]{2,1,0:T(8,128)(2,1)S(1)}, bf16[2,8,8192]{2,1,0:T(8,128)(2,1)S(1)}, u32[]{:S(2)}, u32[]{:S(2)}) collective-permute-start(bf16[2,8,8192]{2,1,0:T(8,128)(2,1)S(1)} %collective-permute-done.6.refs_6_), channel_id=1, source_target_pairs={{0,28},{1,5},{2,30},{3,7},{4,0},{5,9},{6,2},{7,11},{8,4},{9,13},{1... | collective-permute-start | bytes 786440 | tf_op jit(solution)/shard_map/ppermute | solution.py:224
  25.6 8.9 %collective-permute-start.4 = (bf16[2,8,8192]{2,1,0:T(8,128)(2,1)S(1)}, bf16[2,8,8192]{2,1,0:T(8,128)(2,1)S(1)}, u32[]{:S(2)}, u32[]{:S(2)}) collective-permute-start(bf16[2,8,8192]{2,1,0:T(8,128)(2,1)S(1)} %collective-permute-done.3.refs_3_), channel_id=1, source_target_pairs={{0,4},{1,29},{2,6},{3,31},{4,8},{5,1},{6,10},{7,3},{8,12},{9,5},{1... | collective-permute-start | bytes 786440 | tf_op jit(solution)/shard_map/ppermute | solution.py:224
  28.7 9.2 %collective-permute-start.16 = (bf16[2,8,8192]{2,1,0:T(8,128)(2,1)S(1)}, bf16[2,8,8192]{2,1,0:T(8,128)(2,1)S(1)}, u32[]{:S(2)}, u32[]{:S(2)}) collective-permute-start(bf16[2,8,8192]{2,1,0:T(8,128)(2,1)S(1)} %pad_maximum_fusion.refs_7_), channel_id=1, source_target_pairs={{0,1},{1,0},{2,3},{3,2},{4,5},{5,4},{6,7},{7,6},{8,9},{9,8},{10,11... | collective-permute-start | bytes 786440 | tf_op jit(solution)/shard_map/ppermute | solution.py:208
  28.9 10.1 %collective-permute-start.14 = (bf16[2,8,8192]{2,1,0:T(8,128)(2,1)S(1)}, bf16[2,8,8192]{2,1,0:T(8,128)(2,1)S(1)}, u32[]{:S(2)}, u32[]{:S(2)}) collective-permute-start(bf16[2,8,8192]{2,1,0:T(8,128)(2,1)S(1)} %collective-permute-done.2.refs_5_), channel_id=1, source_target_pairs={{0,1},{1,0},{2,3},{3,2},{4,5},{5,4},{6,7},{7,6},{8,9},{9,8},{10,11... | collective-permute-start | bytes 786440 | tf_op jit(solution)/shard_map/ppermute | solution.py:208
  29.2 9.9 %collective-permute-start.15 = (bf16[2,8,8192]{2,1,0:T(8,128)(2,1)S(1)}, bf16[2,8,8192]{2,1,0:T(8,128)(2,1)S(1)}, u32[]{:S(2)}, u32[]{:S(2)}) collective-permute-start(bf16[2,8,8192]{2,1,0:T(8,128)(2,1)S(1)} %collective-permute-done.6.refs_6_), channel_id=1, source_target_pairs={{0,1},{1,0},{2,3},{3,2},{4,5},{5,4},{6,7},{7,6},{8,9},{9,8},{10,11... | collective-permute-start | bytes 786440 | tf_op jit(solution)/shard_map/ppermute | solution.py:208
  31.0 8.5 %collective-permute-start.8 = (bf16[2,8,8192]{2,1,0:T(8,128)(2,1)S(1)}, bf16[2,8,8192]{2,1,0:T(8,128)(2,1)S(1)}, u32[]{:S(2)}, u32[]{:S(2)}) collective-permute-start(bf16[2,8,8192]{2,1,0:T(8,128)(2,1)S(1)} %collective-permute-done.7.refs_4_), channel_id=1, source_target_pairs={{0,28},{1,5},{2,30},{3,7},{4,0},{5,9},{6,2},{7,11},{8,4},{9,13},{1... | collective-permute-start | bytes 786440 | tf_op jit(solution)/shard_map/ppermute | solution.py:224
  34.5 9.9 %collective-permute-start.5 = (bf16[2,8,8192]{2,1,0:T(8,128)(2,1)S(1)}, bf16[2,8,8192]{2,1,0:T(8,128)(2,1)S(1)}, u32[]{:S(2)}, u32[]{:S(2)}) collective-permute-start(bf16[2,8,8192]{2,1,0:T(8,128)(2,1)S(1)} %collective-permute-done.4.refs_1_), channel_id=1, source_target_pairs={{0,4},{1,29},{2,6},{3,31},{4,8},{5,1},{6,10},{7,3},{8,12},{9,5},{1... | collective-permute-start | bytes 786440 | tf_op jit(solution)/shard_map/ppermute | solution.py:224
  37.9 8.6 %collective-permute-start.12 = (bf16[2,8,8192]{2,1,0:T(8,128)(2,1)S(1)}, bf16[2,8,8192]{2,1,0:T(8,128)(2,1)S(1)}, u32[]{:S(2)}, u32[]{:S(2)}) collective-permute-start(bf16[2,8,8192]{2,1,0:T(8,128)(2,1)S(1)} %collective-permute-done.3.refs_3_), channel_id=1, source_target_pairs={{0,1},{1,0},{2,3},{3,2},{4,5},{5,4},{6,7},{7,6},{8,9},{9,8},{10,11... | collective-permute-start | bytes 786440 | tf_op jit(solution)/shard_map/ppermute | solution.py:208
  39.0 7.5 %collective-permute-start.13 = (bf16[2,8,8192]{2,1,0:T(8,128)(2,1)S(1)}, bf16[2,8,8192]{2,1,0:T(8,128)(2,1)S(1)}, u32[]{:S(2)}, u32[]{:S(2)}) collective-permute-start(bf16[2,8,8192]{2,1,0:T(8,128)(2,1)S(1)} %collective-permute-done.7.refs_4_), channel_id=1, source_target_pairs={{0,1},{1,0},{2,3},{3,2},{4,5},{5,4},{6,7},{7,6},{8,9},{9,8},{10,11... | collective-permute-start | bytes 786440 | tf_op jit(solution)/shard_map/ppermute | solution.py:208
  39.1 7.4 %collective-permute-start.10 = (bf16[2,8,8192]{2,1,0:T(8,128)(2,1)S(1)}, bf16[2,8,8192]{2,1,0:T(8,128)(2,1)S(1)}, u32[]{:S(2)}, u32[]{:S(2)}) collective-permute-start(bf16[2,8,8192]{2,1,0:T(8,128)(2,1)S(1)} %collective-permute-done.4.refs_1_), channel_id=1, source_target_pairs={{0,1},{1,0},{2,3},{3,2},{4,5},{5,4},{6,7},{7,6},{8,9},{9,8},{10,11... | collective-permute-start | bytes 786440 | tf_op jit(solution)/shard_map/ppermute | solution.py:208
  39.5 7.0 %collective-permute-start.11 = (bf16[2,8,8192]{2,1,0:T(8,128)(2,1)S(1)}, bf16[2,8,8192]{2,1,0:T(8,128)(2,1)S(1)}, u32[]{:S(2)}, u32[]{:S(2)}) collective-permute-start(bf16[2,8,8192]{2,1,0:T(8,128)(2,1)S(1)} %collective-permute-done.8.refs_2_), channel_id=1, source_target_pairs={{0,1},{1,0},{2,3},{3,2},{4,5},{5,4},{6,7},{7,6},{8,9},{9,8},{10,11... | collective-permute-start | bytes 786440 | tf_op jit(solution)/shard_map/ppermute | solution.py:208
  44.4 3.2 %collective-permute-start.9 = (bf16[2,8,8192]{2,1,0:T(8,128)(2,1)S(1)}, bf16[2,8,8192]{2,1,0:T(8,128)(2,1)S(1)}, u32[]{:S(2)}, u32[]{:S(2)}) collective-permute-start(bf16[2,8,8192]{2,1,0:T(8,128)(2,1)S(1)} %collective-permute-done.5.refs_0_), channel_id=1, source_target_pairs={{0,1},{1,0},{2,3},{3,2},{4,5},{5,4},{6,7},{7,6},{8,9},{9,8},{10,11... | collective-permute-start | bytes 786440 | tf_op jit(solution)/shard_map/ppermute | solution.py:208
  56.2 4.2 %collective-permute-start.17 = (bf16[2,64,8192]{2,1,0:T(8,128)(2,1)S(1)}, bf16[2,64,8192]{2,1,0:T(8,128)(2,1)S(1)}, u32[]{:S(2)}, u32[]{:S(2)}) collective-permute-start(bf16[2,64,8192]{2,1,0:T(8,128)(2,1)S(1)} %get-tuple-element.75), channel_id=1, source_target_pairs={{0,1},{1,0},{2,3},{3,2},{4,5},{5,4},{6,7},{7,6},{8,9},{9,8},{10,11... | collective-permute-start | bytes 6291464 | tf_op jit(solution)/shard_map/ppermute | solution.py:208
  60.5 8.1 %collective-permute-start.19 = (bf16[2,8,8192]{2,1,0:T(8,128)(2,1)S(1)}, bf16[2,8,8192]{2,1,0:T(8,128)(2,1)S(1)}, u32[]{:S(2)}, u32[]{:S(2)}) collective-permute-start(bf16[2,8,8192]{2,1,0:T(8,128)(2,1)S(1)} %get-tuple-element.118), channel_id=1, source_target_pairs={{0,28},{1,5},{2,30},{3,7},{4,0},{5,9},{6,2},{7,11},{8,4},{9,13},{1... | collective-permute-start | bytes 786440 | tf_op jit(solution)/shard_map/ppermute | solution.py:224
  60.6 8.7 %collective-permute-start.18 = (bf16[2,8,8192]{2,1,0:T(8,128)(2,1)S(1)}, bf16[2,8,8192]{2,1,0:T(8,128)(2,1)S(1)}, u32[]{:S(2)}, u32[]{:S(2)}) collective-permute-start(bf16[2,8,8192]{2,1,0:T(8,128)(2,1)S(1)} %get-tuple-element.119), channel_id=1, source_target_pairs={{0,4},{1,29},{2,6},{3,31},{4,8},{5,1},{6,10},{7,3},{8,12},{9,5},{1... | collective-permute-start | bytes 786440 | tf_op jit(solution)/shard_map/ppermute | solution.py:224
  63.3 26.5 %collective-permute-start.27 = (bf16[4,64,16,128]{3,2,1,0:T(8,128)(2,1)S(1)}, bf16[4,64,16,128]{3,2,1,0:T(8,128)(2,1)S(1)}, u32[]{:S(2)}, u32[]{:S(2)}) collective-permute-start(bf16[4,64,16,128]{3,2,1,0:T(8,128)(2,1)S(1)} %get-tuple-element.100), channel_id=1, source_target_pairs={{0,128},{128,0},{1,129},{129,1},{2,130},{130,2},{3,131},{131,3},{4... | collective-permute-start | bytes 3145736 | tf_op jit(solution)/shard_map/ppermute | solution.py:208
  66.1 13.3 %collective-permute-start.22 = (bf16[2,64,16,128]{3,2,1,0:T(8,128)(2,1)S(1)}, bf16[2,64,16,128]{3,2,1,0:T(8,128)(2,1)S(1)}, u32[]{:S(2)}, u32[]{:S(2)}) collective-permute-start(bf16[2,64,16,128]{3,2,1,0:T(8,128)(2,1)S(1)} %get-tuple-element.91), channel_id=1, source_target_pairs={{0,32},{1,97},{32,64},{33,1},{64,96},{65,33},{96,0},{97,65},{2,34}... | collective-permute-start | bytes 1572872 | tf_op jit(solution)/shard_map/ppermute | solution.py:225
  68.6 13.1 %collective-permute-start.23 = (bf16[2,64,16,128]{3,2,1,0:T(8,128)(2,1)S(1)}, bf16[2,64,16,128]{3,2,1,0:T(8,128)(2,1)S(1)}, u32[]{:S(2)}, u32[]{:S(2)}) collective-permute-start(bf16[2,64,16,128]{3,2,1,0:T(8,128)(2,1)S(1)} %get-tuple-element.92), channel_id=1, source_target_pairs={{0,96},{1,33},{32,0},{33,65},{64,32},{65,97},{96,64},{97,1},{2,98}... | collective-permute-start | bytes 1572872 | tf_op jit(solution)/shard_map/ppermute | solution.py:225
  69.5 13.7 %collective-permute-start.21 = (bf16[2,8,8192]{2,1,0:T(8,128)(2,1)S(1)}, bf16[2,8,8192]{2,1,0:T(8,128)(2,1)S(1)}, u32[]{:S(2)}, u32[]{:S(2)}) collective-permute-start(bf16[2,8,8192]{2,1,0:T(8,128)(2,1)S(1)} %get-tuple-element.89), channel_id=1, source_target_pairs={{0,28},{1,5},{2,30},{3,7},{4,0},{5,9},{6,2},{7,11},{8,4},{9,13},{1... | collective-permute-start | bytes 786440 | tf_op jit(solution)/shard_map/ppermute | solution.py:224
  69.6 13.6 %collective-permute-start.20 = (bf16[2,8,8192]{2,1,0:T(8,128)(2,1)S(1)}, bf16[2,8,8192]{2,1,0:T(8,128)(2,1)S(1)}, u32[]{:S(2)}, u32[]{:S(2)}) collective-permute-start(bf16[2,8,8192]{2,1,0:T(8,128)(2,1)S(1)} %get-tuple-element.88), channel_id=1, source_target_pairs={{0,4},{1,29},{2,6},{3,31},{4,8},{5,1},{6,10},{7,3},{8,12},{9,5},{1... | collective-permute-start | bytes 786440 | tf_op jit(solution)/shard_map/ppermute | solution.py:224
  81.9 10.8 %collective-permute-start.26 = (bf16[2,64,16,128]{3,2,1,0:T(8,128)(2,1)S(1)}, bf16[2,64,16,128]{3,2,1,0:T(8,128)(2,1)S(1)}, u32[]{:S(2)}, u32[]{:S(2)}) collective-permute-start(bf16[2,64,16,128]{3,2,1,0:T(8,128)(2,1)S(1)} %add_convert_fusion), channel_id=1, source_target_pairs={{0,32},{1,97},{32,64},{33,1},{64,96},{65,33},{96,0},{97,65},{2,34}... | collective-permute-start | bytes 1572872 | tf_op jit(solution)/shard_map/ppermute | solution.py:225
  83.4 12.8 %collective-permute-start.24 = (bf16[2,8,8192]{2,1,0:T(8,128)(2,1)S(1)}, bf16[2,8,8192]{2,1,0:T(8,128)(2,1)S(1)}, u32[]{:S(2)}, u32[]{:S(2)}) collective-permute-start(bf16[2,8,8192]{2,1,0:T(8,128)(2,1)S(1)} %get-tuple-element.96), channel_id=1, source_target_pairs={{0,4},{1,29},{2,6},{3,31},{4,8},{5,1},{6,10},{7,3},{8,12},{9,5},{1... | collective-permute-start | bytes 786440 | tf_op jit(solution)/shard_map/ppermute | solution.py:224
  89.8 6.4 %collective-permute-start.25 = (bf16[2,8,8192]{2,1,0:T(8,128)(2,1)S(1)}, bf16[2,8,8192]{2,1,0:T(8,128)(2,1)S(1)}, u32[]{:S(2)}, u32[]{:S(2)}) collective-permute-start(bf16[2,8,8192]{2,1,0:T(8,128)(2,1)S(1)} %get-tuple-element.97), channel_id=1, source_target_pairs={{0,28},{1,5},{2,30},{3,7},{4,0},{5,9},{6,2},{7,11},{8,4},{9,13},{1... | collective-permute-start | bytes 786440 | tf_op jit(solution)/shard_map/ppermute | solution.py:224
  89.9 9.4 %collective-permute-start.30 = (bf16[64,16,128]{2,1,0:T(8,128)(2,1)S(1)}, bf16[64,16,128]{2,1,0:T(8,128)(2,1)S(1)}, u32[]{:S(2)}, u32[]{:S(2)}) collective-permute-start(bf16[64,16,128]{2,1,0:T(8,128)(2,1)S(1)} %get-tuple-element.106), channel_id=1, source_target_pairs={{0,96},{1,33},{32,0},{33,65},{64,32},{65,97},{96,64},{97,1},{2,98}... | collective-permute-start | bytes 786440 | tf_op jit(solution)/shard_map/ppermute | solution.py:225
  91.2 8.1 %collective-permute-start.29 = (bf16[64,16,128]{2,1,0:T(8,128)(2,1)S(1)}, bf16[64,16,128]{2,1,0:T(8,128)(2,1)S(1)}, u32[]{:S(2)}, u32[]{:S(2)}) collective-permute-start(bf16[64,16,128]{2,1,0:T(8,128)(2,1)S(1)} %get-tuple-element.102), channel_id=1, source_target_pairs={{0,32},{1,97},{32,64},{33,1},{64,96},{65,33},{96,0},{97,65},{2,34}... | collective-permute-start | bytes 786440 | tf_op jit(solution)/shard_map/ppermute | solution.py:225
  96.3 6.0 %collective-permute-start.28 = (bf16[2,8,8192]{2,1,0:T(8,128)(2,1)S(1)}, bf16[2,8,8192]{2,1,0:T(8,128)(2,1)S(1)}, u32[]{:S(2)}, u32[]{:S(2)}) collective-permute-start(bf16[2,8,8192]{2,1,0:T(8,128)(2,1)S(1)} %add_convert_fusion.1), channel_id=1, source_target_pairs={{0,4},{1,29},{2,6},{3,31},{4,8},{5,1},{6,10},{7,3},{8,12},{9,5},{1... | collective-permute-start | bytes 786440 | tf_op jit(solution)/shard_map/ppermute | solution.py:224
  96.4 9.0 %collective-permute-start.33 = (bf16[64,16,128]{2,1,0:T(8,128)(2,1)S(1)}, bf16[64,16,128]{2,1,0:T(8,128)(2,1)S(1)}, u32[]{:S(2)}, u32[]{:S(2)}) collective-permute-start(bf16[64,16,128]{2,1,0:T(8,128)(2,1)S(1)} %fusion.5), channel_id=1, source_target_pairs={{0,128},{128,0},{1,129},{129,1},{2,130},{130,2},{3,131},{131,3},{4... | collective-permute-start | bytes 786440 | tf_op jit(solution)/shard_map/ppermute | solution.py:208
  99.5 6.8 %collective-permute-start.32 = (bf16[64,16,128]{2,1,0:T(8,128)(2,1)S(1)}, bf16[64,16,128]{2,1,0:T(8,128)(2,1)S(1)}, u32[]{:S(2)}, u32[]{:S(2)}) collective-permute-start(bf16[64,16,128]{2,1,0:T(8,128)(2,1)S(1)} %fusion.2), channel_id=1, source_target_pairs={{0,32},{1,97},{32,64},{33,1},{64,96},{65,33},{96,0},{97,65},{2,34}... | collective-permute-start | bytes 786440 | tf_op jit(solution)/shard_map/ppermute | solution.py:225
  102.5 5.8 %collective-permute-start.31 = (bf16[2,4,8192]{2,1,0:T(4,128)(2,1)S(1)}, bf16[2,4,8192]{2,1,0:T(4,128)(2,1)S(1)}, u32[]{:S(2)}, u32[]{:S(2)}) collective-permute-start(bf16[2,4,8192]{2,1,0:T(4,128)(2,1)S(1)} %slice.164), channel_id=1, source_target_pairs={{0,2},{2,0},{1,3},{3,1},{4,6},{6,4},{5,7},{7,5},{8,10},{10,8},{9,1... | collective-permute-start | bytes 393224 | tf_op jit(solution)/shard_map/ppermute | solution.py:208

commit v4 on v3

v4 whole, which is shorter than its diff:
```python
import jax
import jax.numpy as jnp
from jax import lax
from jax.experimental import pallas as pl
from jax.experimental.pallas import tpu as pltpu
from jax.sharding import Mesh
from jax.sharding import PartitionSpec as P

AXES = ("yh", "x", "z", "yl", "c")
SIZES = (2, 4, 8, 2, 2)
BLK = 128
SB = 4
CAP = 64
DB = 64
WIDTH = DB * BLK
F32 = jnp.float32
BF16 = jnp.bfloat16
FEW = 0
R1, C1, R2, C2, LIVE1, LIVE2, CORE, PX, PYH = 0, 64, 128, 192, 256, 257, 258, 259, 260
MB = 1024 * 1024


def gelu_pair(v):
    a = 0.7978845608028654
    b = 0.044715
    v2 = v * v
    t = jnp.tanh(a * v * (1.0 + b * v2))
    half = 0.5 * (1.0 + t)
    slope = half + 0.5 * v * (1.0 - t * t) * (a * (1.0 + 3.0 * b * v2))
    return v * half, slope


def lanes(block):
    return pl.ds(pl.multiple_of(block * BLK, BLK), BLK)


def loop(body, start=0, group=64):
    def step(i, carry):
        for j in range(group):
            body(start + i * group + j)
        return carry

    lax.fori_loop(0, (CAP - start) // group, step, 0)


def dot(a, b, dims):
    return lax.dot_general(a, b, (dims, ((), ())), preferred_element_type=F32)


def hidden_kernel(meta, w1, w2, *refs):
    p, q, pm, qm = refs[:5], refs[5:9], refs[9:13], refs[13:16]
    hid, gp, tok, grad, pre, back = refs[16:]
    low = meta[CORE] == 0

    def put(unit, a, b):
        rows = slice(16 * unit, 16 * unit + 16)
        a, b = a[...], b[...]
        tok[rows] = jnp.where(low, a, b)
        grad[rows] = jnp.where(low, b, a)

    put(0, p[4], pm[3])
    for i, k in enumerate((3, 2, 1)):
        put(1 + i, p[k], q[k])
        put(4 + i, qm[k - 1], pm[k - 1])
    put(7, p[0], q[0])
    pre[...] = jnp.zeros_like(pre)
    back[...] = jnp.zeros_like(back)

    def up(s):
        pre[meta[C1 + s]] += dot(tok[:, lanes(meta[R1 + s])], w1[s], ((1,), (0,)))

    loop(up)

    def down(s):
        back[meta[R2 + s]] += dot(grad[:, lanes(meta[C2 + s])], w2[s], ((1,), (1,)))

    loop(down)
    for k in range(SB):
        h, slope = gelu_pair(pre[k])
        hid[k] = h.astype(BF16)
        gp[k] = (back[k] * slope).astype(BF16)


def partial_kernel(meta, w1, w2, hid, gp, after, far, send_far, near, send, acc):
    core = meta[CORE]

    def finish(stream):
        for b in range(DB):
            here = slice(b * BLK, (b + 1) * BLK)
            v = acc[b].astype(BF16)
            if stream == 0:
                far[:, here] = v[:16]
            else:
                send_far[:, here] = v[:16]
            send[1 - stream, :, here] = v[16:64]
            near[stream, :, here] = v[64:]

    def finish_array(which):
        pl.when(core == which)(lambda: finish(0))
        pl.when(core != which)(lambda: finish(1))

    acc[...] = jnp.zeros_like(acc)

    def out(s):
        acc[meta[C2 + s]] += dot(hid[meta[R2 + s]], w2[s], ((1,), (0,)))

    loop(out)
    finish_array(0)
    acc[...] = jnp.zeros_like(acc)

    def tback(s):
        acc[meta[R1 + s]] += dot(gp[meta[C1 + s]], w1[s], ((1,), (1,)))

    loop(tback)
    finish_array(1)


def rel_x(meta, j):
    d = j % 4 - meta[PX]
    return jnp.where(meta[CORE] == 0, d, -d) & 3


def weight_kernel(meta, hid, gp, tok, grad, near, far, *refs):
    outs, stage, sem = refs[:4], refs[4], refs[5]
    n1 = meta[LIVE1]
    n2 = meta[LIVE2]
    pyh = meta[PYH]

    def put(slot, v):
        for j in range(8):
            stage[rel_x(meta, j), (j // 4) ^ pyh, slot] = v[16 * j : 16 * j + 16]

    def second(s):
        v = dot(hid[meta[R2 + s]], grad[:, lanes(meta[C2 + s])], ((0,), (0,)))
        put(s, jnp.where(s < n2, v, 0.0).astype(BF16))

    def first(s):
        v = dot(tok[:, lanes(meta[R1 + s])], gp[meta[C1 + s]], ((0,), (0,)))
        return jnp.where(s < n1, v, 0.0).astype(BF16)

    loop(second)
    for s in range(FEW):
        put(CAP + s, first(s))
    copies = [pltpu.make_async_copy(stage.at[k], outs[k], sem.at[k]) for k in range(4)]
    for cp in copies:
        cp.start()

    def rest(s):
        v = first(s)
        for j in range(4):
            k = rel_x(meta, j)
            low, high = v[16 * j : 16 * j + 16], v[16 * j + 64 : 16 * j + 80]
            near[k, s - FEW] = jnp.where(pyh == 0, low, high)
            far[k, s - FEW] = jnp.where(pyh == 0, high, low)

    loop(rest, FEW)
    for cp in copies:
        cp.wait()


def chunk_kernel(core, x, xc, y, yc, p, q):
    low = core[0] == 0
    both = []
    for which in range(2):
        rows = []
        for a, b in ((x, xc), (y, yc)):
            a, b = a[which].astype(F32), b[which].astype(F32)
            rows += [jnp.where(low, a, b), jnp.where(low, b, a)]
        both.append(jnp.concatenate(rows, axis=0))
    p[...] = jnp.where(low, both[0], both[1]).astype(BF16)
    q[...] = jnp.where(low, both[1], both[0]).astype(BF16)


VMEM = pl.BlockSpec(memory_space=pltpu.VMEM)
SMEM = pl.BlockSpec(memory_space=pltpu.SMEM)
ANY = pl.BlockSpec(memory_space=pl.ANY)


def sds(*shape):
    return jax.ShapeDtypeStruct(shape, BF16)


def run_hidden(meta, w1, w2, pieces):
    return pl.pallas_call(
        hidden_kernel,
        out_shape=[sds(SB, BLK, BLK)] * 2 + [sds(BLK, WIDTH)] * 2,
        in_specs=[SMEM, VMEM, VMEM] + [VMEM] * 16,
        out_specs=[VMEM] * 4,
        scratch_shapes=[pltpu.VMEM((SB, BLK, BLK), F32)] * 2,
        compiler_params=pltpu.CompilerParams(vmem_limit_bytes=24 * MB),
        cost_estimate=pl.CostEstimate(flops=1 << 31, bytes_accessed=12 * MB, transcendentals=1 << 16),
        name="hidden",
    )(meta, w1, w2, *pieces)


def run_partial(meta, w1, w2, hid, gp, after):
    return pl.pallas_call(
        partial_kernel,
        out_shape=[sds(16, WIDTH)] * 2 + [sds(2, 64, WIDTH), sds(2, 48, WIDTH)],
        in_specs=[SMEM] + [VMEM] * 4 + [ANY],
        out_specs=[VMEM] * 4,
        scratch_shapes=[pltpu.VMEM((DB, BLK, BLK), F32)],
        compiler_params=pltpu.CompilerParams(vmem_limit_bytes=24 * MB),
        cost_estimate=pl.CostEstimate(flops=1 << 31, bytes_accessed=12 * MB, transcendentals=0),
        name="partial",
    )(meta, w1, w2, hid, gp, after)


def run_weight(meta, hid, gp, tok, grad):
    return pl.pallas_call(
        weight_kernel,
        out_shape=[sds(4, CAP - FEW, 16, BLK)] * 2 + [sds(2, CAP + FEW, 16, BLK)] * 4,
        in_specs=[SMEM] + [VMEM] * 4,
        out_specs=[VMEM] * 2 + [ANY] * 4,
        scratch_shapes=[
            pltpu.VMEM((4, 2, CAP + FEW, 16, BLK), BF16),
            pltpu.SemaphoreType.DMA((4,)),
        ],
        compiler_params=pltpu.CompilerParams(vmem_limit_bytes=16 * MB),
        cost_estimate=pl.CostEstimate(flops=1 << 31, bytes_accessed=8 * MB, transcendentals=0),
        name="weight",
    )(meta, hid, gp, tok, grad)


def run_chunk(core, *rows):
    return pl.pallas_call(
        chunk_kernel,
        out_shape=[sds(16, WIDTH)] * 2,
        in_specs=[SMEM] + [VMEM] * 4,
        out_specs=[VMEM] * 2,
        compiler_params=pltpu.CompilerParams(vmem_limit_bytes=8 * MB),
        name="chunk",
    )(core, *rows)


def add(terms, after=(), out=BF16):
    terms = [t if isinstance(t, tuple) else (t, ()) for t in terms]
    count = len(terms)

    def kernel(*refs):
        total = None
        for ref, (_, index) in zip(refs, terms):
            v = (ref[index] if index else ref[...]).astype(F32)
            total = v if total is None else total + v
        refs[-1][...] = total.astype(out)

    shape = jax.eval_shape(lambda a: a[terms[0][1]], terms[0][0]).shape
    return pl.pallas_call(
        kernel,
        out_shape=jax.ShapeDtypeStruct(shape, out),
        in_specs=[VMEM] * count + [ANY] * len(after),
        out_specs=VMEM,
        compiler_params=pltpu.CompilerParams(vmem_limit_bytes=12 * MB),
        cost_estimate=pl.CostEstimate(flops=1, bytes_accessed=MB, transcendentals=0),
        name="add",
    )(*(t[0] for t in terms), *after)


def home_kernel(core, home, p, q, after, away, keep):
    low = core[0] == 0
    p = home[0, 48:].astype(F32) + p[...].astype(F32)
    q = home[1, 48:].astype(F32) + q[...].astype(F32)
    for which, t in enumerate((jnp.where(low, p, q), jnp.where(low, q, p))):
        first = jnp.concatenate([t[0:4], t[8:12]], axis=0)
        second = jnp.concatenate([t[4:8], t[12:16]], axis=0)
        keep[which] = jnp.where(low, first, second)
        away[which] = jnp.where(low, second, first).astype(BF16)


def half_kernel(mine, got, away, keep):
    for which in range(2):
        t = mine[which] + got[which].astype(F32)
        keep[which] = t[:4]
        away[which] = t[4:].astype(BF16)


def run_home(home, p, q, after):
    core = lax.axis_index("c").astype(jnp.int32).reshape(1)
    return pl.pallas_call(
        home_kernel,
        out_shape=[sds(2, 8, WIDTH), jax.ShapeDtypeStruct((2, 8, WIDTH), F32)],
        in_specs=[SMEM] + [VMEM] * 3 + [ANY],
        out_specs=[VMEM] * 2,
        compiler_params=pltpu.CompilerParams(vmem_limit_bytes=12 * MB),
        name="home",
    )(core, home, p, q, after)


def run_half(mine, got):
    return pl.pallas_call(
        half_kernel,
        out_shape=[sds(2, 4, WIDTH), jax.ShapeDtypeStruct((2, 4, WIDTH), F32)],
        in_specs=[VMEM] * 2,
        out_specs=[VMEM] * 2,
        compiler_params=pltpu.CompilerParams(vmem_limit_bytes=12 * MB),
        name="half",
    )(mine, got)


def swap(v, axis):
    return lax.ppermute(v, axis, [(0, 1), (1, 0)])


def ring(v, axis, n, sign):
    pairs = []
    for i in range(n):
        for c in range(2):
            step = sign if c == 0 else -sign
            pairs.append((i * 2 + c, ((i + step) % n) * 2 + c))
    if axis == "z":
        full = []
        for i in range(n):
            for y in range(2):
                for c in range(2):
                    step = sign if c == 0 else -sign
                    full.append(((i * 2 + y) * 2 + c, (((i + step) % n) * 2 + y) * 2 + c))
        return lax.ppermute(v, ("z", "yl", "c"), full)
    return lax.ppermute(v, (axis, "c"), pairs)


def f32(v):
    return v.astype(F32)


def narrow(v):
    return v.astype(BF16)


def tie(*values):
    return lax.optimization_barrier(values)


def gather_rows(tokens, grads, early):
    x = jnp.stack([tokens, grads])
    y = swap(x, "yl")
    core = lax.axis_index("c").astype(jnp.int32).reshape(1)
    p0, q0 = run_chunk(core, x, swap(x, "c"), y, swap(y, "c"))
    w1, w2, count1, count2 = early[0], early[1], early[4], early[7]
    meta = prepare(*tie(p0, *early[2:])[1:])
    p = [p0, ring(p0, "z", 8, 1)]
    q = [q0, ring(q0, "z", 8, 1)]
    p[1], meta = tie(p[1], meta)
    p[1], w1, w2 = tie(p[1], w1, w2)
    slot = jnp.arange(CAP, dtype=jnp.int32)[:, None, None]
    live1 = jnp.where(slot < count1[0], w1, jnp.zeros_like(w1))
    live2 = jnp.where(slot < count2[0], w2, jnp.zeros_like(w2))
    p.append(ring(p[1], "z", 8, 1))
    q.append(ring(q[1], "z", 8, 1))
    p[2], live1, live2 = tie(p[2], live1, live2)
    p.append(ring(p[2], "z", 8, 1))
    q.append(ring(q[2], "z", 8, 1))
    p.append(ring(p[-1], "z", 8, 1))
    return p + q + [swap(v, "c") for v in p[1:]] + [swap(v, "c") for v in q[1:]], (live1, live2, meta)


def reduce_all(far, got_far, near, got, mine1, across1, parts):
    def part(stream, k):
        here = (stream, slice(16 * (3 - k), 16 * (4 - k)))
        return [(near, here), (got, here)]

    op = add([far, got_far])
    p = ring(op, "z", 8, 1)
    op = add(part(1, 3), [op])
    q = ring(op, "z", 8, 1)
    xa = ring(parts[2], "x", 4, 1)
    xb = ring(parts[3], "x", 4, -1)

    op = add([parts[1], xa], [op])
    xa = ring(op, "x", 4, 1)

    op = add(part(0, 3) + [p], [op])
    p = ring(op, "z", 8, 1)
    op = add(part(1, 2) + [q], [op])
    q = ring(op, "z", 8, 1)

    op = add(part(0, 2) + [p], [op])
    p = ring(op, "z", 8, 1)
    op = add(part(1, 1) + [q], [op])
    q = ring(op, "z", 8, 1)

    op = add([(parts[0], (1,)), (xa, (1,)), (xb, (1,))], [op])
    across2 = swap(op, "yh")

    op = add(part(0, 1) + [p], [op])
    p = ring(op, "z", 8, 1)

    op = add([(mine1, (2,)), (across1, (2,))], [op])
    xc = ring(op, "x", 4, 1)
    op = add([(mine1, (3,)), (across1, (3,))], [op])
    xd = ring(op, "x", 4, -1)

    grad_w2 = add([(parts[0], (0,)), (xa, (0,)), (xb, (0,)), across2], [op], F32)
    away, keep = run_home(near, p, q, grad_w2)
    got = swap(away, "c")
    op = add([(mine1, (1,)), (across1, (1,)), xc], [away, xd])
    xc = ring(op, "x", 4, 1)
    away, keep = run_half(keep, got)
    got = swap(away, "yl")
    grad_w1 = add([(mine1, (0,)), (across1, (0,)), xc, xd], [away], F32)
    t = narrow(keep + f32(got))
    return t[0], t[1], grad_w1, grad_w2


def prepare(w1_rows, w1_cols, w1_count, w2_rows, w2_cols, w2_count):
    stripe = (lax.axis_index("z") * 2 + lax.axis_index("yl")) * 2 + lax.axis_index("c")
    here = jnp.stack([lax.axis_index("c"), lax.axis_index("x"), lax.axis_index("yh")])
    meta = jnp.concatenate(
        [
            w1_rows,
            jnp.clip(w1_cols - stripe * SB, 0, SB - 1),
            jnp.clip(w2_rows - stripe * SB, 0, SB - 1),
            w2_cols,
            w1_count,
            w2_count,
            here.astype(jnp.int32),
        ]
    )
    return meta


def shards(tokens, grads, w1, w1_rows, w1_cols, w1_count, w2, w2_rows, w2_cols, w2_count):
    early = (w1, w2, w1_rows, w1_cols, w1_count, w2_rows, w2_cols, w2_count)
    pieces, (live1, live2, meta) = gather_rows(tokens, grads, early)
    hid, gp, tok, grad = run_hidden(meta, live1, live2, pieces)
    mine1, away1, *parts = run_weight(meta, hid, gp, tok, grad)
    far, send_far, near, send = run_partial(meta, live1, live2, hid, gp, mine1)
    got_far = swap(send_far, "c")
    got = swap(send, "c")
    layer_out, grad_tokens, grad_w1, grad_w2 = reduce_all(
        far, got_far, near, got, mine1, swap(away1, "yh"), parts
    )
    return layer_out, grad_tokens, grad_w1, grad_w2


def solution(mesh):
    fine = Mesh(mesh.devices.reshape(SIZES), AXES)
    rows = P(AXES, None)
    stripe = ("z", "yl", "c")
    flat = P(stripe)
    blocks = P(stripe, None, None)
    in_specs = (rows, rows, blocks, flat, flat, flat, blocks, flat, flat, flat)
    grads = P(stripe, ("yh", "x"), None)
    out_specs = (rows, rows, grads, grads)
    return jax.shard_map(
        shards, mesh=fine, in_specs=in_specs, out_specs=out_specs, check_vma=False
    )
```

time: 110 us -> 103 us (0.936)
  waiting for transfers between devices: 33.7 us -> 20.4 us
  starting transfers between devices: 51.5 us -> 58.8 us
  other arithmetic: 8.27 us -> 3.73 us
  Pallas kernels: 11.9 us -> 13.6 us
    ppermute x14 -> x16, starting transfers between devices: 18.9 us -> 26.4 us  [swap(): return lax.ppermute(v, axis, [(0, 1), (1, 0)])]
    ppermute x14, waiting for transfers between devices: 14.4 us -> 8.43 us  [ring(): return lax.ppermute(v, ('z', 'yl', 'c'), full)]
    ppermute x6, waiting for transfers between devices: 8.7 us -> 4.83 us  [ring(): return lax.ppermute(v, (axis, 'c'), pairs)]
    ppermute x14 -> x16, waiting for transfers between devices: 10.6 us -> 7.15 us  [swap(): return lax.ppermute(v, axis, [(0, 1), (1, 0)])]
    add x4 -> x0, other arithmetic: 2.1 us -> none  [the longest x1 0.93 us: reduce_all(): grad_w1 = w1[0] + f32(xc) + f32(xd)]
    pallas_call x3 -> x19, Pallas kernels: 8.02 us -> 10.1 us  [the longest x1 3.94 us: run_partial(): pl.pallas_call(partial_kernel, out_shape=[sds(16, WIDTH)] * 2 + [sds(2, 6...]
    ppermute x14, starting transfers between devices: 23.2 us -> 21.3 us  [ring(): return lax.ppermute(v, ('z', 'yl', 'c'), full)]
    ppermute x6, starting transfers between devices: 9.41 us -> 11.1 us  [ring(): return lax.ppermute(v, (axis, 'c'), pairs)]
  transfers between devices with their start and end apart: 34 -> 36, of which waited for: 15 -> 14; matrix products, arithmetic and copies ran while one was open for 7% -> 3% of each run, Pallas kernels for 3% -> 3%
where the time goes in v4:
time: 103 us; the launch traced here: 101 us
  starting transfers between devices  58.8 us (57%)
  waiting for transfers between devices  20.4 us (20%)
  Pallas kernels  13.6 us (13%)
  other arithmetic  3.73 us (4%)
  local copies, waits for them, and re-layouts  2.49 us (2%)
  between operations  2.15 us (2%)
    ppermute x16, starting transfers between devices, swap(): return lax.ppermute(v, axis, [(0, 1), (1, 0)])  26.4 us
    ppermute x14, starting transfers between devices, ring(): return lax.ppermute(v, ('z', 'yl', 'c'), full)  21.3 us
    ppermute x6, starting transfers between devices, ring(): return lax.ppermute(v, (axis, 'c'), pairs)  11.1 us
    ppermute x14, waiting for transfers between devices, ring(): return lax.ppermute(v, ('z', 'yl', 'c'), full)  8.43 us
    ppermute x16, waiting for transfers between devices, swap(): return lax.ppermute(v, axis, [(0, 1), (1, 0)])  7.15 us
    ppermute x6, waiting for transfers between devices, ring(): return lax.ppermute(v, (axis, 'c'), pairs)  4.83 us
    pallas_call x1, Pallas kernels, run_partial(): pl.pallas_call(partial_kernel, out_shape=[sds(16, WIDTH)] * 2 + [sds(2, 6...  3.94 us
    pallas_call x1, Pallas kernels, run_hidden(): pl.pallas_call(hidden_kernel, out_shape=[sds(SB, BLK, BLK)] * 2 + [sds(BL...  3.51 us
  transfers between devices with their start and end apart: 36, of which 14 were waited for; matrix products, arithmetic and copies ran while one was open for 3% of the time, Pallas kernels for 3%

profile of v4, /device:TPU:1, one launch (start us, length us, event | category | flops | bytes accessed | tf_op | source)
XLA Modules:
  0.0 101.2 jit_solution(1076604237336016446)
XLA Ops:
  0.6 1.0 pad_maximum_fusion.x
  1.6 2.2 %collective-permute-start.1 = (bf16[2,4,8192]{2,1,0:T(4,128)(2,1)S(1)}, bf16[2,4,8192]{2,1,0:T(4,128)(2,1)S(1)}, u32[]{:S(2)}, u32[]{:S(2)}) collective-permute-start(bf16[2,4,8192]{2,1,0:T(4,128)(2,1)S(1)} %pad_maximum_fusion.x), channel_id=1, source_target_pairs={{0,2},{2,0},{1,3},{3,1},{4,6},{6,4},{5,7},{7,5},{8,10},{10,8},{9,1... | collective-permute-start | bytes 393224 | tf_op jit(solution)/shard_map/ppermute | solution.py:301
  3.8 1.2 %collective-permute-start = (bf16[2,4,8192]{2,1,0:T(4,128)(2,1)S(1)}, bf16[2,4,8192]{2,1,0:T(4,128)(2,1)S(1)}, u32[]{:S(2)}, u32[]{:S(2)}) collective-permute-start(bf16[2,4,8192]{2,1,0:T(4,128)(2,1)S(1)} %pad_maximum_fusion.x), channel_id=1, source_target_pairs={{0,1},{1,0},{2,3},{3,2},{4,5},{5,4},{6,7},{7,6},{8,9},{9,8},{10,11... | collective-permute-start | bytes 393224 | tf_op jit(solution)/shard_map/ppermute | solution.py:301
  5.0 1.1 %collective-permute-done.1.y = bf16[2,4,8192]{2,1,0:T(4,128)(2,1)S(1)} collective-permute-done((bf16[2,4,8192]{2,1,0:T(4,128)(2,1)S(1)}, bf16[2,4,8192]{2,1,0:T(4,128)(2,1)S(1)}, u32[]{:S(2)}, u32[]{:S(2)}) %collective-permute-start.1) | collective-permute-done | bytes 131104 | tf_op jit(solution)/shard_map/ppermute | solution.py:301
  6.2 3.7 %collective-permute-start.2 = (bf16[2,4,8192]{2,1,0:T(4,128)(2,1)S(1)}, bf16[2,4,8192]{2,1,0:T(4,128)(2,1)S(1)}, u32[]{:S(2)}, u32[]{:S(2)}) collective-permute-start(bf16[2,4,8192]{2,1,0:T(4,128)(2,1)S(1)} %collective-permute-done.1.y), channel_id=1, source_target_pairs={{0,1},{1,0},{2,3},{3,2},{4,5},{5,4},{6,7},{7,6},{8,9},{9,8},{10,11... | collective-permute-start | bytes 393224 | tf_op jit(solution)/shard_map/ppermute | solution.py:301
  11.4 4.2 %collective-permute-start.3 = (bf16[16,8192]{1,0:T(8,128)(2,1)S(1)}, bf16[16,8192]{1,0:T(8,128)(2,1)S(1)}, u32[]{:S(2)}, u32[]{:S(2)}) collective-permute-start(bf16[16,8192]{1,0:T(8,128)(2,1)S(1)} %get-tuple-element.38.refs_0_), channel_id=1, source_target_pairs={{0,4},{1,29},{2,6},{3,31},{4,8},{5,1},{6,10},{7,3},{8,12},{9,5},{1... | collective-permute-start | bytes 786440 | tf_op jit(solution)/shard_map/ppermute | solution.py:317
  15.6 0.7 collective-permute-start.7
  16.4 0.7 subtract_clamp_fusion
  17.0 0.7 concatenate.3.meta
  17.8 1.2 %collective-permute-done.3.refs_1_ = bf16[16,8192]{1,0:T(8,128)(2,1)S(1)} collective-permute-done((bf16[16,8192]{1,0:T(8,128)(2,1)S(1)}, bf16[16,8192]{1,0:T(8,128)(2,1)S(1)}, u32[]{:S(2)}, u32[]{:S(2)}) %collective-permute-start.3) | collective-permute-done | bytes 262176 | tf_op jit(solution)/shard_map/ppermute | solution.py:317
  18.9 3.1 %collective-permute-start.4 = (bf16[16,8192]{1,0:T(8,128)(2,1)S(1)}, bf16[16,8192]{1,0:T(8,128)(2,1)S(1)}, u32[]{:S(2)}, u32[]{:S(2)}) collective-permute-start(bf16[16,8192]{1,0:T(8,128)(2,1)S(1)} %collective-permute-done.3.refs_1_), channel_id=1, source_target_pairs={{0,4},{1,29},{2,6},{3,31},{4,8},{5,1},{6,10},{7,3},{8,12},{9,5},{1... | collective-permute-start | bytes 786440 | tf_op jit(solution)/shard_map/ppermute | solution.py:317
  22.1 1.8 %broadcast_select_fusion.1.w1 = bf16[64,128,128]{2,1,0:T(8,128)(2,1)S(1)} fusion(bf16[64,128,128]{2,1,0:T(8,128)(2,1)} %param.12, pred[64]{0:T(512)(128)(4,1)S(1)} %iota_compare_fusion.1), kind=kLoop, calls=%fused_computation.1 | loop fusion | flops 1048576 | bytes 4194368 | tf_op jit(solution)/shard_map/jit(_where)/select_n | solution.py:345
  23.9 1.0 collective-permute-start.8
  25.4 3.1 %collective-permute-start.5 = (bf16[16,8192]{1,0:T(8,128)(2,1)S(1)}, bf16[16,8192]{1,0:T(8,128)(2,1)S(1)}, u32[]{:S(2)}, u32[]{:S(2)}) collective-permute-start(bf16[16,8192]{1,0:T(8,128)(2,1)S(1)} %collective-permute-done.4.refs_2_), channel_id=1, source_target_pairs={{0,4},{1,29},{2,6},{3,31},{4,8},{5,1},{6,10},{7,3},{8,12},{9,5},{1... | collective-permute-start | bytes 786440 | tf_op jit(solution)/shard_map/ppermute | solution.py:317
  29.5 1.8 %collective-permute-start.9 = (bf16[16,8192]{1,0:T(8,128)(2,1)S(1)}, bf16[16,8192]{1,0:T(8,128)(2,1)S(1)}, u32[]{:S(2)}, u32[]{:S(2)}) collective-permute-start(bf16[16,8192]{1,0:T(8,128)(2,1)S(1)} %collective-permute-done.8.refs_7_), channel_id=1, source_target_pairs={{0,4},{1,29},{2,6},{3,31},{4,8},{5,1},{6,10},{7,3},{8,12},{9,5},{1... | collective-permute-start | bytes 786440 | tf_op jit(solution)/shard_map/ppermute | solution.py:317
  31.3 1.0 collective-permute-done.5.refs_3_
  32.3 2.6 %collective-permute-start.6 = (bf16[16,8192]{1,0:T(8,128)(2,1)S(1)}, bf16[16,8192]{1,0:T(8,128)(2,1)S(1)}, u32[]{:S(2)}, u32[]{:S(2)}) collective-permute-start(bf16[16,8192]{1,0:T(8,128)(2,1)S(1)} %collective-permute-done.5.refs_3_), channel_id=1, source_target_pairs={{0,4},{1,29},{2,6},{3,31},{4,8},{5,1},{6,10},{7,3},{8,12},{9,5},{1... | collective-permute-start | bytes 786440 | tf_op jit(solution)/shard_map/ppermute | solution.py:317
  36.0 2.3 %collective-permute-start.16 = (bf16[16,8192]{1,0:T(8,128)(2,1)S(1)}, bf16[16,8192]{1,0:T(8,128)(2,1)S(1)}, u32[]{:S(2)}, u32[]{:S(2)}) collective-permute-start(bf16[16,8192]{1,0:T(8,128)(2,1)S(1)} %collective-permute-done.9.refs_8_), channel_id=1, source_target_pairs={{0,1},{1,0},{2,3},{3,2},{4,5},{5,4},{6,7},{7,6},{8,9},{9,8},{10,11... | collective-permute-start | bytes 786440 | tf_op jit(solution)/shard_map/ppermute | solution.py:301
  38.3 4.8 %collective-permute-start.13 = (bf16[16,8192]{1,0:T(8,128)(2,1)S(1)}, bf16[16,8192]{1,0:T(8,128)(2,1)S(1)}, u32[]{:S(2)}, u32[]{:S(2)}) collective-permute-start(bf16[16,8192]{1,0:T(8,128)(2,1)S(1)} %collective-permute-done.6.refs_4_), channel_id=1, source_target_pairs={{0,1},{1,0},{2,3},{3,2},{4,5},{5,4},{6,7},{7,6},{8,9},{9,8},{10,11... | collective-permute-start | bytes 786440 | tf_op jit(solution)/shard_map/ppermute | solution.py:301
  43.0 1.1 %collective-permute-done.13.refs_12_ = bf16[16,8192]{1,0:T(8,128)(2,1)S(1)} collective-permute-done((bf16[16,8192]{1,0:T(8,128)(2,1)S(1)}, bf16[16,8192]{1,0:T(8,128)(2,1)S(1)}, u32[]{:S(2)}, u32[]{:S(2)}) %collective-permute-start.13) | collective-permute-done | bytes 262176 | tf_op jit(solution)/shard_map/ppermute | solution.py:301
  44.2 3.5 %hidden.1 = (bf16[4,128,128]{2,1,0:T(8,128)(2,1)S(1)}, bf16[4,128,128]{2,1,0:T(8,128)(2,1)S(1)}, bf16[128,8192]{1,0:T(8,128)(2,1)S(1)}, bf16[128,8192]{1,0:T(8,128)(2,1)S(1)}) custom-call(s32[261]{0:T(512)S(1)} %concatenate.3.meta, bf16[64,128,128]{2,1,0:T(8,128)(2,1)S(1)} %broadcast_select_fusion.1.w1, bf16[64,128,128]{2,1,0:T(8,128)(2,1)S(1)} %broadcast_select_fusion.w2, ...), custom_call_target="tpu_custom_call" | custom-call | flops 2147483648 | bytes 12582912 | tf_op jit(solution)/shard_map/hidden/pallas_call | solution.py:184
  47.7 2.8 %weight.1 = (bf16[4,64,16,128]{3,2,1,0:T(8,128)(2,1)S(1)}, bf16[4,64,16,128]{3,2,1,0:T(8,128)(2,1)S(1)}, bf16[2,64,16,128]{3,2,1,0:T(8,128)(2,1)S(1)}, bf16[2,64...) custom-call(s32[261]{0:T(512)S(1)} %concatenate.3.meta, ...), custom_call_target="tpu_custom_call" | custom-call | flops 2147483648 | bytes 8388608 | tf_op jit(solution)/shard_map/weight/pallas_call | solution.py:210
  50.5 3.9 %partial.1 = (bf16[16,8192]{1,0:T(8,128)(2,1)S(1)}, bf16[16,8192]{1,0:T(8,128)(2,1)S(1)}, bf16[2,64,8192]{2,1,0:T(8,128)(2,1)S(1)}, bf16[2,48,8192]{2,1,0:T(8,128)(2,1)S(1)}) custom-call(s32[261]{0:T(512)S(1)} %concatenate.3.meta, bf16[64,128,128]{2,1,0:T(8,128)(2,1)S(1)} %broadcast_select_fusion.1.w1, bf16[64,128,128]{2,1,0:T(8,128)(2,1)S(1)} %broadcast_select_fusion.w2, ...), custom_call_target="tpu_custom_call" | custom-call | flops 2147483648 | bytes 12582912 | tf_op jit(solution)/shard_map/partial/pallas_call | solution.py:197
  54.9 2.5 %collective-permute-start.20 = (bf16[2,64,16,128]{3,2,1,0:T(8,128)(2,1)S(1)}, bf16[2,64,16,128]{3,2,1,0:T(8,128)(2,1)S(1)}, u32[]{:S(2)}, u32[]{:S(2)}) collective-permute-start(bf16[2,64,16,128]{3,2,1,0:T(8,128)(2,1)S(1)} %get-tuple-element.64), channel_id=1, source_target_pairs={{0,32},{1,97},{32,64},{33,1},{64,96},{65,33},{96,0},{97,65},{2,34}... | collective-permute-start | bytes 1572872 | tf_op jit(solution)/shard_map/ppermute | solution.py:318
  57.4 2.9 %collective-permute-start.30 = (bf16[4,64,16,128]{3,2,1,0:T(8,128)(2,1)S(1)}, bf16[4,64,16,128]{3,2,1,0:T(8,128)(2,1)S(1)}, u32[]{:S(2)}, u32[]{:S(2)}) collective-permute-start(bf16[4,64,16,128]{3,2,1,0:T(8,128)(2,1)S(1)} %get-tuple-element.67), channel_id=1, source_target_pairs={{0,128},{128,0},{1,129},{129,1},{2,130},{130,2},{3,131},{131,3},{4... | collective-permute-start | bytes 3145736 | tf_op jit(solution)/shard_map/ppermute | solution.py:301
  60.6 0.7 collective-permute-start.25
  61.3 2.2 %collective-permute-done.20.refs_1_ = bf16[2,64,16,128]{3,2,1,0:T(8,128)(2,1)S(1)} collective-permute-done((bf16[2,64,16,128]{3,2,1,0:T(8,128)(2,1)S(1)}, bf16[2,64,16,128]{3,2,1,0:T(8,128)(2,1)S(1)}, u32[]{:S(2)}, u32[]{:S(2)}) %collective-permute-start.20) | collective-permute-done | bytes 524320 | tf_op jit(solution)/shard_map/ppermute | solution.py:318
  63.6 3.7 %collective-permute-start.24 = (bf16[2,64,16,128]{3,2,1,0:T(8,128)(2,1)S(1)}, bf16[2,64,16,128]{3,2,1,0:T(8,128)(2,1)S(1)}, u32[]{:S(2)}, u32[]{:S(2)}) collective-permute-start(bf16[2,64,16,128]{3,2,1,0:T(8,128)(2,1)S(1)} %add.29.refs_3_), channel_id=1, source_target_pairs={{0,32},{1,97},{32,64},{33,1},{64,96},{65,33},{96,0},{97,65},{2,34}... | collective-permute-start | bytes 1572872 | tf_op jit(solution)/shard_map/ppermute | solution.py:318
  67.5 1.3 %collective-permute-done.22.refs_2_ = bf16[16,8192]{1,0:T(8,128)(2,1)S(1)} collective-permute-done((bf16[16,8192]{1,0:T(8,128)(2,1)S(1)}, bf16[16,8192]{1,0:T(8,128)(2,1)S(1)}, u32[]{:S(2)}, u32[]{:S(2)}) %collective-permute-start.22) | collective-permute-done | bytes 262176 | tf_op jit(solution)/shard_map/ppermute | solution.py:317
  68.8 1.3 %collective-permute-start.26 = (bf16[16,8192]{1,0:T(8,128)(2,1)S(1)}, bf16[16,8192]{1,0:T(8,128)(2,1)S(1)}, u32[]{:S(2)}, u32[]{:S(2)}) collective-permute-start(bf16[16,8192]{1,0:T(8,128)(2,1)S(1)} %add.31.refs_3_), channel_id=1, source_target_pairs={{0,4},{1,29},{2,6},{3,31},{4,8},{5,1},{6,10},{7,3},{8,12},{9,5},{1... | collective-permute-start | bytes 786440 | tf_op jit(solution)/shard_map/ppermute | solution.py:317
  70.1 2.9 %collective-permute-done.21.refs_2_ = bf16[16,8192]{1,0:T(8,128)(2,1)S(1)} collective-permute-done((bf16[16,8192]{1,0:T(8,128)(2,1)S(1)}, bf16[16,8192]{1,0:T(8,128)(2,1)S(1)}, u32[]{:S(2)}, u32[]{:S(2)}) %collective-permute-start.21) | collective-permute-done | bytes 262176 | tf_op jit(solution)/shard_map/ppermute | solution.py:317
  73.1 1.3 %collective-permute-start.23 = (bf16[16,8192]{1,0:T(8,128)(2,1)S(1)}, bf16[16,8192]{1,0:T(8,128)(2,1)S(1)}, u32[]{:S(2)}, u32[]{:S(2)}) collective-permute-start(bf16[16,8192]{1,0:T(8,128)(2,1)S(1)} %add.32.refs_3_), channel_id=1, source_target_pairs={{0,4},{1,29},{2,6},{3,31},{4,8},{5,1},{6,10},{7,3},{8,12},{9,5},{1... | collective-permute-start | bytes 786440 | tf_op jit(solution)/shard_map/ppermute | solution.py:317
  74.4 1.4 %collective-permute-done.26.refs_2_ = bf16[16,8192]{1,0:T(8,128)(2,1)S(1)} collective-permute-done((bf16[16,8192]{1,0:T(8,128)(2,1)S(1)}, bf16[16,8192]{1,0:T(8,128)(2,1)S(1)}, u32[]{:S(2)}, u32[]{:S(2)}) %collective-permute-start.26) | collective-permute-done | bytes 262176 | tf_op jit(solution)/shard_map/ppermute | solution.py:317
  75.9 1.3 %collective-permute-start.28 = (bf16[16,8192]{1,0:T(8,128)(2,1)S(1)}, bf16[16,8192]{1,0:T(8,128)(2,1)S(1)}, u32[]{:S(2)}, u32[]{:S(2)}) collective-permute-start(bf16[16,8192]{1,0:T(8,128)(2,1)S(1)} %add.33.refs_3_), channel_id=1, source_target_pairs={{0,4},{1,29},{2,6},{3,31},{4,8},{5,1},{6,10},{7,3},{8,12},{9,5},{1... | collective-permute-start | bytes 786440 | tf_op jit(solution)/shard_map/ppermute | solution.py:317
  77.3 3.3 %collective-permute-start.29 = (bf16[64,16,128]{2,1,0:T(8,128)(2,1)S(1)}, bf16[64,16,128]{2,1,0:T(8,128)(2,1)S(1)}, u32[]{:S(2)}, u32[]{:S(2)}) collective-permute-start(bf16[64,16,128]{2,1,0:T(8,128)(2,1)S(1)} %add.34.refs_3_), channel_id=1, source_target_pairs={{0,128},{128,0},{1,129},{129,1},{2,130},{130,2},{3,131},{131,3},{4... | collective-permute-start | bytes 786440 | tf_op jit(solution)/shard_map/ppermute | solution.py:301
  80.7 0.6 collective-permute-start.27
  81.3 1.8 %collective-permute-done.30.refs_1_ = bf16[4,64,16,128]{3,2,1,0:T(8,128)(2,1)S(1)} collective-permute-done((bf16[4,64,16,128]{3,2,1,0:T(8,128)(2,1)S(1)}, bf16[4,64,16,128]{3,2,1,0:T(8,128)(2,1)S(1)}, u32[]{:S(2)}, u32[]{:S(2)}) %collective-permute-start.30) | collective-permute-done | bytes 1048608 | tf_op jit(solution)/shard_map/ppermute | solution.py:301
  83.2 1.0 %collective-permute-start.34 = (bf16[64,16,128]{2,1,0:T(8,128)(2,1)S(1)}, bf16[64,16,128]{2,1,0:T(8,128)(2,1)S(1)}, u32[]{:S(2)}, u32[]{:S(2)}) collective-permute-start(bf16[64,16,128]{2,1,0:T(8,128)(2,1)S(1)} %add.37.refs_4_), channel_id=1, source_target_pairs={{0,96},{1,33},{32,0},{33,65},{64,32},{65,97},{96,64},{97,1},{2,98}... | collective-permute-start | bytes 786440 | tf_op jit(solution)/shard_map/ppermute | solution.py:318
  84.2 1.7 %collective-permute-start.33 = (bf16[64,16,128]{2,1,0:T(8,128)(2,1)S(1)}, bf16[64,16,128]{2,1,0:T(8,128)(2,1)S(1)}, u32[]{:S(2)}, u32[]{:S(2)}) collective-permute-start(bf16[64,16,128]{2,1,0:T(8,128)(2,1)S(1)} %add.36.refs_2_), channel_id=1, source_target_pairs={{0,32},{1,97},{32,64},{33,1},{64,96},{65,33},{96,0},{97,65},{2,34}... | collective-permute-start | bytes 786440 | tf_op jit(solution)/shard_map/ppermute | solution.py:318
  86.0 2.7 %collective-permute-done.29.refs_3_ = bf16[64,16,128]{2,1,0:T(8,128)(2,1)S(1)} collective-permute-done((bf16[64,16,128]{2,1,0:T(8,128)(2,1)S(1)}, bf16[64,16,128]{2,1,0:T(8,128)(2,1)S(1)}, u32[]{:S(2)}, u32[]{:S(2)}) %collective-permute-start.29) | collective-permute-done | bytes 262176 | tf_op jit(solution)/shard_map/ppermute | solution.py:301
  88.7 0.9 add.38.after
  89.6 1.0 %copy-done = f32[64,16,128]{2,1,0:T(8,128)S(1)} copy-done((f32[64,16,128]{2,1,0:T(8,128)S(1)}, f32[64,16,128]{2,1,0:T(8,128)}, u32[]{:S(2)}) %copy-start) | copy-done | bytes 524312
  90.9 2.5 %collective-permute-start.31 = (bf16[2,8,8192]{2,1,0:T(8,128)(2,1)S(1)}, bf16[2,8,8192]{2,1,0:T(8,128)(2,1)S(1)}, u32[]{:S(2)}, u32[]{:S(2)}) collective-permute-start(bf16[2,8,8192]{2,1,0:T(8,128)(2,1)S(1)} %get-tuple-element.69.refs_3_), channel_id=1, source_target_pairs={{0,1},{1,0},{2,3},{3,2},{4,5},{5,4},{6,7},{7,6},{8,9},{9,8},{10,11... | collective-permute-start | bytes 786440 | tf_op jit(solution)/shard_map/ppermute | solution.py:301
  93.6 1.5 %collective-permute-start.35 = (bf16[64,16,128]{2,1,0:T(8,128)(2,1)S(1)}, bf16[64,16,128]{2,1,0:T(8,128)(2,1)S(1)}, u32[]{:S(2)}, u32[]{:S(2)}) collective-permute-start(bf16[64,16,128]{2,1,0:T(8,128)(2,1)S(1)} %add.39), channel_id=1, source_target_pairs={{0,32},{1,97},{32,64},{33,1},{64,96},{65,33},{96,0},{97,65},{2,34}... | collective-permute-start | bytes 786440 | tf_op jit(solution)/shard_map/ppermute | solution.py:318
  95.1 1.4 %collective-permute-start.32 = (bf16[2,4,8192]{2,1,0:T(4,128)(2,1)S(1)}, bf16[2,4,8192]{2,1,0:T(4,128)(2,1)S(1)}, u32[]{:S(2)}, u32[]{:S(2)}) collective-permute-start(bf16[2,4,8192]{2,1,0:T(4,128)(2,1)S(1)} %get-tuple-element.71.refs_4_), channel_id=1, source_target_pairs={{0,2},{2,0},{1,3},{3,1},{4,6},{6,4},{5,7},{7,5},{8,10},{10,8},{9,1... | collective-permute-start | bytes 393224 | tf_op jit(solution)/shard_map/ppermute | solution.py:301
  96.6 2.6 %collective-permute-done.35.refs_2_ = bf16[64,16,128]{2,1,0:T(8,128)(2,1)S(1)} collective-permute-done((bf16[64,16,128]{2,1,0:T(8,128)(2,1)S(1)}, bf16[64,16,128]{2,1,0:T(8,128)(2,1)S(1)}, u32[]{:S(2)}, u32[]{:S(2)}) %collective-permute-start.35) | collective-permute-done | bytes 262176 | tf_op jit(solution)/shard_map/ppermute | solution.py:318
  99.2 0.9 add.40
  100.5 0.7 slice_bitcast_fusion
  (57 shorter events, 5.3 us)
Async XLA Ops:
  1.6 4.6 %collective-permute-start.1 = (bf16[2,4,8192]{2,1,0:T(4,128)(2,1)S(1)}, bf16[2,4,8192]{2,1,0:T(4,128)(2,1)S(1)}, u32[]{:S(2)}, u32[]{:S(2)}) collective-permute-start(bf16[2,4,8192]{2,1,0:T(4,128)(2,1)S(1)} %pad_maximum_fusion.x), channel_id=1, source_target_pairs={{0,2},{2,0},{1,3},{3,1},{4,6},{6,4},{5,7},{7,5},{8,10},{10,8},{9,1... | collective-permute-start | bytes 393224 | tf_op jit(solution)/shard_map/ppermute | solution.py:301
  3.8 7.4 %collective-permute-start = (bf16[2,4,8192]{2,1,0:T(4,128)(2,1)S(1)}, bf16[2,4,8192]{2,1,0:T(4,128)(2,1)S(1)}, u32[]{:S(2)}, u32[]{:S(2)}) collective-permute-start(bf16[2,4,8192]{2,1,0:T(4,128)(2,1)S(1)} %pad_maximum_fusion.x), channel_id=1, source_target_pairs={{0,1},{1,0},{2,3},{3,2},{4,5},{5,4},{6,7},{7,6},{8,9},{9,8},{10,11... | collective-permute-start | bytes 393224 | tf_op jit(solution)/shard_map/ppermute | solution.py:301
  6.2 5.0 %collective-permute-start.2 = (bf16[2,4,8192]{2,1,0:T(4,128)(2,1)S(1)}, bf16[2,4,8192]{2,1,0:T(4,128)(2,1)S(1)}, u32[]{:S(2)}, u32[]{:S(2)}) collective-permute-start(bf16[2,4,8192]{2,1,0:T(4,128)(2,1)S(1)} %collective-permute-done.1.y), channel_id=1, source_target_pairs={{0,1},{1,0},{2,3},{3,2},{4,5},{5,4},{6,7},{7,6},{8,9},{9,8},{10,11... | collective-permute-start | bytes 393224 | tf_op jit(solution)/shard_map/ppermute | solution.py:301
  11.4 7.5 %collective-permute-start.3 = (bf16[16,8192]{1,0:T(8,128)(2,1)S(1)}, bf16[16,8192]{1,0:T(8,128)(2,1)S(1)}, u32[]{:S(2)}, u32[]{:S(2)}) collective-permute-start(bf16[16,8192]{1,0:T(8,128)(2,1)S(1)} %get-tuple-element.38.refs_0_), channel_id=1, source_target_pairs={{0,4},{1,29},{2,6},{3,31},{4,8},{5,1},{6,10},{7,3},{8,12},{9,5},{1... | collective-permute-start | bytes 786440 | tf_op jit(solution)/shard_map/ppermute | solution.py:317
  15.6 8.2 %collective-permute-start.7 = (bf16[16,8192]{1,0:T(8,128)(2,1)S(1)}, bf16[16,8192]{1,0:T(8,128)(2,1)S(1)}, u32[]{:S(2)}, u32[]{:S(2)}) collective-permute-start(bf16[16,8192]{1,0:T(8,128)(2,1)S(1)} %get-tuple-element.53.refs_5_), channel_id=1, source_target_pairs={{0,4},{1,29},{2,6},{3,31},{4,8},{5,1},{6,10},{7,3},{8,12},{9,5},{1... | collective-permute-start | bytes 786440 | tf_op jit(solution)/shard_map/ppermute | solution.py:317
  17.8 7.1 %copy-start.1 = (bf16[64,128,128]{2,1,0:T(8,128)(2,1)S(1)}, bf16[64,128,128]{2,1,0:T(8,128)(2,1)}, u32[]{:S(2)}) copy-start(bf16[64,128,128]{2,1,0:T(8,128)(2,1)} %param.16) | copy-start | bytes 6291460
  18.9 6.4 %collective-permute-start.4 = (bf16[16,8192]{1,0:T(8,128)(2,1)S(1)}, bf16[16,8192]{1,0:T(8,128)(2,1)S(1)}, u32[]{:S(2)}, u32[]{:S(2)}) collective-permute-start(bf16[16,8192]{1,0:T(8,128)(2,1)S(1)} %collective-permute-done.3.refs_1_), channel_id=1, source_target_pairs={{0,4},{1,29},{2,6},{3,31},{4,8},{5,1},{6,10},{7,3},{8,12},{9,5},{1... | collective-permute-start | bytes 786440 | tf_op jit(solution)/shard_map/ppermute | solution.py:317
  23.9 5.6 %collective-permute-start.8 = (bf16[16,8192]{1,0:T(8,128)(2,1)S(1)}, bf16[16,8192]{1,0:T(8,128)(2,1)S(1)}, u32[]{:S(2)}, u32[]{:S(2)}) collective-permute-start(bf16[16,8192]{1,0:T(8,128)(2,1)S(1)} %collective-permute-done.7.refs_6_), channel_id=1, source_target_pairs={{0,4},{1,29},{2,6},{3,31},{4,8},{5,1},{6,10},{7,3},{8,12},{9,5},{1... | collective-permute-start | bytes 786440 | tf_op jit(solution)/shard_map/ppermute | solution.py:317
  25.4 6.9 %collective-permute-start.5 = (bf16[16,8192]{1,0:T(8,128)(2,1)S(1)}, bf16[16,8192]{1,0:T(8,128)(2,1)S(1)}, u32[]{:S(2)}, u32[]{:S(2)}) collective-permute-start(bf16[16,8192]{1,0:T(8,128)(2,1)S(1)} %collective-permute-done.4.refs_2_), channel_id=1, source_target_pairs={{0,4},{1,29},{2,6},{3,31},{4,8},{5,1},{6,10},{7,3},{8,12},{9,5},{1... | collective-permute-start | bytes 786440 | tf_op jit(solution)/shard_map/ppermute | solution.py:317
  28.5 6.9 %collective-permute-start.14 = (bf16[16,8192]{1,0:T(8,128)(2,1)S(1)}, bf16[16,8192]{1,0:T(8,128)(2,1)S(1)}, u32[]{:S(2)}, u32[]{:S(2)}) collective-permute-start(bf16[16,8192]{1,0:T(8,128)(2,1)S(1)} %collective-permute-done.7.refs_6_), channel_id=1, source_target_pairs={{0,1},{1,0},{2,3},{3,2},{4,5},{5,4},{6,7},{7,6},{8,9},{9,8},{10,11... | collective-permute-start | bytes 786440 | tf_op jit(solution)/shard_map/ppermute | solution.py:301
  28.5 7.0 %collective-permute-start.10 = (bf16[16,8192]{1,0:T(8,128)(2,1)S(1)}, bf16[16,8192]{1,0:T(8,128)(2,1)S(1)}, u32[]{:S(2)}, u32[]{:S(2)}) collective-permute-start(bf16[16,8192]{1,0:T(8,128)(2,1)S(1)} %collective-permute-done.3.refs_1_), channel_id=1, source_target_pairs={{0,1},{1,0},{2,3},{3,2},{4,5},{5,4},{6,7},{7,6},{8,9},{9,8},{10,11... | collective-permute-start | bytes 786440 | tf_op jit(solution)/shard_map/ppermute | solution.py:301
  29.5 6.5 %collective-permute-start.9 = (bf16[16,8192]{1,0:T(8,128)(2,1)S(1)}, bf16[16,8192]{1,0:T(8,128)(2,1)S(1)}, u32[]{:S(2)}, u32[]{:S(2)}) collective-permute-start(bf16[16,8192]{1,0:T(8,128)(2,1)S(1)} %collective-permute-done.8.refs_7_), channel_id=1, source_target_pairs={{0,4},{1,29},{2,6},{3,31},{4,8},{5,1},{6,10},{7,3},{8,12},{9,5},{1... | collective-permute-start | bytes 786440 | tf_op jit(solution)/shard_map/ppermute | solution.py:317
  32.3 6.0 %collective-permute-start.6 = (bf16[16,8192]{1,0:T(8,128)(2,1)S(1)}, bf16[16,8192]{1,0:T(8,128)(2,1)S(1)}, u32[]{:S(2)}, u32[]{:S(2)}) collective-permute-start(bf16[16,8192]{1,0:T(8,128)(2,1)S(1)} %collective-permute-done.5.refs_3_), channel_id=1, source_target_pairs={{0,4},{1,29},{2,6},{3,31},{4,8},{5,1},{6,10},{7,3},{8,12},{9,5},{1... | collective-permute-start | bytes 786440 | tf_op jit(solution)/shard_map/ppermute | solution.py:317
  34.9 8.1 %collective-permute-start.11 = (bf16[16,8192]{1,0:T(8,128)(2,1)S(1)}, bf16[16,8192]{1,0:T(8,128)(2,1)S(1)}, u32[]{:S(2)}, u32[]{:S(2)}) collective-permute-start(bf16[16,8192]{1,0:T(8,128)(2,1)S(1)} %collective-permute-done.4.refs_2_), channel_id=1, source_target_pairs={{0,1},{1,0},{2,3},{3,2},{4,5},{5,4},{6,7},{7,6},{8,9},{9,8},{10,11... | collective-permute-start | bytes 786440 | tf_op jit(solution)/shard_map/ppermute | solution.py:301
  35.4 7.6 %collective-permute-start.15 = (bf16[16,8192]{1,0:T(8,128)(2,1)S(1)}, bf16[16,8192]{1,0:T(8,128)(2,1)S(1)}, u32[]{:S(2)}, u32[]{:S(2)}) collective-permute-start(bf16[16,8192]{1,0:T(8,128)(2,1)S(1)} %collective-permute-done.8.refs_7_), channel_id=1, source_target_pairs={{0,1},{1,0},{2,3},{3,2},{4,5},{5,4},{6,7},{7,6},{8,9},{9,8},{10,11... | collective-permute-start | bytes 786440 | tf_op jit(solution)/shard_map/ppermute | solution.py:301
  35.5 7.5 %collective-permute-start.12 = (bf16[16,8192]{1,0:T(8,128)(2,1)S(1)}, bf16[16,8192]{1,0:T(8,128)(2,1)S(1)}, u32[]{:S(2)}, u32[]{:S(2)}) collective-permute-start(bf16[16,8192]{1,0:T(8,128)(2,1)S(1)} %collective-permute-done.5.refs_3_), channel_id=1, source_target_pairs={{0,1},{1,0},{2,3},{3,2},{4,5},{5,4},{6,7},{7,6},{8,9},{9,8},{10,11... | collective-permute-start | bytes 786440 | tf_op jit(solution)/shard_map/ppermute | solution.py:301
  36.0 7.1 %collective-permute-start.16 = (bf16[16,8192]{1,0:T(8,128)(2,1)S(1)}, bf16[16,8192]{1,0:T(8,128)(2,1)S(1)}, u32[]{:S(2)}, u32[]{:S(2)}) collective-permute-start(bf16[16,8192]{1,0:T(8,128)(2,1)S(1)} %collective-permute-done.9.refs_8_), channel_id=1, source_target_pairs={{0,1},{1,0},{2,3},{3,2},{4,5},{5,4},{6,7},{7,6},{8,9},{9,8},{10,11... | collective-permute-start | bytes 786440 | tf_op jit(solution)/shard_map/ppermute | solution.py:301
  38.3 5.9 %collective-permute-start.13 = (bf16[16,8192]{1,0:T(8,128)(2,1)S(1)}, bf16[16,8192]{1,0:T(8,128)(2,1)S(1)}, u32[]{:S(2)}, u32[]{:S(2)}) collective-permute-start(bf16[16,8192]{1,0:T(8,128)(2,1)S(1)} %collective-permute-done.6.refs_4_), channel_id=1, source_target_pairs={{0,1},{1,0},{2,3},{3,2},{4,5},{5,4},{6,7},{7,6},{8,9},{9,8},{10,11... | collective-permute-start | bytes 786440 | tf_op jit(solution)/shard_map/ppermute | solution.py:301
  54.4 6.0 %collective-permute-start.17 = (bf16[2,48,8192]{2,1,0:T(8,128)(2,1)S(1)}, bf16[2,48,8192]{2,1,0:T(8,128)(2,1)S(1)}, u32[]{:S(2)}, u32[]{:S(2)}) collective-permute-start(bf16[2,48,8192]{2,1,0:T(8,128)(2,1)S(1)} %get-tuple-element.60), channel_id=1, source_target_pairs={{0,1},{1,0},{2,3},{3,2},{4,5},{5,4},{6,7},{7,6},{8,9},{9,8},{10,11... | collective-permute-start | bytes 4718600 | tf_op jit(solution)/shard_map/ppermute | solution.py:301
  54.9 8.6 %collective-permute-start.20 = (bf16[2,64,16,128]{3,2,1,0:T(8,128)(2,1)S(1)}, bf16[2,64,16,128]{3,2,1,0:T(8,128)(2,1)S(1)}, u32[]{:S(2)}, u32[]{:S(2)}) collective-permute-start(bf16[2,64,16,128]{3,2,1,0:T(8,128)(2,1)S(1)} %get-tuple-element.64), channel_id=1, source_target_pairs={{0,32},{1,97},{32,64},{33,1},{64,96},{65,33},{96,0},{97,65},{2,34}... | collective-permute-start | bytes 1572872 | tf_op jit(solution)/shard_map/ppermute | solution.py:318
  57.3 2.9 %collective-permute-start.18 = (bf16[16,8192]{1,0:T(8,128)(2,1)S(1)}, bf16[16,8192]{1,0:T(8,128)(2,1)S(1)}, u32[]{:S(2)}, u32[]{:S(2)}) collective-permute-start(bf16[16,8192]{1,0:T(8,128)(2,1)S(1)} %get-tuple-element.62), channel_id=1, source_target_pairs={{0,1},{1,0},{2,3},{3,2},{4,5},{5,4},{6,7},{7,6},{8,9},{9,8},{10,11... | collective-permute-start | bytes 786440 | tf_op jit(solution)/shard_map/ppermute | solution.py:301
  57.4 25.7 %collective-permute-start.30 = (bf16[4,64,16,128]{3,2,1,0:T(8,128)(2,1)S(1)}, bf16[4,64,16,128]{3,2,1,0:T(8,128)(2,1)S(1)}, u32[]{:S(2)}, u32[]{:S(2)}) collective-permute-start(bf16[4,64,16,128]{3,2,1,0:T(8,128)(2,1)S(1)} %get-tuple-element.67), channel_id=1, source_target_pairs={{0,128},{128,0},{1,129},{129,1},{2,130},{130,2},{3,131},{131,3},{4... | collective-permute-start | bytes 3145736 | tf_op jit(solution)/shard_map/ppermute | solution.py:301
  60.3 7.0 %collective-permute-start.19 = (bf16[16,8192]{1,0:T(8,128)(2,1)S(1)}, bf16[16,8192]{1,0:T(8,128)(2,1)S(1)}, u32[]{:S(2)}, u32[]{:S(2)}) collective-permute-start(bf16[16,8192]{1,0:T(8,128)(2,1)S(1)} %add.27.refs_2_), channel_id=1, source_target_pairs={{0,4},{1,29},{2,6},{3,31},{4,8},{5,1},{6,10},{7,3},{8,12},{9,5},{1... | collective-permute-start | bytes 786440 | tf_op jit(solution)/shard_map/ppermute | solution.py:317
  60.5 8.2 %collective-permute-start.22 = (bf16[16,8192]{1,0:T(8,128)(2,1)S(1)}, bf16[16,8192]{1,0:T(8,128)(2,1)S(1)}, u32[]{:S(2)}, u32[]{:S(2)}) collective-permute-start(bf16[16,8192]{1,0:T(8,128)(2,1)S(1)} %add.28.refs_2_), channel_id=1, source_target_pairs={{0,4},{1,29},{2,6},{3,31},{4,8},{5,1},{6,10},{7,3},{8,12},{9,5},{1... | collective-permute-start | bytes 786440 | tf_op jit(solution)/shard_map/ppermute | solution.py:317
  60.6 16.6 %collective-permute-start.25 = (bf16[2,64,16,128]{3,2,1,0:T(8,128)(2,1)S(1)}, bf16[2,64,16,128]{3,2,1,0:T(8,128)(2,1)S(1)}, u32[]{:S(2)}, u32[]{:S(2)}) collective-permute-start(bf16[2,64,16,128]{3,2,1,0:T(8,128)(2,1)S(1)} %get-tuple-element.66), channel_id=1, source_target_pairs={{0,96},{1,33},{32,0},{33,65},{64,32},{65,97},{96,64},{97,1},{2,98}... | collective-permute-start | bytes 1572872 | tf_op jit(solution)/shard_map/ppermute | solution.py:318
  63.6 13.6 %collective-permute-start.24 = (bf16[2,64,16,128]{3,2,1,0:T(8,128)(2,1)S(1)}, bf16[2,64,16,128]{3,2,1,0:T(8,128)(2,1)S(1)}, u32[]{:S(2)}, u32[]{:S(2)}) collective-permute-start(bf16[2,64,16,128]{3,2,1,0:T(8,128)(2,1)S(1)} %add.29.refs_3_), channel_id=1, source_target_pairs={{0,32},{1,97},{32,64},{33,1},{64,96},{65,33},{96,0},{97,65},{2,34}... | collective-permute-start | bytes 1572872 | tf_op jit(solution)/shard_map/ppermute | solution.py:318
  67.4 5.6 %collective-permute-start.21 = (bf16[16,8192]{1,0:T(8,128)(2,1)S(1)}, bf16[16,8192]{1,0:T(8,128)(2,1)S(1)}, u32[]{:S(2)}, u32[]{:S(2)}) collective-permute-start(bf16[16,8192]{1,0:T(8,128)(2,1)S(1)} %add.30.refs_3_), channel_id=1, source_target_pairs={{0,4},{1,29},{2,6},{3,31},{4,8},{5,1},{6,10},{7,3},{8,12},{9,5},{1... | collective-permute-start | bytes 786440 | tf_op jit(solution)/shard_map/ppermute | solution.py:317
  68.8 7.0 %collective-permute-start.26 = (bf16[16,8192]{1,0:T(8,128)(2,1)S(1)}, bf16[16,8192]{1,0:T(8,128)(2,1)S(1)}, u32[]{:S(2)}, u32[]{:S(2)}) collective-permute-start(bf16[16,8192]{1,0:T(8,128)(2,1)S(1)} %add.31.refs_3_), channel_id=1, source_target_pairs={{0,4},{1,29},{2,6},{3,31},{4,8},{5,1},{6,10},{7,3},{8,12},{9,5},{1... | collective-permute-start | bytes 786440 | tf_op jit(solution)/shard_map/ppermute | solution.py:317
  73.1 7.5 %collective-permute-start.23 = (bf16[16,8192]{1,0:T(8,128)(2,1)S(1)}, bf16[16,8192]{1,0:T(8,128)(2,1)S(1)}, u32[]{:S(2)}, u32[]{:S(2)}) collective-permute-start(bf16[16,8192]{1,0:T(8,128)(2,1)S(1)} %add.32.refs_3_), channel_id=1, source_target_pairs={{0,4},{1,29},{2,6},{3,31},{4,8},{5,1},{6,10},{7,3},{8,12},{9,5},{1... | collective-permute-start | bytes 786440 | tf_op jit(solution)/shard_map/ppermute | solution.py:317
  75.9 13.7 %collective-permute-start.28 = (bf16[16,8192]{1,0:T(8,128)(2,1)S(1)}, bf16[16,8192]{1,0:T(8,128)(2,1)S(1)}, u32[]{:S(2)}, u32[]{:S(2)}) collective-permute-start(bf16[16,8192]{1,0:T(8,128)(2,1)S(1)} %add.33.refs_3_), channel_id=1, source_target_pairs={{0,4},{1,29},{2,6},{3,31},{4,8},{5,1},{6,10},{7,3},{8,12},{9,5},{1... | collective-permute-start | bytes 786440 | tf_op jit(solution)/shard_map/ppermute | solution.py:317
  77.3 11.4 %collective-permute-start.29 = (bf16[64,16,128]{2,1,0:T(8,128)(2,1)S(1)}, bf16[64,16,128]{2,1,0:T(8,128)(2,1)S(1)}, u32[]{:S(2)}, u32[]{:S(2)}) collective-permute-start(bf16[64,16,128]{2,1,0:T(8,128)(2,1)S(1)} %add.34.refs_3_), channel_id=1, source_target_pairs={{0,128},{128,0},{1,129},{129,1},{2,130},{130,2},{3,131},{131,3},{4... | collective-permute-start | bytes 786440 | tf_op jit(solution)/shard_map/ppermute | solution.py:301
  80.7 8.9 %collective-permute-start.27 = (bf16[16,8192]{1,0:T(8,128)(2,1)S(1)}, bf16[16,8192]{1,0:T(8,128)(2,1)S(1)}, u32[]{:S(2)}, u32[]{:S(2)}) collective-permute-start(bf16[16,8192]{1,0:T(8,128)(2,1)S(1)} %add.35.refs_2_), channel_id=1, source_target_pairs={{0,4},{1,29},{2,6},{3,31},{4,8},{5,1},{6,10},{7,3},{8,12},{9,5},{1... | collective-permute-start | bytes 786440 | tf_op jit(solution)/shard_map/ppermute | solution.py:317
  83.2 10.3 %collective-permute-start.34 = (bf16[64,16,128]{2,1,0:T(8,128)(2,1)S(1)}, bf16[64,16,128]{2,1,0:T(8,128)(2,1)S(1)}, u32[]{:S(2)}, u32[]{:S(2)}) collective-permute-start(bf16[64,16,128]{2,1,0:T(8,128)(2,1)S(1)} %add.37.refs_4_), channel_id=1, source_target_pairs={{0,96},{1,33},{32,0},{33,65},{64,32},{65,97},{96,64},{97,1},{2,98}... | collective-permute-start | bytes 786440 | tf_op jit(solution)/shard_map/ppermute | solution.py:318
  84.2 9.3 %collective-permute-start.33 = (bf16[64,16,128]{2,1,0:T(8,128)(2,1)S(1)}, bf16[64,16,128]{2,1,0:T(8,128)(2,1)S(1)}, u32[]{:S(2)}, u32[]{:S(2)}) collective-permute-start(bf16[64,16,128]{2,1,0:T(8,128)(2,1)S(1)} %add.36.refs_2_), channel_id=1, source_target_pairs={{0,32},{1,97},{32,64},{33,1},{64,96},{65,33},{96,0},{97,65},{2,34}... | collective-permute-start | bytes 786440 | tf_op jit(solution)/shard_map/ppermute | solution.py:318
  89.6 1.0 %copy-start = (f32[64,16,128]{2,1,0:T(8,128)S(1)}, f32[64,16,128]{2,1,0:T(8,128)}, u32[]{:S(2)}) copy-start(f32[64,16,128]{2,1,0:T(8,128)} %add.38.after) | copy-start | bytes 1572868
  90.9 4.1 %collective-permute-start.31 = (bf16[2,8,8192]{2,1,0:T(8,128)(2,1)S(1)}, bf16[2,8,8192]{2,1,0:T(8,128)(2,1)S(1)}, u32[]{:S(2)}, u32[]{:S(2)}) collective-permute-start(bf16[2,8,8192]{2,1,0:T(8,128)(2,1)S(1)} %get-tuple-element.69.refs_3_), channel_id=1, source_target_pairs={{0,1},{1,0},{2,3},{3,2},{4,5},{5,4},{6,7},{7,6},{8,9},{9,8},{10,11... | collective-permute-start | bytes 786440 | tf_op jit(solution)/shard_map/ppermute | solution.py:301
  93.6 5.6 %collective-permute-start.35 = (bf16[64,16,128]{2,1,0:T(8,128)(2,1)S(1)}, bf16[64,16,128]{2,1,0:T(8,128)(2,1)S(1)}, u32[]{:S(2)}, u32[]{:S(2)}) collective-permute-start(bf16[64,16,128]{2,1,0:T(8,128)(2,1)S(1)} %add.39), channel_id=1, source_target_pairs={{0,32},{1,97},{32,64},{33,1},{64,96},{65,33},{96,0},{97,65},{2,34}... | collective-permute-start | bytes 786440 | tf_op jit(solution)/shard_map/ppermute | solution.py:318
  95.1 5.3 %collective-permute-start.32 = (bf16[2,4,8192]{2,1,0:T(4,128)(2,1)S(1)}, bf16[2,4,8192]{2,1,0:T(4,128)(2,1)S(1)}, u32[]{:S(2)}, u32[]{:S(2)}) collective-permute-start(bf16[2,4,8192]{2,1,0:T(4,128)(2,1)S(1)} %get-tuple-element.71.refs_4_), channel_id=1, source_target_pairs={{0,2},{2,0},{1,3},{3,1},{4,6},{6,4},{5,7},{7,5},{8,10},{10,8},{9,1... | collective-permute-start | bytes 393224 | tf_op jit(solution)/shard_map/ppermute | solution.py:301

commit v5 on v4

--- a/solution.py
+++ b/solution.py
@@ -233,7 +233,7 @@
     )(core, *rows)
 
 
-def add(terms, after=(), out=BF16):
+def add(terms, after=(), out=BF16, token=False):
     terms = [t if isinstance(t, tuple) else (t, ()) for t in terms]
     count = len(terms)
 
@@ -242,18 +242,24 @@
         for ref, (_, index) in zip(refs, terms):
             v = (ref[index] if index else ref[...]).astype(F32)
             total = v if total is None else total + v
-        refs[-1][...] = total.astype(out)
+        refs[count + len(after)][...] = total.astype(out)
+        if token:
+            refs[-1][...] = jnp.zeros((8, BLK), F32)
 
     shape = jax.eval_shape(lambda a: a[terms[0][1]], terms[0][0]).shape
-    return pl.pallas_call(
+    outs = [jax.ShapeDtypeStruct(shape, out)]
+    if token:
+        outs.append(jax.ShapeDtypeStruct((8, BLK), F32))
+    done = pl.pallas_call(
         kernel,
-        out_shape=jax.ShapeDtypeStruct(shape, out),
+        out_shape=outs,
         in_specs=[VMEM] * count + [ANY] * len(after),
-        out_specs=VMEM,
+        out_specs=[VMEM] * len(outs),
         compiler_params=pltpu.CompilerParams(vmem_limit_bytes=12 * MB),
         cost_estimate=pl.CostEstimate(flops=1, bytes_accessed=MB, transcendentals=0),
         name="add",
     )(*(t[0] for t in terms), *after)
+    return done if token else done[0]
 
 
 def home_kernel(core, home, p, q, after, away, keep):
@@ -272,6 +278,23 @@
         t = mine[which] + got[which].astype(F32)
         keep[which] = t[:4]
         away[which] = t[4:].astype(BF16)
+
+
+def last_kernel(own, more, keep, got, first, second, whole):
+    whole[...] = own[...] + more[...].astype(F32)
+    for which, dst in enumerate((first, second)):
+        dst[...] = (keep[which] + got[which].astype(F32)).astype(BF16)
+
+
+def run_last(own, more, keep, got):
+    return pl.pallas_call(
+        last_kernel,
+        out_shape=[sds(4, WIDTH)] * 2 + [jax.ShapeDtypeStruct((CAP, 16, BLK), F32)],
+        in_specs=[VMEM] * 4,
+        out_specs=[VMEM] * 3,
+        compiler_params=pltpu.CompilerParams(vmem_limit_bytes=12 * MB),
+        name="last",
+    )(own, more, keep, got)
 
 
 def run_home(home, p, q, after):
@@ -389,16 +412,17 @@
     op = add([(mine1, (3,)), (across1, (3,))], [op])
     xd = ring(op, "x", 4, -1)
 
-    grad_w2 = add([(parts[0], (0,)), (xa, (0,)), (xb, (0,)), across2], [op], F32)
-    away, keep = run_home(near, p, q, grad_w2)
+    terms = [(parts[0], (0,)), (xa, (0,)), (xb, (0,)), across2]
+    grad_w2, ready = add(terms, [op], F32, True)
+    away, keep = run_home(near, p, q, ready)
     got = swap(away, "c")
     op = add([(mine1, (1,)), (across1, (1,)), xc], [away, xd])
     xc = ring(op, "x", 4, 1)
     away, keep = run_half(keep, got)
     got = swap(away, "yl")
-    grad_w1 = add([(mine1, (0,)), (across1, (0,)), xc, xd], [away], F32)
-    t = narrow(keep + f32(got))
-    return t[0], t[1], grad_w1, grad_w2
+    own = add([(mine1, (0,)), (across1, (0,)), xd], [away], F32)
+    layer_out, grad_tokens, grad_w1 = run_last(own, xc, keep, got)
+    return layer_out, grad_tokens, grad_w1, grad_w2
 
 
 def prepare(w1_rows, w1_cols, w1_count, w2_rows, w2_cols, w2_count):

time: 103 us -> 102 us (level); the launches traced: 101 us -> 101 us
  local copies, waits for them, and re-layouts: 2.49 us -> 0.75 us
    ppermute x16, waiting for transfers between devices: 7.15 us -> 8.87 us  [swap(): return lax.ppermute(v, axis, [(0, 1), (1, 0)])]
    ppermute x6, starting transfers between devices: 11.1 us -> 12.2 us  [ring(): return lax.ppermute(v, (axis, 'c'), pairs)]
    unnamed x4 -> x2, local copies, waits for them, and re-layouts: 1.04 us -> 0.01 us
    pallas_call x14 -> x15, Pallas kernels: 2.88 us -> 2.94 us  [the longest x14 2.06 us: add(): pl.pallas_call(kernel, out_shape=outs, in_specs=[VMEM] * count + [ANY] *...]
  transfers between devices with their start and end apart: 36 -> 36, of which waited for: 14 -> 14; matrix products, arithmetic and copies ran while one was open for 3% -> 3% of each run, Pallas kernels for 3% -> 2%
where the time goes in v5:
time: 102 us; the launch traced here: 101 us
  starting transfers between devices  59.8 us (59%)
  waiting for transfers between devices  21.3 us (21%)
  Pallas kernels  13.7 us (13%)
  other arithmetic  3.66 us (4%)
  between operations  2.15 us (2%)
    ppermute x16, starting transfers between devices, swap(): return lax.ppermute(v, axis, [(0, 1), (1, 0)])  26.3 us
    ppermute x14, starting transfers between devices, ring(): return lax.ppermute(v, ('z', 'yl', 'c'), full)  21.3 us
    ppermute x6, starting transfers between devices, ring(): return lax.ppermute(v, (axis, 'c'), pairs)  12.2 us
    ppermute x16, waiting for transfers between devices, swap(): return lax.ppermute(v, axis, [(0, 1), (1, 0)])  8.87 us
    ppermute x14, waiting for transfers between devices, ring(): return lax.ppermute(v, ('z', 'yl', 'c'), full)  8.43 us
    ppermute x6, waiting for transfers between devices, ring(): return lax.ppermute(v, (axis, 'c'), pairs)  3.98 us
    pallas_call x1, Pallas kernels, run_partial(): pl.pallas_call(partial_kernel, out_shape=[sds(16, WIDTH)] * 2 + [sds(2, 6...  3.94 us
    pallas_call x1, Pallas kernels, run_hidden(): pl.pallas_call(hidden_kernel, out_shape=[sds(SB, BLK, BLK)] * 2 + [sds(BL...  3.51 us
  transfers between devices with their start and end apart: 36, of which 14 were waited for; matrix products, arithmetic and copies ran while one was open for 3% of the time, Pallas kernels for 2%

profile of v5, /device:TPU:1, one launch (start us, length us, event | category | flops | bytes accessed | tf_op | source)
XLA Modules:
  0.0 101.4 jit_solution(17713195307750580236)
XLA Ops:
  0.6 1.0 pad_maximum_fusion.x
  1.6 2.2 %collective-permute-start.1 = (bf16[2,4,8192]{2,1,0:T(4,128)(2,1)S(1)}, bf16[2,4,8192]{2,1,0:T(4,128)(2,1)S(1)}, u32[]{:S(2)}, u32[]{:S(2)}) collective-permute-start(bf16[2,4,8192]{2,1,0:T(4,128)(2,1)S(1)} %pad_maximum_fusion.x), channel_id=1, source_target_pairs={{0,2},{2,0},{1,3},{3,1},{4,6},{6,4},{5,7},{7,5},{8,10},{10,8},{9,1... | collective-permute-start | bytes 393224 | tf_op jit(solution)/shard_map/ppermute | solution.py:324
  3.8 1.2 %collective-permute-start = (bf16[2,4,8192]{2,1,0:T(4,128)(2,1)S(1)}, bf16[2,4,8192]{2,1,0:T(4,128)(2,1)S(1)}, u32[]{:S(2)}, u32[]{:S(2)}) collective-permute-start(bf16[2,4,8192]{2,1,0:T(4,128)(2,1)S(1)} %pad_maximum_fusion.x), channel_id=1, source_target_pairs={{0,1},{1,0},{2,3},{3,2},{4,5},{5,4},{6,7},{7,6},{8,9},{9,8},{10,11... | collective-permute-start | bytes 393224 | tf_op jit(solution)/shard_map/ppermute | solution.py:324
  5.0 1.1 %collective-permute-done.1.y = bf16[2,4,8192]{2,1,0:T(4,128)(2,1)S(1)} collective-permute-done((bf16[2,4,8192]{2,1,0:T(4,128)(2,1)S(1)}, bf16[2,4,8192]{2,1,0:T(4,128)(2,1)S(1)}, u32[]{:S(2)}, u32[]{:S(2)}) %collective-permute-start.1) | collective-permute-done | bytes 131104 | tf_op jit(solution)/shard_map/ppermute | solution.py:324
  6.2 3.7 %collective-permute-start.2 = (bf16[2,4,8192]{2,1,0:T(4,128)(2,1)S(1)}, bf16[2,4,8192]{2,1,0:T(4,128)(2,1)S(1)}, u32[]{:S(2)}, u32[]{:S(2)}) collective-permute-start(bf16[2,4,8192]{2,1,0:T(4,128)(2,1)S(1)} %collective-permute-done.1.y), channel_id=1, source_target_pairs={{0,1},{1,0},{2,3},{3,2},{4,5},{5,4},{6,7},{7,6},{8,9},{9,8},{10,11... | collective-permute-start | bytes 393224 | tf_op jit(solution)/shard_map/ppermute | solution.py:324
  11.4 4.2 %collective-permute-start.3 = (bf16[16,8192]{1,0:T(8,128)(2,1)S(1)}, bf16[16,8192]{1,0:T(8,128)(2,1)S(1)}, u32[]{:S(2)}, u32[]{:S(2)}) collective-permute-start(bf16[16,8192]{1,0:T(8,128)(2,1)S(1)} %get-tuple-element.43.refs_0_), channel_id=1, source_target_pairs={{0,4},{1,29},{2,6},{3,31},{4,8},{5,1},{6,10},{7,3},{8,12},{9,5},{1... | collective-permute-start | bytes 786440 | tf_op jit(solution)/shard_map/ppermute | solution.py:340
  15.6 0.7 collective-permute-start.7
  16.4 0.7 subtract_clamp_fusion
  17.0 0.7 concatenate.3.meta
  17.8 1.2 %collective-permute-done.3.refs_1_ = bf16[16,8192]{1,0:T(8,128)(2,1)S(1)} collective-permute-done((bf16[16,8192]{1,0:T(8,128)(2,1)S(1)}, bf16[16,8192]{1,0:T(8,128)(2,1)S(1)}, u32[]{:S(2)}, u32[]{:S(2)}) %collective-permute-start.3) | collective-permute-done | bytes 262176 | tf_op jit(solution)/shard_map/ppermute | solution.py:340
  18.9 3.1 %collective-permute-start.4 = (bf16[16,8192]{1,0:T(8,128)(2,1)S(1)}, bf16[16,8192]{1,0:T(8,128)(2,1)S(1)}, u32[]{:S(2)}, u32[]{:S(2)}) collective-permute-start(bf16[16,8192]{1,0:T(8,128)(2,1)S(1)} %collective-permute-done.3.refs_1_), channel_id=1, source_target_pairs={{0,4},{1,29},{2,6},{3,31},{4,8},{5,1},{6,10},{7,3},{8,12},{9,5},{1... | collective-permute-start | bytes 786440 | tf_op jit(solution)/shard_map/ppermute | solution.py:340
  22.1 1.8 %broadcast_select_fusion.1.w1 = bf16[64,128,128]{2,1,0:T(8,128)(2,1)S(1)} fusion(bf16[64,128,128]{2,1,0:T(8,128)(2,1)} %param.12, pred[64]{0:T(512)(128)(4,1)S(1)} %iota_compare_fusion.1), kind=kLoop, calls=%fused_computation.1 | loop fusion | flops 1048576 | bytes 4194368 | tf_op jit(solution)/shard_map/jit(_where)/select_n | solution.py:368
  23.9 1.0 collective-permute-start.8
  25.4 3.1 %collective-permute-start.5 = (bf16[16,8192]{1,0:T(8,128)(2,1)S(1)}, bf16[16,8192]{1,0:T(8,128)(2,1)S(1)}, u32[]{:S(2)}, u32[]{:S(2)}) collective-permute-start(bf16[16,8192]{1,0:T(8,128)(2,1)S(1)} %collective-permute-done.4.refs_2_), channel_id=1, source_target_pairs={{0,4},{1,29},{2,6},{3,31},{4,8},{5,1},{6,10},{7,3},{8,12},{9,5},{1... | collective-permute-start | bytes 786440 | tf_op jit(solution)/shard_map/ppermute | solution.py:340
  29.5 1.8 %collective-permute-start.9 = (bf16[16,8192]{1,0:T(8,128)(2,1)S(1)}, bf16[16,8192]{1,0:T(8,128)(2,1)S(1)}, u32[]{:S(2)}, u32[]{:S(2)}) collective-permute-start(bf16[16,8192]{1,0:T(8,128)(2,1)S(1)} %collective-permute-done.8.refs_7_), channel_id=1, source_target_pairs={{0,4},{1,29},{2,6},{3,31},{4,8},{5,1},{6,10},{7,3},{8,12},{9,5},{1... | collective-permute-start | bytes 786440 | tf_op jit(solution)/shard_map/ppermute | solution.py:340
  31.3 1.0 collective-permute-done.5.refs_3_
  32.3 2.6 %collective-permute-start.6 = (bf16[16,8192]{1,0:T(8,128)(2,1)S(1)}, bf16[16,8192]{1,0:T(8,128)(2,1)S(1)}, u32[]{:S(2)}, u32[]{:S(2)}) collective-permute-start(bf16[16,8192]{1,0:T(8,128)(2,1)S(1)} %collective-permute-done.5.refs_3_), channel_id=1, source_target_pairs={{0,4},{1,29},{2,6},{3,31},{4,8},{5,1},{6,10},{7,3},{8,12},{9,5},{1... | collective-permute-start | bytes 786440 | tf_op jit(solution)/shard_map/ppermute | solution.py:340
  34.9 0.5 collective-permute-start.11
  36.0 2.3 %collective-permute-start.16 = (bf16[16,8192]{1,0:T(8,128)(2,1)S(1)}, bf16[16,8192]{1,0:T(8,128)(2,1)S(1)}, u32[]{:S(2)}, u32[]{:S(2)}) collective-permute-start(bf16[16,8192]{1,0:T(8,128)(2,1)S(1)} %collective-permute-done.9.refs_8_), channel_id=1, source_target_pairs={{0,1},{1,0},{2,3},{3,2},{4,5},{5,4},{6,7},{7,6},{8,9},{9,8},{10,11... | collective-permute-start | bytes 786440 | tf_op jit(solution)/shard_map/ppermute | solution.py:324
  38.3 4.8 %collective-permute-start.13 = (bf16[16,8192]{1,0:T(8,128)(2,1)S(1)}, bf16[16,8192]{1,0:T(8,128)(2,1)S(1)}, u32[]{:S(2)}, u32[]{:S(2)}) collective-permute-start(bf16[16,8192]{1,0:T(8,128)(2,1)S(1)} %collective-permute-done.6.refs_4_), channel_id=1, source_target_pairs={{0,1},{1,0},{2,3},{3,2},{4,5},{5,4},{6,7},{7,6},{8,9},{9,8},{10,11... | collective-permute-start | bytes 786440 | tf_op jit(solution)/shard_map/ppermute | solution.py:324
  43.0 1.1 %collective-permute-done.13.refs_12_ = bf16[16,8192]{1,0:T(8,128)(2,1)S(1)} collective-permute-done((bf16[16,8192]{1,0:T(8,128)(2,1)S(1)}, bf16[16,8192]{1,0:T(8,128)(2,1)S(1)}, u32[]{:S(2)}, u32[]{:S(2)}) %collective-permute-start.13) | collective-permute-done | bytes 262176 | tf_op jit(solution)/shard_map/ppermute | solution.py:324
  44.2 3.5 %hidden.1 = (bf16[4,128,128]{2,1,0:T(8,128)(2,1)S(1)}, bf16[4,128,128]{2,1,0:T(8,128)(2,1)S(1)}, bf16[128,8192]{1,0:T(8,128)(2,1)S(1)}, bf16[128,8192]{1,0:T(8,128)(2,1)S(1)}) custom-call(s32[261]{0:T(512)S(1)} %concatenate.3.meta, bf16[64,128,128]{2,1,0:T(8,128)(2,1)S(1)} %broadcast_select_fusion.1.w1, bf16[64,128,128]{2,1,0:T(8,128)(2,1)S(1)} %broadcast_select_fusion.w2, ...), custom_call_target="tpu_custom_call" | custom-call | flops 2147483648 | bytes 12582912 | tf_op jit(solution)/shard_map/hidden/pallas_call | solution.py:184
  47.7 2.8 %weight.1 = (bf16[4,64,16,128]{3,2,1,0:T(8,128)(2,1)S(1)}, bf16[4,64,16,128]{3,2,1,0:T(8,128)(2,1)S(1)}, bf16[2,64,16,128]{3,2,1,0:T(8,128)(2,1)S(1)}, bf16[2,64...) custom-call(s32[261]{0:T(512)S(1)} %concatenate.3.meta, ...), custom_call_target="tpu_custom_call" | custom-call | flops 2147483648 | bytes 8388608 | tf_op jit(solution)/shard_map/weight/pallas_call | solution.py:210
  50.5 3.9 %partial.1 = (bf16[16,8192]{1,0:T(8,128)(2,1)S(1)}, bf16[16,8192]{1,0:T(8,128)(2,1)S(1)}, bf16[2,64,8192]{2,1,0:T(8,128)(2,1)S(1)}, bf16[2,48,8192]{2,1,0:T(8,128)(2,1)S(1)}) custom-call(s32[261]{0:T(512)S(1)} %concatenate.3.meta, bf16[64,128,128]{2,1,0:T(8,128)(2,1)S(1)} %broadcast_select_fusion.1.w1, bf16[64,128,128]{2,1,0:T(8,128)(2,1)S(1)} %broadcast_select_fusion.w2, ...), custom_call_target="tpu_custom_call" | custom-call | flops 2147483648 | bytes 12582912 | tf_op jit(solution)/shard_map/partial/pallas_call | solution.py:197
  54.9 2.5 %collective-permute-start.21 = (bf16[2,64,16,128]{3,2,1,0:T(8,128)(2,1)S(1)}, bf16[2,64,16,128]{3,2,1,0:T(8,128)(2,1)S(1)}, u32[]{:S(2)}, u32[]{:S(2)}) collective-permute-start(bf16[2,64,16,128]{3,2,1,0:T(8,128)(2,1)S(1)} %get-tuple-element.70), channel_id=1, source_target_pairs={{0,32},{1,97},{32,64},{33,1},{64,96},{65,33},{96,0},{97,65},{2,34}... | collective-permute-start | bytes 1572872 | tf_op jit(solution)/shard_map/ppermute | solution.py:341
  57.4 2.9 %collective-permute-start.17 = (bf16[4,64,16,128]{3,2,1,0:T(8,128)(2,1)S(1)}, bf16[4,64,16,128]{3,2,1,0:T(8,128)(2,1)S(1)}, u32[]{:S(2)}, u32[]{:S(2)}) collective-permute-start(bf16[4,64,16,128]{3,2,1,0:T(8,128)(2,1)S(1)} %get-tuple-element.64), channel_id=1, source_target_pairs={{0,128},{128,0},{1,129},{129,1},{2,130},{130,2},{3,131},{131,3},{4... | collective-permute-start | bytes 3145736 | tf_op jit(solution)/shard_map/ppermute | solution.py:324
  60.6 0.7 collective-permute-start.26
  61.3 2.2 %collective-permute-done.21.refs_1_ = bf16[2,64,16,128]{3,2,1,0:T(8,128)(2,1)S(1)} collective-permute-done((bf16[2,64,16,128]{3,2,1,0:T(8,128)(2,1)S(1)}, bf16[2,64,16,128]{3,2,1,0:T(8,128)(2,1)S(1)}, u32[]{:S(2)}, u32[]{:S(2)}) %collective-permute-start.21) | collective-permute-done | bytes 524320 | tf_op jit(solution)/shard_map/ppermute | solution.py:341
  63.6 3.7 %collective-permute-start.25 = (bf16[2,64,16,128]{3,2,1,0:T(8,128)(2,1)S(1)}, bf16[2,64,16,128]{3,2,1,0:T(8,128)(2,1)S(1)}, u32[]{:S(2)}, u32[]{:S(2)}) collective-permute-start(bf16[2,64,16,128]{3,2,1,0:T(8,128)(2,1)S(1)} %add.24.refs_3_), channel_id=1, source_target_pairs={{0,32},{1,97},{32,64},{33,1},{64,96},{65,33},{96,0},{97,65},{2,34}... | collective-permute-start | bytes 1572872 | tf_op jit(solution)/shard_map/ppermute | solution.py:341
  67.5 1.2 %collective-permute-done.23.refs_2_ = bf16[16,8192]{1,0:T(8,128)(2,1)S(1)} collective-permute-done((bf16[16,8192]{1,0:T(8,128)(2,1)S(1)}, bf16[16,8192]{1,0:T(8,128)(2,1)S(1)}, u32[]{:S(2)}, u32[]{:S(2)}) %collective-permute-start.23) | collective-permute-done | bytes 262176 | tf_op jit(solution)/shard_map/ppermute | solution.py:340
  68.8 1.3 %collective-permute-start.27 = (bf16[16,8192]{1,0:T(8,128)(2,1)S(1)}, bf16[16,8192]{1,0:T(8,128)(2,1)S(1)}, u32[]{:S(2)}, u32[]{:S(2)}) collective-permute-start(bf16[16,8192]{1,0:T(8,128)(2,1)S(1)} %add.26.refs_3_), channel_id=1, source_target_pairs={{0,4},{1,29},{2,6},{3,31},{4,8},{5,1},{6,10},{7,3},{8,12},{9,5},{1... | collective-permute-start | bytes 786440 | tf_op jit(solution)/shard_map/ppermute | solution.py:340
  70.1 2.9 %collective-permute-done.22.refs_2_ = bf16[16,8192]{1,0:T(8,128)(2,1)S(1)} collective-permute-done((bf16[16,8192]{1,0:T(8,128)(2,1)S(1)}, bf16[16,8192]{1,0:T(8,128)(2,1)S(1)}, u32[]{:S(2)}, u32[]{:S(2)}) %collective-permute-start.22) | collective-permute-done | bytes 262176 | tf_op jit(solution)/shard_map/ppermute | solution.py:340
  73.1 1.3 %collective-permute-start.24 = (bf16[16,8192]{1,0:T(8,128)(2,1)S(1)}, bf16[16,8192]{1,0:T(8,128)(2,1)S(1)}, u32[]{:S(2)}, u32[]{:S(2)}) collective-permute-start(bf16[16,8192]{1,0:T(8,128)(2,1)S(1)} %add.27.refs_3_), channel_id=1, source_target_pairs={{0,4},{1,29},{2,6},{3,31},{4,8},{5,1},{6,10},{7,3},{8,12},{9,5},{1... | collective-permute-start | bytes 786440 | tf_op jit(solution)/shard_map/ppermute | solution.py:340
  74.4 1.4 %collective-permute-done.27.refs_2_ = bf16[16,8192]{1,0:T(8,128)(2,1)S(1)} collective-permute-done((bf16[16,8192]{1,0:T(8,128)(2,1)S(1)}, bf16[16,8192]{1,0:T(8,128)(2,1)S(1)}, u32[]{:S(2)}, u32[]{:S(2)}) %collective-permute-start.27) | collective-permute-done | bytes 262176 | tf_op jit(solution)/shard_map/ppermute | solution.py:340
  75.9 1.3 %collective-permute-start.30 = (bf16[16,8192]{1,0:T(8,128)(2,1)S(1)}, bf16[16,8192]{1,0:T(8,128)(2,1)S(1)}, u32[]{:S(2)}, u32[]{:S(2)}) collective-permute-start(bf16[16,8192]{1,0:T(8,128)(2,1)S(1)} %add.28.refs_3_), channel_id=1, source_target_pairs={{0,4},{1,29},{2,6},{3,31},{4,8},{5,1},{6,10},{7,3},{8,12},{9,5},{1... | collective-permute-start | bytes 786440 | tf_op jit(solution)/shard_map/ppermute | solution.py:340
  77.3 3.3 %collective-permute-start.31 = (bf16[64,16,128]{2,1,0:T(8,128)(2,1)S(1)}, bf16[64,16,128]{2,1,0:T(8,128)(2,1)S(1)}, u32[]{:S(2)}, u32[]{:S(2)}) collective-permute-start(bf16[64,16,128]{2,1,0:T(8,128)(2,1)S(1)} %add.29.refs_3_), channel_id=1, source_target_pairs={{0,128},{128,0},{1,129},{129,1},{2,130},{130,2},{3,131},{131,3},{4... | collective-permute-start | bytes 786440 | tf_op jit(solution)/shard_map/ppermute | solution.py:324
  80.7 0.6 collective-permute-start.29
  81.3 1.8 %collective-permute-done.17.refs_1_ = bf16[4,64,16,128]{3,2,1,0:T(8,128)(2,1)S(1)} collective-permute-done((bf16[4,64,16,128]{3,2,1,0:T(8,128)(2,1)S(1)}, bf16[4,64,16,128]{3,2,1,0:T(8,128)(2,1)S(1)}, u32[]{:S(2)}, u32[]{:S(2)}) %collective-permute-start.17) | collective-permute-done | bytes 1048608 | tf_op jit(solution)/shard_map/ppermute | solution.py:324
  83.2 1.0 %collective-permute-start.28 = (bf16[64,16,128]{2,1,0:T(8,128)(2,1)S(1)}, bf16[64,16,128]{2,1,0:T(8,128)(2,1)S(1)}, u32[]{:S(2)}, u32[]{:S(2)}) collective-permute-start(bf16[64,16,128]{2,1,0:T(8,128)(2,1)S(1)} %add.32.refs_4_), channel_id=1, source_target_pairs={{0,96},{1,33},{32,0},{33,65},{64,32},{65,97},{96,64},{97,1},{2,98}... | collective-permute-start | bytes 786440 | tf_op jit(solution)/shard_map/ppermute | solution.py:341
  84.2 1.7 %collective-permute-start.33 = (bf16[64,16,128]{2,1,0:T(8,128)(2,1)S(1)}, bf16[64,16,128]{2,1,0:T(8,128)(2,1)S(1)}, u32[]{:S(2)}, u32[]{:S(2)}) collective-permute-start(bf16[64,16,128]{2,1,0:T(8,128)(2,1)S(1)} %add.31.refs_2_), channel_id=1, source_target_pairs={{0,32},{1,97},{32,64},{33,1},{64,96},{65,33},{96,0},{97,65},{2,34}... | collective-permute-start | bytes 786440 | tf_op jit(solution)/shard_map/ppermute | solution.py:341
  86.0 2.7 %collective-permute-done.31.refs_3_ = bf16[64,16,128]{2,1,0:T(8,128)(2,1)S(1)} collective-permute-done((bf16[64,16,128]{2,1,0:T(8,128)(2,1)S(1)}, bf16[64,16,128]{2,1,0:T(8,128)(2,1)S(1)}, u32[]{:S(2)}, u32[]{:S(2)}) %collective-permute-start.31) | collective-permute-done | bytes 262176 | tf_op jit(solution)/shard_map/ppermute | solution.py:324
  88.7 0.9 add.33
  89.9 2.5 %collective-permute-start.32 = (bf16[2,8,8192]{2,1,0:T(8,128)(2,1)S(1)}, bf16[2,8,8192]{2,1,0:T(8,128)(2,1)S(1)}, u32[]{:S(2)}, u32[]{:S(2)}) collective-permute-start(bf16[2,8,8192]{2,1,0:T(8,128)(2,1)S(1)} %get-tuple-element.75.refs_3_), channel_id=1, source_target_pairs={{0,1},{1,0},{2,3},{3,2},{4,5},{5,4},{6,7},{7,6},{8,9},{9,8},{10,11... | collective-permute-start | bytes 786440 | tf_op jit(solution)/shard_map/ppermute | solution.py:324
  92.5 2.6 %collective-permute-start.34 = (bf16[64,16,128]{2,1,0:T(8,128)(2,1)S(1)}, bf16[64,16,128]{2,1,0:T(8,128)(2,1)S(1)}, u32[]{:S(2)}, u32[]{:S(2)}) collective-permute-start(bf16[64,16,128]{2,1,0:T(8,128)(2,1)S(1)} %add.35), channel_id=1, source_target_pairs={{0,32},{1,97},{32,64},{33,1},{64,96},{65,33},{96,0},{97,65},{2,34}... | collective-permute-start | bytes 786440 | tf_op jit(solution)/shard_map/ppermute | solution.py:341
  95.2 1.4 %collective-permute-start.35 = (bf16[2,4,8192]{2,1,0:T(4,128)(2,1)S(1)}, bf16[2,4,8192]{2,1,0:T(4,128)(2,1)S(1)}, u32[]{:S(2)}, u32[]{:S(2)}) collective-permute-start(bf16[2,4,8192]{2,1,0:T(4,128)(2,1)S(1)} %get-tuple-element.76.refs_3_), channel_id=1, source_target_pairs={{0,2},{2,0},{1,3},{3,1},{4,6},{6,4},{5,7},{7,5},{8,10},{10,8},{9,1... | collective-permute-start | bytes 393224 | tf_op jit(solution)/shard_map/ppermute | solution.py:324
  96.7 1.8 %collective-permute-done.34.more = bf16[64,16,128]{2,1,0:T(8,128)(2,1)S(1)} collective-permute-done((bf16[64,16,128]{2,1,0:T(8,128)(2,1)S(1)}, bf16[64,16,128]{2,1,0:T(8,128)(2,1)S(1)}, u32[]{:S(2)}, u32[]{:S(2)}) %collective-permute-start.34) | collective-permute-done | bytes 262176 | tf_op jit(solution)/shard_map/ppermute | solution.py:341
  98.4 2.1 %collective-permute-done.35.got = bf16[2,4,8192]{2,1,0:T(4,128)(2,1)S(1)} collective-permute-done((bf16[2,4,8192]{2,1,0:T(4,128)(2,1)S(1)}, bf16[2,4,8192]{2,1,0:T(4,128)(2,1)S(1)}, u32[]{:S(2)}, u32[]{:S(2)}) %collective-permute-start.35) | collective-permute-done | bytes 131104 | tf_op jit(solution)/shard_map/ppermute | solution.py:324
  100.5 0.9 last.1
  (54 shorter events, 4.4 us)
Async XLA Ops:
  1.6 4.6 %collective-permute-start.1 = (bf16[2,4,8192]{2,1,0:T(4,128)(2,1)S(1)}, bf16[2,4,8192]{2,1,0:T(4,128)(2,1)S(1)}, u32[]{:S(2)}, u32[]{:S(2)}) collective-permute-start(bf16[2,4,8192]{2,1,0:T(4,128)(2,1)S(1)} %pad_maximum_fusion.x), channel_id=1, source_target_pairs={{0,2},{2,0},{1,3},{3,1},{4,6},{6,4},{5,7},{7,5},{8,10},{10,8},{9,1... | collective-permute-start | bytes 393224 | tf_op jit(solution)/shard_map/ppermute | solution.py:324
  3.8 7.4 %collective-permute-start = (bf16[2,4,8192]{2,1,0:T(4,128)(2,1)S(1)}, bf16[2,4,8192]{2,1,0:T(4,128)(2,1)S(1)}, u32[]{:S(2)}, u32[]{:S(2)}) collective-permute-start(bf16[2,4,8192]{2,1,0:T(4,128)(2,1)S(1)} %pad_maximum_fusion.x), channel_id=1, source_target_pairs={{0,1},{1,0},{2,3},{3,2},{4,5},{5,4},{6,7},{7,6},{8,9},{9,8},{10,11... | collective-permute-start | bytes 393224 | tf_op jit(solution)/shard_map/ppermute | solution.py:324
  6.2 5.0 %collective-permute-start.2 = (bf16[2,4,8192]{2,1,0:T(4,128)(2,1)S(1)}, bf16[2,4,8192]{2,1,0:T(4,128)(2,1)S(1)}, u32[]{:S(2)}, u32[]{:S(2)}) collective-permute-start(bf16[2,4,8192]{2,1,0:T(4,128)(2,1)S(1)} %collective-permute-done.1.y), channel_id=1, source_target_pairs={{0,1},{1,0},{2,3},{3,2},{4,5},{5,4},{6,7},{7,6},{8,9},{9,8},{10,11... | collective-permute-start | bytes 393224 | tf_op jit(solution)/shard_map/ppermute | solution.py:324
  11.4 7.5 %collective-permute-start.3 = (bf16[16,8192]{1,0:T(8,128)(2,1)S(1)}, bf16[16,8192]{1,0:T(8,128)(2,1)S(1)}, u32[]{:S(2)}, u32[]{:S(2)}) collective-permute-start(bf16[16,8192]{1,0:T(8,128)(2,1)S(1)} %get-tuple-element.43.refs_0_), channel_id=1, source_target_pairs={{0,4},{1,29},{2,6},{3,31},{4,8},{5,1},{6,10},{7,3},{8,12},{9,5},{1... | collective-permute-start | bytes 786440 | tf_op jit(solution)/shard_map/ppermute | solution.py:340
  15.6 8.2 %collective-permute-start.7 = (bf16[16,8192]{1,0:T(8,128)(2,1)S(1)}, bf16[16,8192]{1,0:T(8,128)(2,1)S(1)}, u32[]{:S(2)}, u32[]{:S(2)}) collective-permute-start(bf16[16,8192]{1,0:T(8,128)(2,1)S(1)} %get-tuple-element.58.refs_5_), channel_id=1, source_target_pairs={{0,4},{1,29},{2,6},{3,31},{4,8},{5,1},{6,10},{7,3},{8,12},{9,5},{1... | collective-permute-start | bytes 786440 | tf_op jit(solution)/shard_map/ppermute | solution.py:340
  17.8 7.1 %copy-start = (bf16[64,128,128]{2,1,0:T(8,128)(2,1)S(1)}, bf16[64,128,128]{2,1,0:T(8,128)(2,1)}, u32[]{:S(2)}) copy-start(bf16[64,128,128]{2,1,0:T(8,128)(2,1)} %param.16) | copy-start | bytes 6291460
  18.9 6.4 %collective-permute-start.4 = (bf16[16,8192]{1,0:T(8,128)(2,1)S(1)}, bf16[16,8192]{1,0:T(8,128)(2,1)S(1)}, u32[]{:S(2)}, u32[]{:S(2)}) collective-permute-start(bf16[16,8192]{1,0:T(8,128)(2,1)S(1)} %collective-permute-done.3.refs_1_), channel_id=1, source_target_pairs={{0,4},{1,29},{2,6},{3,31},{4,8},{5,1},{6,10},{7,3},{8,12},{9,5},{1... | collective-permute-start | bytes 786440 | tf_op jit(solution)/shard_map/ppermute | solution.py:340
  23.9 5.6 %collective-permute-start.8 = (bf16[16,8192]{1,0:T(8,128)(2,1)S(1)}, bf16[16,8192]{1,0:T(8,128)(2,1)S(1)}, u32[]{:S(2)}, u32[]{:S(2)}) collective-permute-start(bf16[16,8192]{1,0:T(8,128)(2,1)S(1)} %collective-permute-done.7.refs_6_), channel_id=1, source_target_pairs={{0,4},{1,29},{2,6},{3,31},{4,8},{5,1},{6,10},{7,3},{8,12},{9,5},{1... | collective-permute-start | bytes 786440 | tf_op jit(solution)/shard_map/ppermute | solution.py:340
  25.4 6.9 %collective-permute-start.5 = (bf16[16,8192]{1,0:T(8,128)(2,1)S(1)}, bf16[16,8192]{1,0:T(8,128)(2,1)S(1)}, u32[]{:S(2)}, u32[]{:S(2)}) collective-permute-start(bf16[16,8192]{1,0:T(8,128)(2,1)S(1)} %collective-permute-done.4.refs_2_), channel_id=1, source_target_pairs={{0,4},{1,29},{2,6},{3,31},{4,8},{5,1},{6,10},{7,3},{8,12},{9,5},{1... | collective-permute-start | bytes 786440 | tf_op jit(solution)/shard_map/ppermute | solution.py:340
  28.5 6.9 %collective-permute-start.14 = (bf16[16,8192]{1,0:T(8,128)(2,1)S(1)}, bf16[16,8192]{1,0:T(8,128)(2,1)S(1)}, u32[]{:S(2)}, u32[]{:S(2)}) collective-permute-start(bf16[16,8192]{1,0:T(8,128)(2,1)S(1)} %collective-permute-done.7.refs_6_), channel_id=1, source_target_pairs={{0,1},{1,0},{2,3},{3,2},{4,5},{5,4},{6,7},{7,6},{8,9},{9,8},{10,11... | collective-permute-start | bytes 786440 | tf_op jit(solution)/shard_map/ppermute | solution.py:324
  28.5 7.0 %collective-permute-start.10 = (bf16[16,8192]{1,0:T(8,128)(2,1)S(1)}, bf16[16,8192]{1,0:T(8,128)(2,1)S(1)}, u32[]{:S(2)}, u32[]{:S(2)}) collective-permute-start(bf16[16,8192]{1,0:T(8,128)(2,1)S(1)} %collective-permute-done.3.refs_1_), channel_id=1, source_target_pairs={{0,1},{1,0},{2,3},{3,2},{4,5},{5,4},{6,7},{7,6},{8,9},{9,8},{10,11... | collective-permute-start | bytes 786440 | tf_op jit(solution)/shard_map/ppermute | solution.py:324
  29.5 6.5 %collective-permute-start.9 = (bf16[16,8192]{1,0:T(8,128)(2,1)S(1)}, bf16[16,8192]{1,0:T(8,128)(2,1)S(1)}, u32[]{:S(2)}, u32[]{:S(2)}) collective-permute-start(bf16[16,8192]{1,0:T(8,128)(2,1)S(1)} %collective-permute-done.8.refs_7_), channel_id=1, source_target_pairs={{0,4},{1,29},{2,6},{3,31},{4,8},{5,1},{6,10},{7,3},{8,12},{9,5},{1... | collective-permute-start | bytes 786440 | tf_op jit(solution)/shard_map/ppermute | solution.py:340
  32.3 6.0 %collective-permute-start.6 = (bf16[16,8192]{1,0:T(8,128)(2,1)S(1)}, bf16[16,8192]{1,0:T(8,128)(2,1)S(1)}, u32[]{:S(2)}, u32[]{:S(2)}) collective-permute-start(bf16[16,8192]{1,0:T(8,128)(2,1)S(1)} %collective-permute-done.5.refs_3_), channel_id=1, source_target_pairs={{0,4},{1,29},{2,6},{3,31},{4,8},{5,1},{6,10},{7,3},{8,12},{9,5},{1... | collective-permute-start | bytes 786440 | tf_op jit(solution)/shard_map/ppermute | solution.py:340
  34.9 8.1 %collective-permute-start.11 = (bf16[16,8192]{1,0:T(8,128)(2,1)S(1)}, bf16[16,8192]{1,0:T(8,128)(2,1)S(1)}, u32[]{:S(2)}, u32[]{:S(2)}) collective-permute-start(bf16[16,8192]{1,0:T(8,128)(2,1)S(1)} %collective-permute-done.4.refs_2_), channel_id=1, source_target_pairs={{0,1},{1,0},{2,3},{3,2},{4,5},{5,4},{6,7},{7,6},{8,9},{9,8},{10,11... | collective-permute-start | bytes 786440 | tf_op jit(solution)/shard_map/ppermute | solution.py:324
  35.4 7.6 %collective-permute-start.15 = (bf16[16,8192]{1,0:T(8,128)(2,1)S(1)}, bf16[16,8192]{1,0:T(8,128)(2,1)S(1)}, u32[]{:S(2)}, u32[]{:S(2)}) collective-permute-start(bf16[16,8192]{1,0:T(8,128)(2,1)S(1)} %collective-permute-done.8.refs_7_), channel_id=1, source_target_pairs={{0,1},{1,0},{2,3},{3,2},{4,5},{5,4},{6,7},{7,6},{8,9},{9,8},{10,11... | collective-permute-start | bytes 786440 | tf_op jit(solution)/shard_map/ppermute | solution.py:324
  35.5 7.5 %collective-permute-start.12 = (bf16[16,8192]{1,0:T(8,128)(2,1)S(1)}, bf16[16,8192]{1,0:T(8,128)(2,1)S(1)}, u32[]{:S(2)}, u32[]{:S(2)}) collective-permute-start(bf16[16,8192]{1,0:T(8,128)(2,1)S(1)} %collective-permute-done.5.refs_3_), channel_id=1, source_target_pairs={{0,1},{1,0},{2,3},{3,2},{4,5},{5,4},{6,7},{7,6},{8,9},{9,8},{10,11... | collective-permute-start | bytes 786440 | tf_op jit(solution)/shard_map/ppermute | solution.py:324
  36.0 7.1 %collective-permute-start.16 = (bf16[16,8192]{1,0:T(8,128)(2,1)S(1)}, bf16[16,8192]{1,0:T(8,128)(2,1)S(1)}, u32[]{:S(2)}, u32[]{:S(2)}) collective-permute-start(bf16[16,8192]{1,0:T(8,128)(2,1)S(1)} %collective-permute-done.9.refs_8_), channel_id=1, source_target_pairs={{0,1},{1,0},{2,3},{3,2},{4,5},{5,4},{6,7},{7,6},{8,9},{9,8},{10,11... | collective-permute-start | bytes 786440 | tf_op jit(solution)/shard_map/ppermute | solution.py:324
  38.3 5.9 %collective-permute-start.13 = (bf16[16,8192]{1,0:T(8,128)(2,1)S(1)}, bf16[16,8192]{1,0:T(8,128)(2,1)S(1)}, u32[]{:S(2)}, u32[]{:S(2)}) collective-permute-start(bf16[16,8192]{1,0:T(8,128)(2,1)S(1)} %collective-permute-done.6.refs_4_), channel_id=1, source_target_pairs={{0,1},{1,0},{2,3},{3,2},{4,5},{5,4},{6,7},{7,6},{8,9},{9,8},{10,11... | collective-permute-start | bytes 786440 | tf_op jit(solution)/shard_map/ppermute | solution.py:324
  54.4 6.0 %collective-permute-start.18 = (bf16[2,48,8192]{2,1,0:T(8,128)(2,1)S(1)}, bf16[2,48,8192]{2,1,0:T(8,128)(2,1)S(1)}, u32[]{:S(2)}, u32[]{:S(2)}) collective-permute-start(bf16[2,48,8192]{2,1,0:T(8,128)(2,1)S(1)} %get-tuple-element.66), channel_id=1, source_target_pairs={{0,1},{1,0},{2,3},{3,2},{4,5},{5,4},{6,7},{7,6},{8,9},{9,8},{10,11... | collective-permute-start | bytes 4718600 | tf_op jit(solution)/shard_map/ppermute | solution.py:324
  54.9 8.6 %collective-permute-start.21 = (bf16[2,64,16,128]{3,2,1,0:T(8,128)(2,1)S(1)}, bf16[2,64,16,128]{3,2,1,0:T(8,128)(2,1)S(1)}, u32[]{:S(2)}, u32[]{:S(2)}) collective-permute-start(bf16[2,64,16,128]{3,2,1,0:T(8,128)(2,1)S(1)} %get-tuple-element.70), channel_id=1, source_target_pairs={{0,32},{1,97},{32,64},{33,1},{64,96},{65,33},{96,0},{97,65},{2,34}... | collective-permute-start | bytes 1572872 | tf_op jit(solution)/shard_map/ppermute | solution.py:341
  57.4 2.9 %collective-permute-start.19 = (bf16[16,8192]{1,0:T(8,128)(2,1)S(1)}, bf16[16,8192]{1,0:T(8,128)(2,1)S(1)}, u32[]{:S(2)}, u32[]{:S(2)}) collective-permute-start(bf16[16,8192]{1,0:T(8,128)(2,1)S(1)} %get-tuple-element.68), channel_id=1, source_target_pairs={{0,1},{1,0},{2,3},{3,2},{4,5},{5,4},{6,7},{7,6},{8,9},{9,8},{10,11... | collective-permute-start | bytes 786440 | tf_op jit(solution)/shard_map/ppermute | solution.py:324
  57.4 25.7 %collective-permute-start.17 = (bf16[4,64,16,128]{3,2,1,0:T(8,128)(2,1)S(1)}, bf16[4,64,16,128]{3,2,1,0:T(8,128)(2,1)S(1)}, u32[]{:S(2)}, u32[]{:S(2)}) collective-permute-start(bf16[4,64,16,128]{3,2,1,0:T(8,128)(2,1)S(1)} %get-tuple-element.64), channel_id=1, source_target_pairs={{0,128},{128,0},{1,129},{129,1},{2,130},{130,2},{3,131},{131,3},{4... | collective-permute-start | bytes 3145736 | tf_op jit(solution)/shard_map/ppermute | solution.py:324
  60.3 7.0 %collective-permute-start.20 = (bf16[16,8192]{1,0:T(8,128)(2,1)S(1)}, bf16[16,8192]{1,0:T(8,128)(2,1)S(1)}, u32[]{:S(2)}, u32[]{:S(2)}) collective-permute-start(bf16[16,8192]{1,0:T(8,128)(2,1)S(1)} %add.22.refs_2_), channel_id=1, source_target_pairs={{0,4},{1,29},{2,6},{3,31},{4,8},{5,1},{6,10},{7,3},{8,12},{9,5},{1... | collective-permute-start | bytes 786440 | tf_op jit(solution)/shard_map/ppermute | solution.py:340
  60.5 8.2 %collective-permute-start.23 = (bf16[16,8192]{1,0:T(8,128)(2,1)S(1)}, bf16[16,8192]{1,0:T(8,128)(2,1)S(1)}, u32[]{:S(2)}, u32[]{:S(2)}) collective-permute-start(bf16[16,8192]{1,0:T(8,128)(2,1)S(1)} %add.23.refs_2_), channel_id=1, source_target_pairs={{0,4},{1,29},{2,6},{3,31},{4,8},{5,1},{6,10},{7,3},{8,12},{9,5},{1... | collective-permute-start | bytes 786440 | tf_op jit(solution)/shard_map/ppermute | solution.py:340
  60.6 16.6 %collective-permute-start.26 = (bf16[2,64,16,128]{3,2,1,0:T(8,128)(2,1)S(1)}, bf16[2,64,16,128]{3,2,1,0:T(8,128)(2,1)S(1)}, u32[]{:S(2)}, u32[]{:S(2)}) collective-permute-start(bf16[2,64,16,128]{3,2,1,0:T(8,128)(2,1)S(1)} %get-tuple-element.72), channel_id=1, source_target_pairs={{0,96},{1,33},{32,0},{33,65},{64,32},{65,97},{96,64},{97,1},{2,98}... | collective-permute-start | bytes 1572872 | tf_op jit(solution)/shard_map/ppermute | solution.py:341
  63.6 13.6 %collective-permute-start.25 = (bf16[2,64,16,128]{3,2,1,0:T(8,128)(2,1)S(1)}, bf16[2,64,16,128]{3,2,1,0:T(8,128)(2,1)S(1)}, u32[]{:S(2)}, u32[]{:S(2)}) collective-permute-start(bf16[2,64,16,128]{3,2,1,0:T(8,128)(2,1)S(1)} %add.24.refs_3_), channel_id=1, source_target_pairs={{0,32},{1,97},{32,64},{33,1},{64,96},{65,33},{96,0},{97,65},{2,34}... | collective-permute-start | bytes 1572872 | tf_op jit(solution)/shard_map/ppermute | solution.py:341
  67.4 5.6 %collective-permute-start.22 = (bf16[16,8192]{1,0:T(8,128)(2,1)S(1)}, bf16[16,8192]{1,0:T(8,128)(2,1)S(1)}, u32[]{:S(2)}, u32[]{:S(2)}) collective-permute-start(bf16[16,8192]{1,0:T(8,128)(2,1)S(1)} %add.25.refs_3_), channel_id=1, source_target_pairs={{0,4},{1,29},{2,6},{3,31},{4,8},{5,1},{6,10},{7,3},{8,12},{9,5},{1... | collective-permute-start | bytes 786440 | tf_op jit(solution)/shard_map/ppermute | solution.py:340
  68.8 7.0 %collective-permute-start.27 = (bf16[16,8192]{1,0:T(8,128)(2,1)S(1)}, bf16[16,8192]{1,0:T(8,128)(2,1)S(1)}, u32[]{:S(2)}, u32[]{:S(2)}) collective-permute-start(bf16[16,8192]{1,0:T(8,128)(2,1)S(1)} %add.26.refs_3_), channel_id=1, source_target_pairs={{0,4},{1,29},{2,6},{3,31},{4,8},{5,1},{6,10},{7,3},{8,12},{9,5},{1... | collective-permute-start | bytes 786440 | tf_op jit(solution)/shard_map/ppermute | solution.py:340
  73.1 7.5 %collective-permute-start.24 = (bf16[16,8192]{1,0:T(8,128)(2,1)S(1)}, bf16[16,8192]{1,0:T(8,128)(2,1)S(1)}, u32[]{:S(2)}, u32[]{:S(2)}) collective-permute-start(bf16[16,8192]{1,0:T(8,128)(2,1)S(1)} %add.27.refs_3_), channel_id=1, source_target_pairs={{0,4},{1,29},{2,6},{3,31},{4,8},{5,1},{6,10},{7,3},{8,12},{9,5},{1... | collective-permute-start | bytes 786440 | tf_op jit(solution)/shard_map/ppermute | solution.py:340
  75.9 13.7 %collective-permute-start.30 = (bf16[16,8192]{1,0:T(8,128)(2,1)S(1)}, bf16[16,8192]{1,0:T(8,128)(2,1)S(1)}, u32[]{:S(2)}, u32[]{:S(2)}) collective-permute-start(bf16[16,8192]{1,0:T(8,128)(2,1)S(1)} %add.28.refs_3_), channel_id=1, source_target_pairs={{0,4},{1,29},{2,6},{3,31},{4,8},{5,1},{6,10},{7,3},{8,12},{9,5},{1... | collective-permute-start | bytes 786440 | tf_op jit(solution)/shard_map/ppermute | solution.py:340
  77.3 11.4 %collective-permute-start.31 = (bf16[64,16,128]{2,1,0:T(8,128)(2,1)S(1)}, bf16[64,16,128]{2,1,0:T(8,128)(2,1)S(1)}, u32[]{:S(2)}, u32[]{:S(2)}) collective-permute-start(bf16[64,16,128]{2,1,0:T(8,128)(2,1)S(1)} %add.29.refs_3_), channel_id=1, source_target_pairs={{0,128},{128,0},{1,129},{129,1},{2,130},{130,2},{3,131},{131,3},{4... | collective-permute-start | bytes 786440 | tf_op jit(solution)/shard_map/ppermute | solution.py:324
  80.7 8.9 %collective-permute-start.29 = (bf16[16,8192]{1,0:T(8,128)(2,1)S(1)}, bf16[16,8192]{1,0:T(8,128)(2,1)S(1)}, u32[]{:S(2)}, u32[]{:S(2)}) collective-permute-start(bf16[16,8192]{1,0:T(8,128)(2,1)S(1)} %add.30.refs_2_), channel_id=1, source_target_pairs={{0,4},{1,29},{2,6},{3,31},{4,8},{5,1},{6,10},{7,3},{8,12},{9,5},{1... | collective-permute-start | bytes 786440 | tf_op jit(solution)/shard_map/ppermute | solution.py:340
  83.2 9.2 %collective-permute-start.28 = (bf16[64,16,128]{2,1,0:T(8,128)(2,1)S(1)}, bf16[64,16,128]{2,1,0:T(8,128)(2,1)S(1)}, u32[]{:S(2)}, u32[]{:S(2)}) collective-permute-start(bf16[64,16,128]{2,1,0:T(8,128)(2,1)S(1)} %add.32.refs_4_), channel_id=1, source_target_pairs={{0,96},{1,33},{32,0},{33,65},{64,32},{65,97},{96,64},{97,1},{2,98}... | collective-permute-start | bytes 786440 | tf_op jit(solution)/shard_map/ppermute | solution.py:341
  84.2 8.2 %collective-permute-start.33 = (bf16[64,16,128]{2,1,0:T(8,128)(2,1)S(1)}, bf16[64,16,128]{2,1,0:T(8,128)(2,1)S(1)}, u32[]{:S(2)}, u32[]{:S(2)}) collective-permute-start(bf16[64,16,128]{2,1,0:T(8,128)(2,1)S(1)} %add.31.refs_2_), channel_id=1, source_target_pairs={{0,32},{1,97},{32,64},{33,1},{64,96},{65,33},{96,0},{97,65},{2,34}... | collective-permute-start | bytes 786440 | tf_op jit(solution)/shard_map/ppermute | solution.py:341
  89.9 5.2 %collective-permute-start.32 = (bf16[2,8,8192]{2,1,0:T(8,128)(2,1)S(1)}, bf16[2,8,8192]{2,1,0:T(8,128)(2,1)S(1)}, u32[]{:S(2)}, u32[]{:S(2)}) collective-permute-start(bf16[2,8,8192]{2,1,0:T(8,128)(2,1)S(1)} %get-tuple-element.75.refs_3_), channel_id=1, source_target_pairs={{0,1},{1,0},{2,3},{3,2},{4,5},{5,4},{6,7},{7,6},{8,9},{9,8},{10,11... | collective-permute-start | bytes 786440 | tf_op jit(solution)/shard_map/ppermute | solution.py:324
  92.5 5.9 %collective-permute-start.34 = (bf16[64,16,128]{2,1,0:T(8,128)(2,1)S(1)}, bf16[64,16,128]{2,1,0:T(8,128)(2,1)S(1)}, u32[]{:S(2)}, u32[]{:S(2)}) collective-permute-start(bf16[64,16,128]{2,1,0:T(8,128)(2,1)S(1)} %add.35), channel_id=1, source_target_pairs={{0,32},{1,97},{32,64},{33,1},{64,96},{65,33},{96,0},{97,65},{2,34}... | collective-permute-start | bytes 786440 | tf_op jit(solution)/shard_map/ppermute | solution.py:341
  95.2 5.3 %collective-permute-start.35 = (bf16[2,4,8192]{2,1,0:T(4,128)(2,1)S(1)}, bf16[2,4,8192]{2,1,0:T(4,128)(2,1)S(1)}, u32[]{:S(2)}, u32[]{:S(2)}) collective-permute-start(bf16[2,4,8192]{2,1,0:T(4,128)(2,1)S(1)} %get-tuple-element.76.refs_3_), channel_id=1, source_target_pairs={{0,2},{2,0},{1,3},{3,1},{4,6},{6,4},{5,7},{7,5},{8,10},{10,8},{9,1... | collective-permute-start | bytes 393224 | tf_op jit(solution)/shard_map/ppermute | solution.py:324

commit v6 on v5

--- a/solution.py
+++ b/solution.py
@@ -164,7 +164,8 @@
     for which in range(2):
         rows = []
         for a, b in ((x, xc), (y, yc)):
-            a, b = a[which].astype(F32), b[which].astype(F32)
+            here = slice(4 * which, 4 * which + 4)
+            a, b = a[...].astype(F32)[here], b[...].astype(F32)[here]
             rows += [jnp.where(low, a, b), jnp.where(low, b, a)]
         both.append(jnp.concatenate(rows, axis=0))
     p[...] = jnp.where(low, both[0], both[1]).astype(BF16)
@@ -354,7 +355,7 @@
 
 
 def gather_rows(tokens, grads, early):
-    x = jnp.stack([tokens, grads])
+    x = jnp.concatenate([tokens, grads], axis=0)
     y = swap(x, "yl")
     core = lax.axis_index("c").astype(jnp.int32).reshape(1)
     p0, q0 = run_chunk(core, x, swap(x, "c"), y, swap(y, "c"))

time: 102 us -> 102 us (level)
  no operation moved by 1% of the time
where the time goes in v6:
time: 102 us; the launch traced here: 101 us
  starting transfers between devices  59.8 us (59%)
  waiting for transfers between devices  21.3 us (21%)
  Pallas kernels  13.7 us (13%)
  other arithmetic  3.63 us (4%)
  between operations  2.15 us (2%)
    ppermute x16, starting transfers between devices, swap(): return lax.ppermute(v, axis, [(0, 1), (1, 0)])  26.3 us
    ppermute x14, starting transfers between devices, ring(): return lax.ppermute(v, ('z', 'yl', 'c'), full)  21.3 us
    ppermute x6, starting transfers between devices, ring(): return lax.ppermute(v, (axis, 'c'), pairs)  12.1 us
    ppermute x16, waiting for transfers between devices, swap(): return lax.ppermute(v, axis, [(0, 1), (1, 0)])  8.88 us
    ppermute x14, waiting for transfers between devices, ring(): return lax.ppermute(v, ('z', 'yl', 'c'), full)  8.43 us
    ppermute x6, waiting for transfers between devices, ring(): return lax.ppermute(v, (axis, 'c'), pairs)  4.03 us
    pallas_call x1, Pallas kernels, run_partial(): pl.pallas_call(partial_kernel, out_shape=[sds(16, WIDTH)] * 2 + [sds(2, 6...  3.93 us
    pallas_call x1, Pallas kernels, run_hidden(): pl.pallas_call(hidden_kernel, out_shape=[sds(SB, BLK, BLK)] * 2 + [sds(BL...  3.51 us
  transfers between devices with their start and end apart: 36, of which 14 were waited for; matrix products, arithmetic and copies ran while one was open for 3% of the time, Pallas kernels for 2%

profile of v6, /device:TPU:1, one launch (start us, length us, event | category | flops | bytes accessed | tf_op | source)
XLA Modules:
  0.0 101.3 jit_solution(223246102688972450)
XLA Ops:
  0.6 0.9 pad_maximum_fusion.x
  1.6 2.2 %collective-permute-start.1 = (bf16[8,8192]{1,0:T(8,128)(2,1)S(1)}, bf16[8,8192]{1,0:T(8,128)(2,1)S(1)}, u32[]{:S(2)}, u32[]{:S(2)}) collective-permute-start(bf16[8,8192]{1,0:T(8,128)(2,1)S(1)} %pad_maximum_fusion.x), channel_id=1, source_target_pairs={{0,2},{2,0},{1,3},{3,1},{4,6},{6,4},{5,7},{7,5},{8,10},{10,8},{9,1... | collective-permute-start | bytes 393224 | tf_op jit(solution)/shard_map/ppermute | solution.py:325
  3.8 1.2 %collective-permute-start = (bf16[8,8192]{1,0:T(8,128)(2,1)S(1)}, bf16[8,8192]{1,0:T(8,128)(2,1)S(1)}, u32[]{:S(2)}, u32[]{:S(2)}) collective-permute-start(bf16[8,8192]{1,0:T(8,128)(2,1)S(1)} %pad_maximum_fusion.x), channel_id=1, source_target_pairs={{0,1},{1,0},{2,3},{3,2},{4,5},{5,4},{6,7},{7,6},{8,9},{9,8},{10,11... | collective-permute-start | bytes 393224 | tf_op jit(solution)/shard_map/ppermute | solution.py:325
  5.0 1.1 %collective-permute-done.1.y = bf16[8,8192]{1,0:T(8,128)(2,1)S(1)} collective-permute-done((bf16[8,8192]{1,0:T(8,128)(2,1)S(1)}, bf16[8,8192]{1,0:T(8,128)(2,1)S(1)}, u32[]{:S(2)}, u32[]{:S(2)}) %collective-permute-start.1) | collective-permute-done | bytes 131104 | tf_op jit(solution)/shard_map/ppermute | solution.py:325
  6.1 3.7 %collective-permute-start.2 = (bf16[8,8192]{1,0:T(8,128)(2,1)S(1)}, bf16[8,8192]{1,0:T(8,128)(2,1)S(1)}, u32[]{:S(2)}, u32[]{:S(2)}) collective-permute-start(bf16[8,8192]{1,0:T(8,128)(2,1)S(1)} %collective-permute-done.1.y), channel_id=1, source_target_pairs={{0,1},{1,0},{2,3},{3,2},{4,5},{5,4},{6,7},{7,6},{8,9},{9,8},{10,11... | collective-permute-start | bytes 393224 | tf_op jit(solution)/shard_map/ppermute | solution.py:325
  11.4 4.2 %collective-permute-start.3 = (bf16[16,8192]{1,0:T(8,128)(2,1)S(1)}, bf16[16,8192]{1,0:T(8,128)(2,1)S(1)}, u32[]{:S(2)}, u32[]{:S(2)}) collective-permute-start(bf16[16,8192]{1,0:T(8,128)(2,1)S(1)} %get-tuple-element.43.refs_0_), channel_id=1, source_target_pairs={{0,4},{1,29},{2,6},{3,31},{4,8},{5,1},{6,10},{7,3},{8,12},{9,5},{1... | collective-permute-start | bytes 786440 | tf_op jit(solution)/shard_map/ppermute | solution.py:341
  15.6 0.7 collective-permute-start.7
  16.3 0.7 subtract_clamp_fusion
  17.0 0.7 concatenate.7.meta
  17.8 1.2 %collective-permute-done.3.refs_1_ = bf16[16,8192]{1,0:T(8,128)(2,1)S(1)} collective-permute-done((bf16[16,8192]{1,0:T(8,128)(2,1)S(1)}, bf16[16,8192]{1,0:T(8,128)(2,1)S(1)}, u32[]{:S(2)}, u32[]{:S(2)}) %collective-permute-start.3) | collective-permute-done | bytes 262176 | tf_op jit(solution)/shard_map/ppermute | solution.py:341
  18.9 3.1 %collective-permute-start.4 = (bf16[16,8192]{1,0:T(8,128)(2,1)S(1)}, bf16[16,8192]{1,0:T(8,128)(2,1)S(1)}, u32[]{:S(2)}, u32[]{:S(2)}) collective-permute-start(bf16[16,8192]{1,0:T(8,128)(2,1)S(1)} %collective-permute-done.3.refs_1_), channel_id=1, source_target_pairs={{0,4},{1,29},{2,6},{3,31},{4,8},{5,1},{6,10},{7,3},{8,12},{9,5},{1... | collective-permute-start | bytes 786440 | tf_op jit(solution)/shard_map/ppermute | solution.py:341
  22.0 1.8 %broadcast_select_fusion.1.w1 = bf16[64,128,128]{2,1,0:T(8,128)(2,1)S(1)} fusion(bf16[64,128,128]{2,1,0:T(8,128)(2,1)} %param.12, pred[64]{0:T(512)(128)(4,1)S(1)} %iota_compare_fusion.1), kind=kLoop, calls=%fused_computation.1 | loop fusion | flops 1048576 | bytes 4194368 | tf_op jit(solution)/shard_map/jit(_where)/select_n | solution.py:369
  23.8 1.0 collective-permute-start.8
  25.4 3.1 %collective-permute-start.5 = (bf16[16,8192]{1,0:T(8,128)(2,1)S(1)}, bf16[16,8192]{1,0:T(8,128)(2,1)S(1)}, u32[]{:S(2)}, u32[]{:S(2)}) collective-permute-start(bf16[16,8192]{1,0:T(8,128)(2,1)S(1)} %collective-permute-done.4.refs_2_), channel_id=1, source_target_pairs={{0,4},{1,29},{2,6},{3,31},{4,8},{5,1},{6,10},{7,3},{8,12},{9,5},{1... | collective-permute-start | bytes 786440 | tf_op jit(solution)/shard_map/ppermute | solution.py:341
  29.4 1.8 %collective-permute-start.9 = (bf16[16,8192]{1,0:T(8,128)(2,1)S(1)}, bf16[16,8192]{1,0:T(8,128)(2,1)S(1)}, u32[]{:S(2)}, u32[]{:S(2)}) collective-permute-start(bf16[16,8192]{1,0:T(8,128)(2,1)S(1)} %collective-permute-done.8.refs_7_), channel_id=1, source_target_pairs={{0,4},{1,29},{2,6},{3,31},{4,8},{5,1},{6,10},{7,3},{8,12},{9,5},{1... | collective-permute-start | bytes 786440 | tf_op jit(solution)/shard_map/ppermute | solution.py:341
  31.3 1.0 collective-permute-done.5.refs_3_
  32.3 2.6 %collective-permute-start.6 = (bf16[16,8192]{1,0:T(8,128)(2,1)S(1)}, bf16[16,8192]{1,0:T(8,128)(2,1)S(1)}, u32[]{:S(2)}, u32[]{:S(2)}) collective-permute-start(bf16[16,8192]{1,0:T(8,128)(2,1)S(1)} %collective-permute-done.5.refs_3_), channel_id=1, source_target_pairs={{0,4},{1,29},{2,6},{3,31},{4,8},{5,1},{6,10},{7,3},{8,12},{9,5},{1... | collective-permute-start | bytes 786440 | tf_op jit(solution)/shard_map/ppermute | solution.py:341
  34.9 0.5 collective-permute-start.11
  35.9 2.3 %collective-permute-start.16 = (bf16[16,8192]{1,0:T(8,128)(2,1)S(1)}, bf16[16,8192]{1,0:T(8,128)(2,1)S(1)}, u32[]{:S(2)}, u32[]{:S(2)}) collective-permute-start(bf16[16,8192]{1,0:T(8,128)(2,1)S(1)} %collective-permute-done.9.refs_8_), channel_id=1, source_target_pairs={{0,1},{1,0},{2,3},{3,2},{4,5},{5,4},{6,7},{7,6},{8,9},{9,8},{10,11... | collective-permute-start | bytes 786440 | tf_op jit(solution)/shard_map/ppermute | solution.py:325
  38.2 4.8 %collective-permute-start.13 = (bf16[16,8192]{1,0:T(8,128)(2,1)S(1)}, bf16[16,8192]{1,0:T(8,128)(2,1)S(1)}, u32[]{:S(2)}, u32[]{:S(2)}) collective-permute-start(bf16[16,8192]{1,0:T(8,128)(2,1)S(1)} %collective-permute-done.6.refs_4_), channel_id=1, source_target_pairs={{0,1},{1,0},{2,3},{3,2},{4,5},{5,4},{6,7},{7,6},{8,9},{9,8},{10,11... | collective-permute-start | bytes 786440 | tf_op jit(solution)/shard_map/ppermute | solution.py:325
  43.0 1.1 %collective-permute-done.13.refs_12_ = bf16[16,8192]{1,0:T(8,128)(2,1)S(1)} collective-permute-done((bf16[16,8192]{1,0:T(8,128)(2,1)S(1)}, bf16[16,8192]{1,0:T(8,128)(2,1)S(1)}, u32[]{:S(2)}, u32[]{:S(2)}) %collective-permute-start.13) | collective-permute-done | bytes 262176 | tf_op jit(solution)/shard_map/ppermute | solution.py:325
  44.2 3.5 %hidden.1 = (bf16[4,128,128]{2,1,0:T(8,128)(2,1)S(1)}, bf16[4,128,128]{2,1,0:T(8,128)(2,1)S(1)}, bf16[128,8192]{1,0:T(8,128)(2,1)S(1)}, bf16[128,8192]{1,0:T(8,128)(2,1)S(1)}) custom-call(s32[261]{0:T(512)S(1)} %concatenate.7.meta, bf16[64,128,128]{2,1,0:T(8,128)(2,1)S(1)} %broadcast_select_fusion.1.w1, bf16[64,128,128]{2,1,0:T(8,128)(2,1)S(1)} %broadcast_select_fusion.w2, ...), custom_call_target="tpu_custom_call" | custom-call | flops 2147483648 | bytes 12582912 | tf_op jit(solution)/shard_map/hidden/pallas_call | solution.py:185
  47.7 2.8 %weight.1 = (bf16[4,64,16,128]{3,2,1,0:T(8,128)(2,1)S(1)}, bf16[4,64,16,128]{3,2,1,0:T(8,128)(2,1)S(1)}, bf16[2,64,16,128]{3,2,1,0:T(8,128)(2,1)S(1)}, bf16[2,64...) custom-call(s32[261]{0:T(512)S(1)} %concatenate.7.meta, ...), custom_call_target="tpu_custom_call" | custom-call | flops 2147483648 | bytes 8388608 | tf_op jit(solution)/shard_map/weight/pallas_call | solution.py:211
  50.4 3.9 %partial.1 = (bf16[16,8192]{1,0:T(8,128)(2,1)S(1)}, bf16[16,8192]{1,0:T(8,128)(2,1)S(1)}, bf16[2,64,8192]{2,1,0:T(8,128)(2,1)S(1)}, bf16[2,48,8192]{2,1,0:T(8,128)(2,1)S(1)}) custom-call(s32[261]{0:T(512)S(1)} %concatenate.7.meta, bf16[64,128,128]{2,1,0:T(8,128)(2,1)S(1)} %broadcast_select_fusion.1.w1, bf16[64,128,128]{2,1,0:T(8,128)(2,1)S(1)} %broadcast_select_fusion.w2, ...), custom_call_target="tpu_custom_call" | custom-call | flops 2147483648 | bytes 12582912 | tf_op jit(solution)/shard_map/partial/pallas_call | solution.py:198
  54.8 2.5 %collective-permute-start.21 = (bf16[2,64,16,128]{3,2,1,0:T(8,128)(2,1)S(1)}, bf16[2,64,16,128]{3,2,1,0:T(8,128)(2,1)S(1)}, u32[]{:S(2)}, u32[]{:S(2)}) collective-permute-start(bf16[2,64,16,128]{3,2,1,0:T(8,128)(2,1)S(1)} %get-tuple-element.70), channel_id=1, source_target_pairs={{0,32},{1,97},{32,64},{33,1},{64,96},{65,33},{96,0},{97,65},{2,34}... | collective-permute-start | bytes 1572872 | tf_op jit(solution)/shard_map/ppermute | solution.py:342
  57.3 2.9 %collective-permute-start.17 = (bf16[4,64,16,128]{3,2,1,0:T(8,128)(2,1)S(1)}, bf16[4,64,16,128]{3,2,1,0:T(8,128)(2,1)S(1)}, u32[]{:S(2)}, u32[]{:S(2)}) collective-permute-start(bf16[4,64,16,128]{3,2,1,0:T(8,128)(2,1)S(1)} %get-tuple-element.64), channel_id=1, source_target_pairs={{0,128},{128,0},{1,129},{129,1},{2,130},{130,2},{3,131},{131,3},{4... | collective-permute-start | bytes 3145736 | tf_op jit(solution)/shard_map/ppermute | solution.py:325
  60.6 0.6 collective-permute-start.26
  61.2 2.2 %collective-permute-done.21.refs_1_ = bf16[2,64,16,128]{3,2,1,0:T(8,128)(2,1)S(1)} collective-permute-done((bf16[2,64,16,128]{3,2,1,0:T(8,128)(2,1)S(1)}, bf16[2,64,16,128]{3,2,1,0:T(8,128)(2,1)S(1)}, u32[]{:S(2)}, u32[]{:S(2)}) %collective-permute-start.21) | collective-permute-done | bytes 524320 | tf_op jit(solution)/shard_map/ppermute | solution.py:342
  63.6 3.7 %collective-permute-start.25 = (bf16[2,64,16,128]{3,2,1,0:T(8,128)(2,1)S(1)}, bf16[2,64,16,128]{3,2,1,0:T(8,128)(2,1)S(1)}, u32[]{:S(2)}, u32[]{:S(2)}) collective-permute-start(bf16[2,64,16,128]{3,2,1,0:T(8,128)(2,1)S(1)} %add.24.refs_3_), channel_id=1, source_target_pairs={{0,32},{1,97},{32,64},{33,1},{64,96},{65,33},{96,0},{97,65},{2,34}... | collective-permute-start | bytes 1572872 | tf_op jit(solution)/shard_map/ppermute | solution.py:342
  67.5 1.3 %collective-permute-done.23.refs_2_ = bf16[16,8192]{1,0:T(8,128)(2,1)S(1)} collective-permute-done((bf16[16,8192]{1,0:T(8,128)(2,1)S(1)}, bf16[16,8192]{1,0:T(8,128)(2,1)S(1)}, u32[]{:S(2)}, u32[]{:S(2)}) %collective-permute-start.23) | collective-permute-done | bytes 262176 | tf_op jit(solution)/shard_map/ppermute | solution.py:341
  68.8 1.3 %collective-permute-start.27 = (bf16[16,8192]{1,0:T(8,128)(2,1)S(1)}, bf16[16,8192]{1,0:T(8,128)(2,1)S(1)}, u32[]{:S(2)}, u32[]{:S(2)}) collective-permute-start(bf16[16,8192]{1,0:T(8,128)(2,1)S(1)} %add.26.refs_3_), channel_id=1, source_target_pairs={{0,4},{1,29},{2,6},{3,31},{4,8},{5,1},{6,10},{7,3},{8,12},{9,5},{1... | collective-permute-start | bytes 786440 | tf_op jit(solution)/shard_map/ppermute | solution.py:341
  70.1 2.8 %collective-permute-done.22.refs_2_ = bf16[16,8192]{1,0:T(8,128)(2,1)S(1)} collective-permute-done((bf16[16,8192]{1,0:T(8,128)(2,1)S(1)}, bf16[16,8192]{1,0:T(8,128)(2,1)S(1)}, u32[]{:S(2)}, u32[]{:S(2)}) %collective-permute-start.22) | collective-permute-done | bytes 262176 | tf_op jit(solution)/shard_map/ppermute | solution.py:341
  73.1 1.3 %collective-permute-start.24 = (bf16[16,8192]{1,0:T(8,128)(2,1)S(1)}, bf16[16,8192]{1,0:T(8,128)(2,1)S(1)}, u32[]{:S(2)}, u32[]{:S(2)}) collective-permute-start(bf16[16,8192]{1,0:T(8,128)(2,1)S(1)} %add.27.refs_3_), channel_id=1, source_target_pairs={{0,4},{1,29},{2,6},{3,31},{4,8},{5,1},{6,10},{7,3},{8,12},{9,5},{1... | collective-permute-start | bytes 786440 | tf_op jit(solution)/shard_map/ppermute | solution.py:341
  74.3 1.4 %collective-permute-done.27.refs_2_ = bf16[16,8192]{1,0:T(8,128)(2,1)S(1)} collective-permute-done((bf16[16,8192]{1,0:T(8,128)(2,1)S(1)}, bf16[16,8192]{1,0:T(8,128)(2,1)S(1)}, u32[]{:S(2)}, u32[]{:S(2)}) %collective-permute-start.27) | collective-permute-done | bytes 262176 | tf_op jit(solution)/shard_map/ppermute | solution.py:341
  75.9 1.3 %collective-permute-start.30 = (bf16[16,8192]{1,0:T(8,128)(2,1)S(1)}, bf16[16,8192]{1,0:T(8,128)(2,1)S(1)}, u32[]{:S(2)}, u32[]{:S(2)}) collective-permute-start(bf16[16,8192]{1,0:T(8,128)(2,1)S(1)} %add.28.refs_3_), channel_id=1, source_target_pairs={{0,4},{1,29},{2,6},{3,31},{4,8},{5,1},{6,10},{7,3},{8,12},{9,5},{1... | collective-permute-start | bytes 786440 | tf_op jit(solution)/shard_map/ppermute | solution.py:341
  77.3 3.3 %collective-permute-start.31 = (bf16[64,16,128]{2,1,0:T(8,128)(2,1)S(1)}, bf16[64,16,128]{2,1,0:T(8,128)(2,1)S(1)}, u32[]{:S(2)}, u32[]{:S(2)}) collective-permute-start(bf16[64,16,128]{2,1,0:T(8,128)(2,1)S(1)} %add.29.refs_3_), channel_id=1, source_target_pairs={{0,128},{128,0},{1,129},{129,1},{2,130},{130,2},{3,131},{131,3},{4... | collective-permute-start | bytes 786440 | tf_op jit(solution)/shard_map/ppermute | solution.py:325
  80.7 0.6 collective-permute-start.29
  81.3 1.8 %collective-permute-done.17.refs_1_ = bf16[4,64,16,128]{3,2,1,0:T(8,128)(2,1)S(1)} collective-permute-done((bf16[4,64,16,128]{3,2,1,0:T(8,128)(2,1)S(1)}, bf16[4,64,16,128]{3,2,1,0:T(8,128)(2,1)S(1)}, u32[]{:S(2)}, u32[]{:S(2)}) %collective-permute-start.17) | collective-permute-done | bytes 1048608 | tf_op jit(solution)/shard_map/ppermute | solution.py:325
  83.2 1.0 collective-permute-start.28
  84.2 1.7 %collective-permute-start.33 = (bf16[64,16,128]{2,1,0:T(8,128)(2,1)S(1)}, bf16[64,16,128]{2,1,0:T(8,128)(2,1)S(1)}, u32[]{:S(2)}, u32[]{:S(2)}) collective-permute-start(bf16[64,16,128]{2,1,0:T(8,128)(2,1)S(1)} %add.31.refs_2_), channel_id=1, source_target_pairs={{0,32},{1,97},{32,64},{33,1},{64,96},{65,33},{96,0},{97,65},{2,34}... | collective-permute-start | bytes 786440 | tf_op jit(solution)/shard_map/ppermute | solution.py:342
  85.9 2.7 %collective-permute-done.31.refs_3_ = bf16[64,16,128]{2,1,0:T(8,128)(2,1)S(1)} collective-permute-done((bf16[64,16,128]{2,1,0:T(8,128)(2,1)S(1)}, bf16[64,16,128]{2,1,0:T(8,128)(2,1)S(1)}, u32[]{:S(2)}, u32[]{:S(2)}) %collective-permute-start.31) | collective-permute-done | bytes 262176 | tf_op jit(solution)/shard_map/ppermute | solution.py:325
  88.7 0.9 add.33
  89.9 2.5 %collective-permute-start.32 = (bf16[2,8,8192]{2,1,0:T(8,128)(2,1)S(1)}, bf16[2,8,8192]{2,1,0:T(8,128)(2,1)S(1)}, u32[]{:S(2)}, u32[]{:S(2)}) collective-permute-start(bf16[2,8,8192]{2,1,0:T(8,128)(2,1)S(1)} %get-tuple-element.75.refs_3_), channel_id=1, source_target_pairs={{0,1},{1,0},{2,3},{3,2},{4,5},{5,4},{6,7},{7,6},{8,9},{9,8},{10,11... | collective-permute-start | bytes 786440 | tf_op jit(solution)/shard_map/ppermute | solution.py:325
  92.5 2.6 %collective-permute-start.34 = (bf16[64,16,128]{2,1,0:T(8,128)(2,1)S(1)}, bf16[64,16,128]{2,1,0:T(8,128)(2,1)S(1)}, u32[]{:S(2)}, u32[]{:S(2)}) collective-permute-start(bf16[64,16,128]{2,1,0:T(8,128)(2,1)S(1)} %add.35), channel_id=1, source_target_pairs={{0,32},{1,97},{32,64},{33,1},{64,96},{65,33},{96,0},{97,65},{2,34}... | collective-permute-start | bytes 786440 | tf_op jit(solution)/shard_map/ppermute | solution.py:342
  95.1 1.4 %collective-permute-start.35 = (bf16[2,4,8192]{2,1,0:T(4,128)(2,1)S(1)}, bf16[2,4,8192]{2,1,0:T(4,128)(2,1)S(1)}, u32[]{:S(2)}, u32[]{:S(2)}) collective-permute-start(bf16[2,4,8192]{2,1,0:T(4,128)(2,1)S(1)} %get-tuple-element.76.refs_3_), channel_id=1, source_target_pairs={{0,2},{2,0},{1,3},{3,1},{4,6},{6,4},{5,7},{7,5},{8,10},{10,8},{9,1... | collective-permute-start | bytes 393224 | tf_op jit(solution)/shard_map/ppermute | solution.py:325
  96.6 1.8 %collective-permute-done.34.more = bf16[64,16,128]{2,1,0:T(8,128)(2,1)S(1)} collective-permute-done((bf16[64,16,128]{2,1,0:T(8,128)(2,1)S(1)}, bf16[64,16,128]{2,1,0:T(8,128)(2,1)S(1)}, u32[]{:S(2)}, u32[]{:S(2)}) %collective-permute-start.34) | collective-permute-done | bytes 262176 | tf_op jit(solution)/shard_map/ppermute | solution.py:342
  98.4 2.1 %collective-permute-done.35.got = bf16[2,4,8192]{2,1,0:T(4,128)(2,1)S(1)} collective-permute-done((bf16[2,4,8192]{2,1,0:T(4,128)(2,1)S(1)}, bf16[2,4,8192]{2,1,0:T(4,128)(2,1)S(1)}, u32[]{:S(2)}, u32[]{:S(2)}) %collective-permute-start.35) | collective-permute-done | bytes 131104 | tf_op jit(solution)/shard_map/ppermute | solution.py:325
  100.4 0.9 last.1
  (54 shorter events, 4.5 us)
Async XLA Ops:
  1.6 4.6 %collective-permute-start.1 = (bf16[8,8192]{1,0:T(8,128)(2,1)S(1)}, bf16[8,8192]{1,0:T(8,128)(2,1)S(1)}, u32[]{:S(2)}, u32[]{:S(2)}) collective-permute-start(bf16[8,8192]{1,0:T(8,128)(2,1)S(1)} %pad_maximum_fusion.x), channel_id=1, source_target_pairs={{0,2},{2,0},{1,3},{3,1},{4,6},{6,4},{5,7},{7,5},{8,10},{10,8},{9,1... | collective-permute-start | bytes 393224 | tf_op jit(solution)/shard_map/ppermute | solution.py:325
  3.8 7.4 %collective-permute-start = (bf16[8,8192]{1,0:T(8,128)(2,1)S(1)}, bf16[8,8192]{1,0:T(8,128)(2,1)S(1)}, u32[]{:S(2)}, u32[]{:S(2)}) collective-permute-start(bf16[8,8192]{1,0:T(8,128)(2,1)S(1)} %pad_maximum_fusion.x), channel_id=1, source_target_pairs={{0,1},{1,0},{2,3},{3,2},{4,5},{5,4},{6,7},{7,6},{8,9},{9,8},{10,11... | collective-permute-start | bytes 393224 | tf_op jit(solution)/shard_map/ppermute | solution.py:325
  6.1 5.0 %collective-permute-start.2 = (bf16[8,8192]{1,0:T(8,128)(2,1)S(1)}, bf16[8,8192]{1,0:T(8,128)(2,1)S(1)}, u32[]{:S(2)}, u32[]{:S(2)}) collective-permute-start(bf16[8,8192]{1,0:T(8,128)(2,1)S(1)} %collective-permute-done.1.y), channel_id=1, source_target_pairs={{0,1},{1,0},{2,3},{3,2},{4,5},{5,4},{6,7},{7,6},{8,9},{9,8},{10,11... | collective-permute-start | bytes 393224 | tf_op jit(solution)/shard_map/ppermute | solution.py:325
  11.4 7.5 %collective-permute-start.3 = (bf16[16,8192]{1,0:T(8,128)(2,1)S(1)}, bf16[16,8192]{1,0:T(8,128)(2,1)S(1)}, u32[]{:S(2)}, u32[]{:S(2)}) collective-permute-start(bf16[16,8192]{1,0:T(8,128)(2,1)S(1)} %get-tuple-element.43.refs_0_), channel_id=1, source_target_pairs={{0,4},{1,29},{2,6},{3,31},{4,8},{5,1},{6,10},{7,3},{8,12},{9,5},{1... | collective-permute-start | bytes 786440 | tf_op jit(solution)/shard_map/ppermute | solution.py:341
  15.6 8.2 %collective-permute-start.7 = (bf16[16,8192]{1,0:T(8,128)(2,1)S(1)}, bf16[16,8192]{1,0:T(8,128)(2,1)S(1)}, u32[]{:S(2)}, u32[]{:S(2)}) collective-permute-start(bf16[16,8192]{1,0:T(8,128)(2,1)S(1)} %get-tuple-element.58.refs_5_), channel_id=1, source_target_pairs={{0,4},{1,29},{2,6},{3,31},{4,8},{5,1},{6,10},{7,3},{8,12},{9,5},{1... | collective-permute-start | bytes 786440 | tf_op jit(solution)/shard_map/ppermute | solution.py:341
  17.8 7.1 %copy-start = (bf16[64,128,128]{2,1,0:T(8,128)(2,1)S(1)}, bf16[64,128,128]{2,1,0:T(8,128)(2,1)}, u32[]{:S(2)}) copy-start(bf16[64,128,128]{2,1,0:T(8,128)(2,1)} %param.16) | copy-start | bytes 6291460
  18.9 6.4 %collective-permute-start.4 = (bf16[16,8192]{1,0:T(8,128)(2,1)S(1)}, bf16[16,8192]{1,0:T(8,128)(2,1)S(1)}, u32[]{:S(2)}, u32[]{:S(2)}) collective-permute-start(bf16[16,8192]{1,0:T(8,128)(2,1)S(1)} %collective-permute-done.3.refs_1_), channel_id=1, source_target_pairs={{0,4},{1,29},{2,6},{3,31},{4,8},{5,1},{6,10},{7,3},{8,12},{9,5},{1... | collective-permute-start | bytes 786440 | tf_op jit(solution)/shard_map/ppermute | solution.py:341
  23.8 5.6 %collective-permute-start.8 = (bf16[16,8192]{1,0:T(8,128)(2,1)S(1)}, bf16[16,8192]{1,0:T(8,128)(2,1)S(1)}, u32[]{:S(2)}, u32[]{:S(2)}) collective-permute-start(bf16[16,8192]{1,0:T(8,128)(2,1)S(1)} %collective-permute-done.7.refs_6_), channel_id=1, source_target_pairs={{0,4},{1,29},{2,6},{3,31},{4,8},{5,1},{6,10},{7,3},{8,12},{9,5},{1... | collective-permute-start | bytes 786440 | tf_op jit(solution)/shard_map/ppermute | solution.py:341
  25.4 6.9 %collective-permute-start.5 = (bf16[16,8192]{1,0:T(8,128)(2,1)S(1)}, bf16[16,8192]{1,0:T(8,128)(2,1)S(1)}, u32[]{:S(2)}, u32[]{:S(2)}) collective-permute-start(bf16[16,8192]{1,0:T(8,128)(2,1)S(1)} %collective-permute-done.4.refs_2_), channel_id=1, source_target_pairs={{0,4},{1,29},{2,6},{3,31},{4,8},{5,1},{6,10},{7,3},{8,12},{9,5},{1... | collective-permute-start | bytes 786440 | tf_op jit(solution)/shard_map/ppermute | solution.py:341
  28.5 6.9 %collective-permute-start.14 = (bf16[16,8192]{1,0:T(8,128)(2,1)S(1)}, bf16[16,8192]{1,0:T(8,128)(2,1)S(1)}, u32[]{:S(2)}, u32[]{:S(2)}) collective-permute-start(bf16[16,8192]{1,0:T(8,128)(2,1)S(1)} %collective-permute-done.7.refs_6_), channel_id=1, source_target_pairs={{0,1},{1,0},{2,3},{3,2},{4,5},{5,4},{6,7},{7,6},{8,9},{9,8},{10,11... | collective-permute-start | bytes 786440 | tf_op jit(solution)/shard_map/ppermute | solution.py:325
  28.5 7.0 %collective-permute-start.10 = (bf16[16,8192]{1,0:T(8,128)(2,1)S(1)}, bf16[16,8192]{1,0:T(8,128)(2,1)S(1)}, u32[]{:S(2)}, u32[]{:S(2)}) collective-permute-start(bf16[16,8192]{1,0:T(8,128)(2,1)S(1)} %collective-permute-done.3.refs_1_), channel_id=1, source_target_pairs={{0,1},{1,0},{2,3},{3,2},{4,5},{5,4},{6,7},{7,6},{8,9},{9,8},{10,11... | collective-permute-start | bytes 786440 | tf_op jit(solution)/shard_map/ppermute | solution.py:325
  29.4 6.5 %collective-permute-start.9 = (bf16[16,8192]{1,0:T(8,128)(2,1)S(1)}, bf16[16,8192]{1,0:T(8,128)(2,1)S(1)}, u32[]{:S(2)}, u32[]{:S(2)}) collective-permute-start(bf16[16,8192]{1,0:T(8,128)(2,1)S(1)} %collective-permute-done.8.refs_7_), channel_id=1, source_target_pairs={{0,4},{1,29},{2,6},{3,31},{4,8},{5,1},{6,10},{7,3},{8,12},{9,5},{1... | collective-permute-start | bytes 786440 | tf_op jit(solution)/shard_map/ppermute | solution.py:341
  32.3 6.0 %collective-permute-start.6 = (bf16[16,8192]{1,0:T(8,128)(2,1)S(1)}, bf16[16,8192]{1,0:T(8,128)(2,1)S(1)}, u32[]{:S(2)}, u32[]{:S(2)}) collective-permute-start(bf16[16,8192]{1,0:T(8,128)(2,1)S(1)} %collective-permute-done.5.refs_3_), channel_id=1, source_target_pairs={{0,4},{1,29},{2,6},{3,31},{4,8},{5,1},{6,10},{7,3},{8,12},{9,5},{1... | collective-permute-start | bytes 786440 | tf_op jit(solution)/shard_map/ppermute | solution.py:341
  34.9 8.1 %collective-permute-start.11 = (bf16[16,8192]{1,0:T(8,128)(2,1)S(1)}, bf16[16,8192]{1,0:T(8,128)(2,1)S(1)}, u32[]{:S(2)}, u32[]{:S(2)}) collective-permute-start(bf16[16,8192]{1,0:T(8,128)(2,1)S(1)} %collective-permute-done.4.refs_2_), channel_id=1, source_target_pairs={{0,1},{1,0},{2,3},{3,2},{4,5},{5,4},{6,7},{7,6},{8,9},{9,8},{10,11... | collective-permute-start | bytes 786440 | tf_op jit(solution)/shard_map/ppermute | solution.py:325
  35.4 7.6 %collective-permute-start.15 = (bf16[16,8192]{1,0:T(8,128)(2,1)S(1)}, bf16[16,8192]{1,0:T(8,128)(2,1)S(1)}, u32[]{:S(2)}, u32[]{:S(2)}) collective-permute-start(bf16[16,8192]{1,0:T(8,128)(2,1)S(1)} %collective-permute-done.8.refs_7_), channel_id=1, source_target_pairs={{0,1},{1,0},{2,3},{3,2},{4,5},{5,4},{6,7},{7,6},{8,9},{9,8},{10,11... | collective-permute-start | bytes 786440 | tf_op jit(solution)/shard_map/ppermute | solution.py:325
  35.5 7.5 %collective-permute-start.12 = (bf16[16,8192]{1,0:T(8,128)(2,1)S(1)}, bf16[16,8192]{1,0:T(8,128)(2,1)S(1)}, u32[]{:S(2)}, u32[]{:S(2)}) collective-permute-start(bf16[16,8192]{1,0:T(8,128)(2,1)S(1)} %collective-permute-done.5.refs_3_), channel_id=1, source_target_pairs={{0,1},{1,0},{2,3},{3,2},{4,5},{5,4},{6,7},{7,6},{8,9},{9,8},{10,11... | collective-permute-start | bytes 786440 | tf_op jit(solution)/shard_map/ppermute | solution.py:325
  35.9 7.1 %collective-permute-start.16 = (bf16[16,8192]{1,0:T(8,128)(2,1)S(1)}, bf16[16,8192]{1,0:T(8,128)(2,1)S(1)}, u32[]{:S(2)}, u32[]{:S(2)}) collective-permute-start(bf16[16,8192]{1,0:T(8,128)(2,1)S(1)} %collective-permute-done.9.refs_8_), channel_id=1, source_target_pairs={{0,1},{1,0},{2,3},{3,2},{4,5},{5,4},{6,7},{7,6},{8,9},{9,8},{10,11... | collective-permute-start | bytes 786440 | tf_op jit(solution)/shard_map/ppermute | solution.py:325
  38.2 5.9 %collective-permute-start.13 = (bf16[16,8192]{1,0:T(8,128)(2,1)S(1)}, bf16[16,8192]{1,0:T(8,128)(2,1)S(1)}, u32[]{:S(2)}, u32[]{:S(2)}) collective-permute-start(bf16[16,8192]{1,0:T(8,128)(2,1)S(1)} %collective-permute-done.6.refs_4_), channel_id=1, source_target_pairs={{0,1},{1,0},{2,3},{3,2},{4,5},{5,4},{6,7},{7,6},{8,9},{9,8},{10,11... | collective-permute-start | bytes 786440 | tf_op jit(solution)/shard_map/ppermute | solution.py:325
  54.4 6.0 %collective-permute-start.18 = (bf16[2,48,8192]{2,1,0:T(8,128)(2,1)S(1)}, bf16[2,48,8192]{2,1,0:T(8,128)(2,1)S(1)}, u32[]{:S(2)}, u32[]{:S(2)}) collective-permute-start(bf16[2,48,8192]{2,1,0:T(8,128)(2,1)S(1)} %get-tuple-element.66), channel_id=1, source_target_pairs={{0,1},{1,0},{2,3},{3,2},{4,5},{5,4},{6,7},{7,6},{8,9},{9,8},{10,11... | collective-permute-start | bytes 4718600 | tf_op jit(solution)/shard_map/ppermute | solution.py:325
  54.8 8.6 %collective-permute-start.21 = (bf16[2,64,16,128]{3,2,1,0:T(8,128)(2,1)S(1)}, bf16[2,64,16,128]{3,2,1,0:T(8,128)(2,1)S(1)}, u32[]{:S(2)}, u32[]{:S(2)}) collective-permute-start(bf16[2,64,16,128]{3,2,1,0:T(8,128)(2,1)S(1)} %get-tuple-element.70), channel_id=1, source_target_pairs={{0,32},{1,97},{32,64},{33,1},{64,96},{65,33},{96,0},{97,65},{2,34}... | collective-permute-start | bytes 1572872 | tf_op jit(solution)/shard_map/ppermute | solution.py:342
  57.3 2.9 %collective-permute-start.19 = (bf16[16,8192]{1,0:T(8,128)(2,1)S(1)}, bf16[16,8192]{1,0:T(8,128)(2,1)S(1)}, u32[]{:S(2)}, u32[]{:S(2)}) collective-permute-start(bf16[16,8192]{1,0:T(8,128)(2,1)S(1)} %get-tuple-element.68), channel_id=1, source_target_pairs={{0,1},{1,0},{2,3},{3,2},{4,5},{5,4},{6,7},{7,6},{8,9},{9,8},{10,11... | collective-permute-start | bytes 786440 | tf_op jit(solution)/shard_map/ppermute | solution.py:325
  57.3 25.7 %collective-permute-start.17 = (bf16[4,64,16,128]{3,2,1,0:T(8,128)(2,1)S(1)}, bf16[4,64,16,128]{3,2,1,0:T(8,128)(2,1)S(1)}, u32[]{:S(2)}, u32[]{:S(2)}) collective-permute-start(bf16[4,64,16,128]{3,2,1,0:T(8,128)(2,1)S(1)} %get-tuple-element.64), channel_id=1, source_target_pairs={{0,128},{128,0},{1,129},{129,1},{2,130},{130,2},{3,131},{131,3},{4... | collective-permute-start | bytes 3145736 | tf_op jit(solution)/shard_map/ppermute | solution.py:325
  60.3 7.0 %collective-permute-start.20 = (bf16[16,8192]{1,0:T(8,128)(2,1)S(1)}, bf16[16,8192]{1,0:T(8,128)(2,1)S(1)}, u32[]{:S(2)}, u32[]{:S(2)}) collective-permute-start(bf16[16,8192]{1,0:T(8,128)(2,1)S(1)} %add.22.refs_2_), channel_id=1, source_target_pairs={{0,4},{1,29},{2,6},{3,31},{4,8},{5,1},{6,10},{7,3},{8,12},{9,5},{1... | collective-permute-start | bytes 786440 | tf_op jit(solution)/shard_map/ppermute | solution.py:341
  60.5 8.2 %collective-permute-start.23 = (bf16[16,8192]{1,0:T(8,128)(2,1)S(1)}, bf16[16,8192]{1,0:T(8,128)(2,1)S(1)}, u32[]{:S(2)}, u32[]{:S(2)}) collective-permute-start(bf16[16,8192]{1,0:T(8,128)(2,1)S(1)} %add.23.refs_2_), channel_id=1, source_target_pairs={{0,4},{1,29},{2,6},{3,31},{4,8},{5,1},{6,10},{7,3},{8,12},{9,5},{1... | collective-permute-start | bytes 786440 | tf_op jit(solution)/shard_map/ppermute | solution.py:341
  60.6 16.6 %collective-permute-start.26 = (bf16[2,64,16,128]{3,2,1,0:T(8,128)(2,1)S(1)}, bf16[2,64,16,128]{3,2,1,0:T(8,128)(2,1)S(1)}, u32[]{:S(2)}, u32[]{:S(2)}) collective-permute-start(bf16[2,64,16,128]{3,2,1,0:T(8,128)(2,1)S(1)} %get-tuple-element.72), channel_id=1, source_target_pairs={{0,96},{1,33},{32,0},{33,65},{64,32},{65,97},{96,64},{97,1},{2,98}... | collective-permute-start | bytes 1572872 | tf_op jit(solution)/shard_map/ppermute | solution.py:342
  63.6 13.6 %collective-permute-start.25 = (bf16[2,64,16,128]{3,2,1,0:T(8,128)(2,1)S(1)}, bf16[2,64,16,128]{3,2,1,0:T(8,128)(2,1)S(1)}, u32[]{:S(2)}, u32[]{:S(2)}) collective-permute-start(bf16[2,64,16,128]{3,2,1,0:T(8,128)(2,1)S(1)} %add.24.refs_3_), channel_id=1, source_target_pairs={{0,32},{1,97},{32,64},{33,1},{64,96},{65,33},{96,0},{97,65},{2,34}... | collective-permute-start | bytes 1572872 | tf_op jit(solution)/shard_map/ppermute | solution.py:342
  67.4 5.6 %collective-permute-start.22 = (bf16[16,8192]{1,0:T(8,128)(2,1)S(1)}, bf16[16,8192]{1,0:T(8,128)(2,1)S(1)}, u32[]{:S(2)}, u32[]{:S(2)}) collective-permute-start(bf16[16,8192]{1,0:T(8,128)(2,1)S(1)} %add.25.refs_3_), channel_id=1, source_target_pairs={{0,4},{1,29},{2,6},{3,31},{4,8},{5,1},{6,10},{7,3},{8,12},{9,5},{1... | collective-permute-start | bytes 786440 | tf_op jit(solution)/shard_map/ppermute | solution.py:341
  68.8 7.0 %collective-permute-start.27 = (bf16[16,8192]{1,0:T(8,128)(2,1)S(1)}, bf16[16,8192]{1,0:T(8,128)(2,1)S(1)}, u32[]{:S(2)}, u32[]{:S(2)}) collective-permute-start(bf16[16,8192]{1,0:T(8,128)(2,1)S(1)} %add.26.refs_3_), channel_id=1, source_target_pairs={{0,4},{1,29},{2,6},{3,31},{4,8},{5,1},{6,10},{7,3},{8,12},{9,5},{1... | collective-permute-start | bytes 786440 | tf_op jit(solution)/shard_map/ppermute | solution.py:341
  73.1 7.5 %collective-permute-start.24 = (bf16[16,8192]{1,0:T(8,128)(2,1)S(1)}, bf16[16,8192]{1,0:T(8,128)(2,1)S(1)}, u32[]{:S(2)}, u32[]{:S(2)}) collective-permute-start(bf16[16,8192]{1,0:T(8,128)(2,1)S(1)} %add.27.refs_3_), channel_id=1, source_target_pairs={{0,4},{1,29},{2,6},{3,31},{4,8},{5,1},{6,10},{7,3},{8,12},{9,5},{1... | collective-permute-start | bytes 786440 | tf_op jit(solution)/shard_map/ppermute | solution.py:341
  75.9 13.7 %collective-permute-start.30 = (bf16[16,8192]{1,0:T(8,128)(2,1)S(1)}, bf16[16,8192]{1,0:T(8,128)(2,1)S(1)}, u32[]{:S(2)}, u32[]{:S(2)}) collective-permute-start(bf16[16,8192]{1,0:T(8,128)(2,1)S(1)} %add.28.refs_3_), channel_id=1, source_target_pairs={{0,4},{1,29},{2,6},{3,31},{4,8},{5,1},{6,10},{7,3},{8,12},{9,5},{1... | collective-permute-start | bytes 786440 | tf_op jit(solution)/shard_map/ppermute | solution.py:341
  77.3 11.4 %collective-permute-start.31 = (bf16[64,16,128]{2,1,0:T(8,128)(2,1)S(1)}, bf16[64,16,128]{2,1,0:T(8,128)(2,1)S(1)}, u32[]{:S(2)}, u32[]{:S(2)}) collective-permute-start(bf16[64,16,128]{2,1,0:T(8,128)(2,1)S(1)} %add.29.refs_3_), channel_id=1, source_target_pairs={{0,128},{128,0},{1,129},{129,1},{2,130},{130,2},{3,131},{131,3},{4... | collective-permute-start | bytes 786440 | tf_op jit(solution)/shard_map/ppermute | solution.py:325
  80.7 8.9 %collective-permute-start.29 = (bf16[16,8192]{1,0:T(8,128)(2,1)S(1)}, bf16[16,8192]{1,0:T(8,128)(2,1)S(1)}, u32[]{:S(2)}, u32[]{:S(2)}) collective-permute-start(bf16[16,8192]{1,0:T(8,128)(2,1)S(1)} %add.30.refs_2_), channel_id=1, source_target_pairs={{0,4},{1,29},{2,6},{3,31},{4,8},{5,1},{6,10},{7,3},{8,12},{9,5},{1... | collective-permute-start | bytes 786440 | tf_op jit(solution)/shard_map/ppermute | solution.py:341
  83.2 9.2 %collective-permute-start.28 = (bf16[64,16,128]{2,1,0:T(8,128)(2,1)S(1)}, bf16[64,16,128]{2,1,0:T(8,128)(2,1)S(1)}, u32[]{:S(2)}, u32[]{:S(2)}) collective-permute-start(bf16[64,16,128]{2,1,0:T(8,128)(2,1)S(1)} %add.32.refs_4_), channel_id=1, source_target_pairs={{0,96},{1,33},{32,0},{33,65},{64,32},{65,97},{96,64},{97,1},{2,98}... | collective-permute-start | bytes 786440 | tf_op jit(solution)/shard_map/ppermute | solution.py:342
  84.2 8.2 %collective-permute-start.33 = (bf16[64,16,128]{2,1,0:T(8,128)(2,1)S(1)}, bf16[64,16,128]{2,1,0:T(8,128)(2,1)S(1)}, u32[]{:S(2)}, u32[]{:S(2)}) collective-permute-start(bf16[64,16,128]{2,1,0:T(8,128)(2,1)S(1)} %add.31.refs_2_), channel_id=1, source_target_pairs={{0,32},{1,97},{32,64},{33,1},{64,96},{65,33},{96,0},{97,65},{2,34}... | collective-permute-start | bytes 786440 | tf_op jit(solution)/shard_map/ppermute | solution.py:342
  89.9 5.2 %collective-permute-start.32 = (bf16[2,8,8192]{2,1,0:T(8,128)(2,1)S(1)}, bf16[2,8,8192]{2,1,0:T(8,128)(2,1)S(1)}, u32[]{:S(2)}, u32[]{:S(2)}) collective-permute-start(bf16[2,8,8192]{2,1,0:T(8,128)(2,1)S(1)} %get-tuple-element.75.refs_3_), channel_id=1, source_target_pairs={{0,1},{1,0},{2,3},{3,2},{4,5},{5,4},{6,7},{7,6},{8,9},{9,8},{10,11... | collective-permute-start | bytes 786440 | tf_op jit(solution)/shard_map/ppermute | solution.py:325
  92.5 5.9 %collective-permute-start.34 = (bf16[64,16,128]{2,1,0:T(8,128)(2,1)S(1)}, bf16[64,16,128]{2,1,0:T(8,128)(2,1)S(1)}, u32[]{:S(2)}, u32[]{:S(2)}) collective-permute-start(bf16[64,16,128]{2,1,0:T(8,128)(2,1)S(1)} %add.35), channel_id=1, source_target_pairs={{0,32},{1,97},{32,64},{33,1},{64,96},{65,33},{96,0},{97,65},{2,34}... | collective-permute-start | bytes 786440 | tf_op jit(solution)/shard_map/ppermute | solution.py:342
  95.1 5.3 %collective-permute-start.35 = (bf16[2,4,8192]{2,1,0:T(4,128)(2,1)S(1)}, bf16[2,4,8192]{2,1,0:T(4,128)(2,1)S(1)}, u32[]{:S(2)}, u32[]{:S(2)}) collective-permute-start(bf16[2,4,8192]{2,1,0:T(4,128)(2,1)S(1)} %get-tuple-element.76.refs_3_), channel_id=1, source_target_pairs={{0,2},{2,0},{1,3},{3,1},{4,6},{6,4},{5,7},{7,5},{8,10},{10,8},{9,1... | collective-permute-start | bytes 393224 | tf_op jit(solution)/shard_map/ppermute | solution.py:325
